TPU v7x, 32 devices: a whole 2x2x4 slice. The times are simulated.
32 devices in a mesh: dp: 4 (over x, core), tensor: 8 (over z, y).
Axes of the slice: x: 2, y: 2, z: 4, core: 2. Of those that a mesh axis runs over, the one named last changes fastest.
Arguments:
- activations: bfloat16 [2048, 8192], P('dp', 'tensor'), may hold values from -6 to 6
- left_factor: bfloat16 [1024, 8192], P(None, 'tensor'), may hold values from -0.0625 to 0.0625
- right_factor: bfloat16 [1024, 16384], P(None, 'tensor'), may hold values from -0.1875 to 0.1875
- out_grad: bfloat16 [2048, 16384], P('dp', 'tensor'), may hold values from -6 to 6
Outputs:
- input_grad: bfloat16 [2048, 8192], P('dp', 'tensor')
- left_grad: float32 [1024, 8192], P('dp', 'tensor')
- right_grad: float32 [1024, 16384], P('dp', 'tensor')
All inputs are finite; a program needn't handle non-finite values.
Results may differ from a plain program's by a relative error of at most 0.0049.
Values may be sent and summed in bfloat16 or wider, within the bound.
No kernel may reach another device: no remote copies, remote signals or barrier semaphores. Data moves between devices by JAX's collectives and lax.ppermute only.
A program may use at most 64 MiB of HBM per device.

v0:
```python
import math

import jax
import jax.numpy as jnp
from jax import lax
from jax.sharding import PartitionSpec as P


def contract_rows(first, second):
    return lax.dot_general(
        first, second, (((0,), (0,)), ((), ())), preferred_element_type=jnp.float32
    )


def contract_cols(first, second):
    return lax.dot_general(
        first, second, (((1,), (1,)), ((), ())), preferred_element_type=jnp.float32
    )


def shards(activations, left_factor, right_factor, out_grad):
    group_count = lax.axis_size("dp")
    scale = 1.0 / math.sqrt(activations.shape[0] * group_count)
    latent_part = contract_cols(activations, left_factor)
    grad_part = contract_cols(out_grad, right_factor)
    latent = lax.psum(latent_part, "tensor").astype(jnp.bfloat16)
    columns = latent
    right_sum = lax.psum_scatter(
        contract_rows(columns, out_grad), "dp", scatter_dimension=0, tiled=True
    )
    latent_grad = lax.psum(grad_part, "tensor").astype(jnp.bfloat16)
    input_grad = jnp.dot(latent_grad, left_factor, preferred_element_type=jnp.float32).astype(
        jnp.bfloat16
    )
    columns = latent_grad
    left_sum = lax.psum_scatter(
        contract_rows(columns, activations), "dp", scatter_dimension=0, tiled=True
    )
    return (input_grad, left_sum * scale, right_sum * scale)


def solution(mesh):
    placed = (P("dp", "tensor"), P(None, "tensor"), P(None, "tensor"), P("dp", "tensor"))
    return jax.shard_map(
        shards,
        mesh=mesh,
        in_specs=placed,
        out_specs=(P("dp", "tensor"), P("dp", "tensor"), P("dp", "tensor")),
        check_vma=False,
    )
```

profile of v0, /device:TPU:0, one launch (start us, length us, event | category | flops | bytes accessed | tf_op | source)
XLA Modules:
  0.0 318.9 jit_solution(917695482466357819)
XLA Ops:
  7.2 0.0 copy-start
  7.2 0.0 copy-start.1
  7.2 0.0 reduce-scatter.3.cloned.1.call-start
  7.2 1.5 copy-done
  8.8 0.0 copy-start.2
  8.8 6.0 %fusion.5 = f32[512,1024]{1,0:T(8,128)} fusion(bf16[512,2048]{1,0:T(8,128)(2,1)S(1)} %copy-done, bf16[1024,2048]{1,0:T(8,128)(2,1)} %param.6), kind=kOutput, calls=%fused_computation.8 | convolution fusion | flops 2147483648 | bytes 8388608 | tf_op jit(solution)/shard_map/dot_general | solution.py:16
  14.8 0.0 copy-done.1
  14.8 0.0 copy-done.2
  14.8 2.6 fusion.6
  17.4 169.1 %all-reduce.2 = (bf16[512,1024]{1,0:T(8,128)(2,1)S(1)}, bf16[512,1024]{1,0:T(8,128)(2,1)}) all-reduce(f32[512,1024]{1,0:T(8,128)} %fusion.5, f32[512,1024]{1,0:T(8,128)} %fusion.6), channel_id=1, replica_groups=mesh['dp'=4,'tensor'=8] {'tensor'}, use_global_device_ids=true, to_apply=%region_0.0 | all-reduce | flops 1048576 | bytes 6291456 | tf_op jit(solution)/shard_map/psum | solution.py:31
  186.5 4.5 %fusion.8 = f32[1024,1024]{1,0:T(8,128)} fusion(bf16[512,1024]{1,0:T(8,128)(2,1)S(1)} %get-tuple-element.3, bf16[512,1024]{1,0:T(8,128)(2,1)} %param.4), kind=kOutput, calls=%fused_computation.11 | convolution fusion | flops 1073741824 | bytes 6291456 | tf_op jit(solution)/shard_map/dot_general | solution.py:10
  191.0 0.0 reduce-scatter.3.cloned.1.call-update
  191.0 0.0 reduce-scatter.5.cloned.1.call-start
  191.1 7.6 %fusion.7 = f32[1024,2048]{1,0:T(8,128)} fusion(bf16[512,1024]{1,0:T(8,128)(2,1)} %get-tuple-element.4, bf16[512,2048]{1,0:T(8,128)(2,1)S(1)} %copy-done), kind=kOutput, calls=%fused_computation.10 | convolution fusion | flops 2147483648 | bytes 11534336 | tf_op jit(solution)/shard_map/dot_general | solution.py:10
  198.7 0.0 reduce-scatter.5.cloned.1.call-update
  198.7 4.0 %convolution_convert_fusion = bf16[512,1024]{1,0:T(8,128)(2,1)} fusion(bf16[1024,1024]{1,0:T(8,128)(2,1)} %param.5, bf16[512,1024]{1,0:T(8,128)(2,1)S(1)} %get-tuple-element.3), kind=kOutput, calls=%fused_computation | convolution fusion | flops 1074266112 | bytes 4194304 | tf_op jit(solution)/shard_map/dot_general | solution.py:32
  202.7 31.6 %reduce-scatter.3.cloned.1.call-done = f32[256,1024]{1,0:T(8,128)} async-done(((f32[1024,1024]{1,0:T(8,128)}), f32[256,1024]{1,0:T(8,128)}) %reduce-scatter.3.cloned.1.call-update) | async-done | bytes 1048592 | tf_op jit(solution)/shard_map/reduce_scatter | solution.py:36
  234.3 2.3 broadcast_multiply_fusion.1
  236.7 72.2 %reduce-scatter.5.cloned.1.call-done = f32[256,2048]{1,0:T(8,128)} async-done(((f32[1024,2048]{1,0:T(8,128)}), f32[256,2048]{1,0:T(8,128)}) %reduce-scatter.5.cloned.1.call-update) | async-done | bytes 2097168 | tf_op jit(solution)/shard_map/reduce_scatter | solution.py:28
  308.8 3.2 %broadcast_multiply_fusion = f32[256,2048]{1,0:T(8,128)} fusion(f32[256,2048]{1,0:T(8,128)} %reduce-scatter.5.cloned.1.call-done), kind=kLoop, calls=%fused_computation.1 | loop fusion | flops 524288 | bytes 4194304 | tf_op jit(solution)/shard_map/mul | solution.py:39
Async XLA Ops:
  7.2 1.6 copy-start
  7.2 7.6 %copy-start.1 = (bf16[512,1024]{1,0:T(8,128)(2,1)S(1)}, bf16[512,1024]{1,0:T(8,128)(2,1)}, u32[]{:S(2)}) copy-start(bf16[512,1024]{1,0:T(8,128)(2,1)} %param.4) | copy-start | bytes 3145732
  7.2 227.1 %reduce-scatter.3.cloned.1.call-start = ((), (), s32[]{:S(2)}) async-start(), calls=%async_computation.2 | async-start | bytes 5242880 | tf_op jit(solution)/shard_map/reduce_scatter | solution.py:36
  8.8 6.0 %copy-start.2 = (bf16[1024,1024]{1,0:T(8,128)(2,1)S(1)}, bf16[1024,1024]{1,0:T(8,128)(2,1)}, u32[]{:S(2)}) copy-start(bf16[1024,1024]{1,0:T(8,128)(2,1)} %param.5) | copy-start | bytes 6291460
  191.0 117.8 %reduce-scatter.5.cloned.1.call-start = ((), (), s32[]{:S(2)}) async-start(), calls=%async_computation.3 | async-start | bytes 10485760 | tf_op jit(solution)/shard_map/reduce_scatter | solution.py:28
Sparse Core Ops, SparseCore 0:
  191.1 43.1 reduce-scatter.2
  237.1 71.6 reduce-scatter.4
where the time goes:
time: 319 us
  blocking collectives  169 us (53%)
  waiting for transfers between devices  104 us (33%)
  matrix products  24.7 us (8%)
  between operations  14.1 us (4%)
  other arithmetic  5.55 us (2%)
    psum x1, blocking collectives, shards(): latent_grad = lax.psum(grad_part, 'tensor').astype(jnp.bfloat16)  169 us
    reduce_scatter x1, waiting for transfers between devices, shards(): lax.psum_scatter(contract_rows(columns, out_grad), 'dp', scatter_dimensio...  72.2 us
    reduce_scatter x1, waiting for transfers between devices, shards(): lax.psum_scatter(contract_rows(columns, activations), 'dp', scatter_dimen...  31.6 us
    dot_general x2, matrix products, contract_rows(): lax.dot_general(first, second, (((0,), (0,)), ((), ())), preferred_elemen...  12.1 us
    dot_general x2, matrix products, contract_cols(): lax.dot_general(first, second, (((1,), (1,)), ((), ())), preferred_elemen...  8.64 us
  transfers between devices with their start and end apart: 2, of which 2 were waited for; matrix products, arithmetic and copies ran while one was open for 4% of the time, Pallas kernels for 0%

commit v1 on v0

v1 whole, which is shorter than its diff:
```python
import math

import jax
import jax.numpy as jnp
from jax import lax
from jax.sharding import PartitionSpec as P

CHUNKS = 1


def rows_by_rows(first, second):
    return lax.dot_general(
        first, second, (((0,), (0,)), ((), ())), preferred_element_type=jnp.float32
    )


def cols_by_cols(first, second):
    return lax.dot_general(
        first, second, (((1,), (1,)), ((), ())), preferred_element_type=jnp.float32
    )


def swap(value, axis, mask):
    size = lax.axis_size(axis)
    return lax.ppermute(value, axis, [(i, i ^ mask) for i in range(size)])


def pick(value, index, size, axis=0):
    return lax.dynamic_slice_in_dim(value, index * size, size, axis)


def summed(part, place):
    width = lax.axis_size("tensor")
    half = part.shape[0] // 2
    low, high = place % 2, place // 2
    sent = swap(pick(part, 1 - low, half).astype(jnp.bfloat16), "tensor", 1)
    total = pick(part, low, half) + sent.astype(jnp.float32)
    share = half // (width // 2)
    mine = pick(total, high, share)
    for step in range(1, width // 2):
        piece = pick(total, high ^ step, share).astype(jnp.bfloat16)
        mine = mine + swap(piece, "tensor", 2 * step).astype(jnp.float32)
    return mine.astype(jnp.bfloat16)


def gathered(mine, place):
    width = lax.axis_size("tensor")
    share = mine.shape[0]
    low, high = place % 2, place // 2
    half = share * (width // 2)
    whole = jnp.zeros((half,) + mine.shape[1:], mine.dtype)
    for step in range(width // 2):
        piece = swap(mine, "tensor", 2 * step) if step else mine
        whole = lax.dynamic_update_slice_in_dim(whole, piece, (high ^ step) * share, 0)
    other = swap(whole, "tensor", 1)
    return jnp.where(
        low == 0, jnp.concatenate([whole, other]), jnp.concatenate([other, whole])
    )


def owned(part, group):
    owners = part.shape[0]
    mine = lax.dynamic_index_in_dim(part, group, 0, False)
    for step in range(1, owners):
        block = lax.dynamic_index_in_dim(part, group ^ step, 0, False)
        mine = mine + swap(block.astype(jnp.bfloat16), "dp", 2 * step).astype(jnp.float32)
    return mine


def shards(activations, left_factor, right_factor, out_grad):
    groups = lax.axis_size("dp")
    tokens = activations.shape[0]
    rank = left_factor.shape[0]
    owners = groups // 2
    rows = rank // groups
    scale = 1.0 / math.sqrt(tokens * groups)
    place = lax.axis_index("tensor")
    spot = lax.axis_index("dp")
    core, group = spot % 2, spot // 2

    def of_core(factor, which):
        blocks = factor.reshape(owners, 2, rows, factor.shape[1])
        return lax.dynamic_index_in_dim(blocks, which, 1, False)

    acts = jnp.concatenate([activations, swap(activations, "dp", 1)])
    grads = jnp.concatenate([out_grad, swap(out_grad, "dp", 1)])
    left = of_core(left_factor, core)
    left_other = of_core(left_factor, 1 - core)
    right = of_core(right_factor, core)

    step = rows // CHUNKS
    spans = [slice(i * step, (i + 1) * step) for i in range(CHUNKS)]

    def part_of(values, factor, span):
        return cols_by_cols(values, factor[:, span].reshape(owners * step, factor.shape[2]))

    latents = [gathered(summed(part_of(acts, left, s), place), place) for s in spans]
    latent_grads = [gathered(summed(part_of(grads, right, s), place), place) for s in spans]

    def weight_grad(pieces, values):
        done = []
        for piece in pieces:
            part = rows_by_rows(piece, values).reshape(owners, step, values.shape[1])
            done.append(owned(part, group) * scale)
        return jnp.concatenate(done)

    right_grad = weight_grad(latents, grads)
    left_grad = weight_grad(latent_grads, acts)

    def flat(factor, span):
        return factor[:, span].reshape(owners * step, factor.shape[2])

    total = 0.0
    for piece, span in zip(latent_grads, spans, strict=True):
        other = swap(piece[tokens:], "dp", 1)
        total = total + jnp.dot(
            piece[:tokens], flat(left, span), preferred_element_type=jnp.float32
        )
        total = total + jnp.dot(other, flat(left_other, span), preferred_element_type=jnp.float32)
    return total.astype(jnp.bfloat16), left_grad, right_grad


def solution(mesh):
    placed = (P("dp", "tensor"), P(None, "tensor"), P(None, "tensor"), P("dp", "tensor"))
    return jax.shard_map(
        shards,
        mesh=mesh,
        in_specs=placed,
        out_specs=(P("dp", "tensor"), P("dp", "tensor"), P("dp", "tensor")),
        check_vma=False,
    )
```

time: 319 us -> 119 us (0.37)
  blocking collectives: 169 us -> 0 us
  waiting for transfers between devices: 104 us -> 53.5 us
  starting transfers between devices: 0.08 us -> 28.2 us
  local copies, waits for them, and re-layouts: 1.54 us -> 14.9 us
  between operations: 14.1 us -> 0.85 us
  matrix products: 24.7 us -> 12.7 us
    psum x1 -> x0, blocking collectives: 169 us -> none  [shards(): latent_grad = lax.psum(grad_part, 'tensor').astype(jnp.bfloat16)]
    reduce_scatter x2 -> x0, waiting for transfers between devices: 104 us -> none  [the longest x1 72.2 us: shards(): lax.psum_scatter(contract_rows(columns, out_grad), 'dp', scatter_dimensio...]
    ppermute x0 -> x21, waiting for transfers between devices: none -> 53.5 us  [swap(): return lax.ppermute(value, axis, [(i, i ^ mask) for i in range(size)])]
    ppermute x0 -> x21, starting transfers between devices: none -> 28.2 us  [swap(): return lax.ppermute(value, axis, [(i, i ^ mask) for i in range(size)])]
    dot_general x5 -> x6, matrix products: 24.7 us -> 12.7 us  [the longest x2 6.6 us: rows_by_rows(): lax.dot_general(first, second, (((0,), (0,)), ((), ())), preferred_elemen...]
    dynamic_update_slice x0 -> x6, local copies, waits for them, and re-layouts: none -> 4.01 us  [gathered(): lax.dynamic_update_slice_in_dim(whole, piece, (high ^ step) * share, 0)]
  transfers between devices with their start and end apart: 2 -> 21, of which waited for: 2 -> 10; matrix products, arithmetic and copies ran while one was open for 4% -> 27% of each run, Pallas kernels for 0% -> 0%
where the time goes in v1:
time: 119 us
  waiting for transfers between devices  53.5 us (45%)
  starting transfers between devices  28.2 us (24%)
  local copies, waits for them, and re-layouts  14.9 us (13%)
  matrix products  12.7 us (11%)
  other arithmetic  8.64 us (7%)
    ppermute x21, waiting for transfers between devices, swap(): return lax.ppermute(value, axis, [(i, i ^ mask) for i in range(size)])  53.5 us
    ppermute x21, starting transfers between devices, swap(): return lax.ppermute(value, axis, [(i, i ^ mask) for i in range(size)])  28.2 us
    dot_general x2, matrix products, rows_by_rows(): lax.dot_general(first, second, (((0,), (0,)), ((), ())), preferred_elemen...  6.6 us
    dynamic_update_slice x6, local copies, waits for them, and re-layouts, gathered(): lax.dynamic_update_slice_in_dim(whole, piece, (high ^ step) * share, 0)  4.01 us
    mul x2, other arithmetic, weight_grad(): done.append(owned(part, group) * scale)  3.99 us
    dot_general x2, matrix products, cols_by_cols(): lax.dot_general(first, second, (((1,), (1,)), ((), ())), preferred_elemen...  3.64 us
    unnamed x20, local copies, waits for them, and re-layouts  3.54 us
  transfers between devices with their start and end apart: 21, of which 10 were waited for; matrix products, arithmetic and copies ran while one was open for 27% of the time, Pallas kernels for 0%

profile of v1, /device:TPU:0, one launch (start us, length us, event | category | flops | bytes accessed | tf_op | source)
XLA Modules:
  0.0 118.7 jit_solution(9447389216468706317)
XLA Ops:
  1.2 1.4 %constant_dynamic-update-slice_fusion.3 = bf16[1024,1024]{1,0:T(8,128)(2,1)S(1)} fusion(bf16[512,1024]{1,0:T(8,128)(2,1)} %param.4), kind=kLoop, calls=%fused_computation.34 | loop fusion | bytes 2097152
  3.8 1.3 %constant_dynamic-update-slice_fusion.2 = bf16[1024,1024]{1,0:T(8,128)(2,1)S(1)} fusion(bf16[1024,1024]{1,0:T(8,128)(2,1)S(1)} %constant_dynamic-update-slice_fusion.3, bf16[512,1024]{1,0:T(8,128)(2,1)} %collective-permute-done.10), kind=kLoop, calls=%fused_computation.33 | loop fusion | bytes 2097152 | tf_op jit(solution)/shard_map/concatenate | solution.py:85
  5.1 1.3 %fusion.16 = f32[1024,512]{1,0:T(8,128)S(1)} fusion(bf16[1024,1024]{1,0:T(8,128)(2,1)S(1)} %constant_dynamic-update-slice_fusion.2, bf16[512,1024]{1,0:T(8,128)(2,1)S(1)} %bitcast.32), kind=kOutput, calls=%fused_computation.50 | convolution fusion | flops 1073741824 | bytes 5242880 | tf_op jit(solution)/shard_map/dot_general | solution.py:18
  6.5 3.0 %collective-permute-start.12 = (bf16[512,512]{1,0:T(8,128)(2,1)S(1)}, bf16[512,512]{1,0:T(8,128)(2,1)S(1)}, u32[]{:S(2)}, u32[]{:S(2)}) collective-permute-start(bf16[512,512]{1,0:T(8,128)(2,1)S(1)} %dynamic-slice_convert_fusion.1), channel_id=1, source_target_pairs={{0,1},{1,0},{2,3},{3,2},{4,5},{5,4},{6,7},{7,6},{8,9},{9,8},{10,11... | collective-permute-start | bytes 1572872 | tf_op jit(solution)/shard_map/ppermute | solution.py:25
  9.8 11.8 %collective-permute-done.12 = bf16[512,512]{1,0:T(8,128)(2,1)S(1)} collective-permute-done((bf16[512,512]{1,0:T(8,128)(2,1)S(1)}, bf16[512,512]{1,0:T(8,128)(2,1)S(1)}, u32[]{:S(2)}, u32[]{:S(2)}) %collective-permute-start.12) | collective-permute-done | bytes 524320 | tf_op jit(solution)/shard_map/ppermute | solution.py:25
  21.9 3.9 %collective-permute-start.15 = (bf16[128,512]{1,0:T(8,128)(2,1)S(1)}, bf16[128,512]{1,0:T(8,128)(2,1)S(1)}, u32[]{:S(2)}, u32[]{:S(2)}) collective-permute-start(bf16[128,512]{1,0:T(8,128)(2,1)S(1)} %get-tuple-element.10), channel_id=1, source_target_pairs={{0,6},{1,7},{2,4},{3,5},{4,2},{5,3},{6,0},{7,1},{8,14},{9,15},{10,... | collective-permute-start | bytes 393224 | tf_op jit(solution)/shard_map/ppermute | solution.py:25
  25.8 0.6 collective-permute-start.13
  26.4 1.7 %constant_dynamic-update-slice_fusion = bf16[1024,2048]{1,0:T(8,128)(2,1)S(1)} fusion(bf16[1024,2048]{1,0:T(8,128)(2,1)S(1)} %constant_dynamic-update-slice_fusion.1, bf16[512,2048]{1,0:T(8,128)(2,1)} %collective-permute-done), kind=kLoop, calls=%fused_computation.31 | loop fusion | bytes 4194304 | tf_op jit(solution)/shard_map/concatenate | solution.py:86
  28.2 2.4 %fusion.13 = f32[1024,512]{1,0:T(8,128)S(1)} fusion(bf16[1024,2048]{1,0:T(8,128)(2,1)S(1)} %constant_dynamic-update-slice_fusion, bf16[512,2048]{1,0:T(8,128)(2,1)S(1)} %bitcast.37), kind=kOutput, calls=%fused_computation.47 | convolution fusion | flops 2147483648 | bytes 8388608 | tf_op jit(solution)/shard_map/dot_general | solution.py:18
  30.6 1.7 %collective-permute-start.1 = (bf16[512,512]{1,0:T(8,128)(2,1)S(1)}, bf16[512,512]{1,0:T(8,128)(2,1)S(1)}, u32[]{:S(2)}, u32[]{:S(2)}) collective-permute-start(bf16[512,512]{1,0:T(8,128)(2,1)S(1)} %dynamic-slice_convert_fusion.3), channel_id=1, source_target_pairs={{0,1},{1,0},{2,3},{3,2},{4,5},{5,4},{6,7},{7,6},{8,9},{9,8},{10,11... | collective-permute-start | bytes 1572872 | tf_op jit(solution)/shard_map/ppermute | solution.py:25
  32.4 4.0 %collective-permute-done.14 = bf16[128,512]{1,0:T(8,128)(2,1)S(1)} collective-permute-done((bf16[128,512]{1,0:T(8,128)(2,1)S(1)}, bf16[128,512]{1,0:T(8,128)(2,1)S(1)}, u32[]{:S(2)}, u32[]{:S(2)}) %collective-permute-start.14) | collective-permute-done | bytes 131104 | tf_op jit(solution)/shard_map/ppermute | solution.py:25
  36.3 0.9 broadcast.7.clone.1
  37.2 0.7 constant_dynamic-update-slice_fusion.7
  37.9 3.1 %collective-permute-start.17 = (bf16[128,512]{1,0:T(8,128)(2,1)S(1)}, bf16[128,512]{1,0:T(8,128)(2,1)S(1)}, u32[]{:S(2)}, u32[]{:S(2)}) collective-permute-start(bf16[128,512]{1,0:T(8,128)(2,1)S(1)} %get-tuple-element.4), channel_id=1, source_target_pairs={{0,4},{1,5},{2,6},{3,7},{4,0},{5,1},{6,2},{7,3},{8,12},{9,13},{10,... | collective-permute-start | bytes 393224 | tf_op jit(solution)/shard_map/ppermute | solution.py:25
  41.0 1.3 %collective-permute-start.18 = (bf16[128,512]{1,0:T(8,128)(2,1)S(1)}, bf16[128,512]{1,0:T(8,128)(2,1)S(1)}, u32[]{:S(2)}, u32[]{:S(2)}) collective-permute-start(bf16[128,512]{1,0:T(8,128)(2,1)S(1)} %get-tuple-element.4), channel_id=1, source_target_pairs={{0,6},{1,7},{2,4},{3,5},{4,2},{5,3},{6,0},{7,1},{8,14},{9,15},{10,... | collective-permute-start | bytes 393224 | tf_op jit(solution)/shard_map/ppermute | solution.py:25
  42.3 1.9 %collective-permute-done.16 = bf16[128,512]{1,0:T(8,128)(2,1)S(1)} collective-permute-done((bf16[128,512]{1,0:T(8,128)(2,1)S(1)}, bf16[128,512]{1,0:T(8,128)(2,1)S(1)}, u32[]{:S(2)}, u32[]{:S(2)}) %collective-permute-start.16) | collective-permute-done | bytes 131104 | tf_op jit(solution)/shard_map/ppermute | solution.py:25
  44.2 0.7 constant_dynamic-update-slice_fusion.6
  44.8 5.5 %collective-permute-done.17 = bf16[128,512]{1,0:T(8,128)(2,1)S(1)} collective-permute-done((bf16[128,512]{1,0:T(8,128)(2,1)S(1)}, bf16[128,512]{1,0:T(8,128)(2,1)S(1)}, u32[]{:S(2)}, u32[]{:S(2)}) %collective-permute-start.17) | collective-permute-done | bytes 131104 | tf_op jit(solution)/shard_map/ppermute | solution.py:25
  50.4 0.7 constant_dynamic-update-slice_fusion.5
  51.0 0.7 constant_dynamic-update-slice_fusion.4
  51.7 1.5 %collective-permute-start.19 = (bf16[512,512]{1,0:T(8,128)(2,1)}, bf16[512,512]{1,0:T(8,128)(2,1)}, u32[]{:S(2)}, u32[]{:S(2)}) collective-permute-start(bf16[512,512]{1,0:T(8,128)(2,1)} %constant_dynamic-update-slice_fusion.4), channel_id=1, source_target_pairs={{0,1},{1,0},{2,3},{3,2},{4,5},{5,4},{6,7},{7,6},{8,9},{9,8},{10,11... | collective-permute-start | bytes 1572872 | tf_op jit(solution)/shard_map/ppermute | solution.py:25
  53.5 1.0 copy-done.2
  54.4 0.8 dynamic-slice_convert_fusion.9
  55.2 1.5 %collective-permute-start.4 = (bf16[128,512]{1,0:T(8,128)(2,1)}, bf16[128,512]{1,0:T(8,128)(2,1)S(1)}, u32[]{:S(2)}, u32[]{:S(2)}) collective-permute-start(bf16[128,512]{1,0:T(8,128)(2,1)} %get-tuple-element.13), channel_id=1, source_target_pairs={{0,6},{1,7},{2,4},{3,5},{4,2},{5,3},{6,0},{7,1},{8,14},{9,15},{10,... | collective-permute-start | bytes 393224 | tf_op jit(solution)/shard_map/ppermute | solution.py:25
  56.7 1.3 %collective-permute-start.3 = (bf16[128,512]{1,0:T(8,128)(2,1)}, bf16[128,512]{1,0:T(8,128)(2,1)S(1)}, u32[]{:S(2)}, u32[]{:S(2)}) collective-permute-start(bf16[128,512]{1,0:T(8,128)(2,1)} %get-tuple-element.14), channel_id=1, source_target_pairs={{0,4},{1,5},{2,6},{3,7},{4,0},{5,1},{6,2},{7,3},{8,12},{9,13},{10,... | collective-permute-start | bytes 393224 | tf_op jit(solution)/shard_map/ppermute | solution.py:25
  58.0 1.6 %collective-permute-start.2 = (bf16[128,512]{1,0:T(8,128)(2,1)}, bf16[128,512]{1,0:T(8,128)(2,1)S(1)}, u32[]{:S(2)}, u32[]{:S(2)}) collective-permute-start(bf16[128,512]{1,0:T(8,128)(2,1)} %get-tuple-element.12), channel_id=1, source_target_pairs={{0,2},{1,3},{2,0},{3,1},{4,6},{5,7},{6,4},{7,5},{8,10},{9,11},{10,... | collective-permute-start | bytes 393224 | tf_op jit(solution)/shard_map/ppermute | solution.py:25
  59.6 2.7 %collective-permute-done.4 = bf16[128,512]{1,0:T(8,128)(2,1)S(1)} collective-permute-done((bf16[128,512]{1,0:T(8,128)(2,1)}, bf16[128,512]{1,0:T(8,128)(2,1)S(1)}, u32[]{:S(2)}, u32[]{:S(2)}) %collective-permute-start.4) | collective-permute-done | bytes 131104 | tf_op jit(solution)/shard_map/ppermute | solution.py:25
  62.3 4.3 %collective-permute-done.3 = bf16[128,512]{1,0:T(8,128)(2,1)S(1)} collective-permute-done((bf16[128,512]{1,0:T(8,128)(2,1)}, bf16[128,512]{1,0:T(8,128)(2,1)S(1)}, u32[]{:S(2)}, u32[]{:S(2)}) %collective-permute-start.3) | collective-permute-done | bytes 131104 | tf_op jit(solution)/shard_map/ppermute | solution.py:25
  66.6 0.8 broadcast.7.clone
  67.5 1.7 %constant_dynamic-update-slice_fusion.11 = (bf16[512,512]{1,0:T(8,128)(2,1)}, bf16[128,512]{1,0:T(8,128)(2,1)S(1)}) fusion(bf16[512,512]{1,0:T(8,128)(2,1)} %broadcast.7.clone, s32[]{:T(128)S(6)} %select_n.97, bf16[128,512]{1,0:T(8,128)(2,1)S(1)} %collective-permute-done.4, bf16[128,512]{1,0:T(8,128)(2,1)S(1)} %collective-permute-done.3, ...), kind=kLoop, calls=%fused_computation.44 | loop fusion | flops 458752 | bytes 917508 | tf_op jit(solution)/shard_map/dynamic_update_slice | solution.py:54
  69.1 1.8 %collective-permute-start.6 = (bf16[128,512]{1,0:T(8,128)(2,1)S(1)}, bf16[128,512]{1,0:T(8,128)(2,1)S(1)}, u32[]{:S(2)}, u32[]{:S(2)}) collective-permute-start(bf16[128,512]{1,0:T(8,128)(2,1)S(1)} %get-tuple-element.6), channel_id=1, source_target_pairs={{0,4},{1,5},{2,6},{3,7},{4,0},{5,1},{6,2},{7,3},{8,12},{9,13},{10,... | collective-permute-start | bytes 393224 | tf_op jit(solution)/shard_map/ppermute | solution.py:25
  70.9 5.3 %fusion.2 = f32[512,2048]{1,0:T(8,128)S(1)} fusion(bf16[1024,2048]{1,0:T(8,128)(2,1)} %copy-done.8, bf16[512,512]{1,0:T(8,128)(2,1)} %collective-permute-done.19, bf16[512,512]{1,0:T(8,128)(2,1)} %constant_dynamic-update-slice_fusion.4, pred[]{:T(512)S(6)} %eq.10), kind=kOutput, calls=%fused_computation.7 | convolution fusion | flops 2152202240 | bytes 9437185 | tf_op jit(solution)/shard_map/dot_general | solution.py:12
  76.3 2.6 %collective-permute-start.7 = (bf16[128,512]{1,0:T(8,128)(2,1)S(1)}, bf16[128,512]{1,0:T(8,128)(2,1)S(1)}, u32[]{:S(2)}, u32[]{:S(2)}) collective-permute-start(bf16[128,512]{1,0:T(8,128)(2,1)S(1)} %get-tuple-element.6), channel_id=1, source_target_pairs={{0,6},{1,7},{2,4},{3,5},{4,2},{5,3},{6,0},{7,1},{8,14},{9,15},{10,... | collective-permute-start | bytes 393224 | tf_op jit(solution)/shard_map/ppermute | solution.py:25
  78.9 0.7 constant_dynamic-update-slice_fusion.10
  79.6 0.7 constant_dynamic-update-slice_fusion.9
  80.3 2.9 %collective-permute-done.7 = bf16[128,512]{1,0:T(8,128)(2,1)S(1)} collective-permute-done((bf16[128,512]{1,0:T(8,128)(2,1)S(1)}, bf16[128,512]{1,0:T(8,128)(2,1)S(1)}, u32[]{:S(2)}, u32[]{:S(2)}) %collective-permute-start.7) | collective-permute-done | bytes 131104 | tf_op jit(solution)/shard_map/ppermute | solution.py:25
  83.1 0.7 constant_dynamic-update-slice_fusion.8
  84.3 1.1 fusion.1
  85.4 1.5 %collective-permute-start.20 = (bf16[256,2048]{1,0:T(8,128)(2,1)}, bf16[256,2048]{1,0:T(8,128)(2,1)}, u32[]{:S(2)}, u32[]{:S(2)}) collective-permute-start(bf16[256,2048]{1,0:T(8,128)(2,1)} %fusion.1), channel_id=1, source_target_pairs={{0,16},{8,24},{16,0},{24,8},{1,17},{9,25},{17,1},{25,9},{2,18},{10... | collective-permute-start | bytes 3145736 | tf_op jit(solution)/shard_map/ppermute | solution.py:25
  86.9 6.7 %collective-permute-done.8 = bf16[512,512]{1,0:T(8,128)(2,1)} collective-permute-done((bf16[512,512]{1,0:T(8,128)(2,1)}, bf16[512,512]{1,0:T(8,128)(2,1)}, u32[]{:S(2)}, u32[]{:S(2)}) %collective-permute-start.8) | collective-permute-done | bytes 524320 | tf_op jit(solution)/shard_map/ppermute | solution.py:25
  93.6 1.9 %maximum_select_fusion = bf16[1024,512]{1,0:T(8,128)(2,1)S(1)} fusion(bf16[512,512]{1,0:T(8,128)(2,1)} %collective-permute-done.8, bf16[512,512]{1,0:T(8,128)(2,1)} %constant_dynamic-update-slice_fusion.8, pred[]{:T(512)S(6)} %eq.10), kind=kLoop, calls=%fused_computation.5 | loop fusion | flops 4718592 | bytes 2097153 | tf_op jit(solution)/shard_map/jit(_where)/select_n | solution.py:56
  95.7 1.3 %fusion.15 = f32[512,1024]{1,0:T(8,128)S(1)} fusion(bf16[1024,512]{1,0:T(8,128)(2,1)S(1)} %maximum_select_fusion, bf16[1024,1024]{1,0:T(8,128)(2,1)S(1)} %constant_dynamic-update-slice_fusion.2), kind=kOutput, calls=%fused_computation.49 | convolution fusion | flops 1073741824 | bytes 5242880 | tf_op jit(solution)/shard_map/dot_general | solution.py:12
  97.0 1.5 %collective-permute-start.11 = (bf16[256,1024]{1,0:T(8,128)(2,1)S(1)}, bf16[256,1024]{1,0:T(8,128)(2,1)S(1)}, u32[]{:S(2)}, u32[]{:S(2)}) collective-permute-start(bf16[256,1024]{1,0:T(8,128)(2,1)S(1)} %fusion.10), channel_id=1, source_target_pairs={{0,16},{8,24},{16,0},{24,8},{1,17},{9,25},{17,1},{25,9},{2,18},{10... | collective-permute-start | bytes 1572872 | tf_op jit(solution)/shard_map/ppermute | solution.py:25
  98.6 13.2 %collective-permute-done.20 = bf16[256,2048]{1,0:T(8,128)(2,1)} collective-permute-done((bf16[256,2048]{1,0:T(8,128)(2,1)}, bf16[256,2048]{1,0:T(8,128)(2,1)}, u32[]{:S(2)}, u32[]{:S(2)}) %collective-permute-start.20) | collective-permute-done | bytes 1048608 | tf_op jit(solution)/shard_map/ppermute | solution.py:25
  111.8 2.9 %fusion = f32[256,2048]{1,0:T(8,128)} fusion(bf16[256,2048]{1,0:T(8,128)(2,1)} %collective-permute-done.20, f32[2,256,2048]{2,1,0:T(8,128)S(1)} %bitcast.35, s32[]{:T(128)S(6)} %select_n.104), kind=kLoop, calls=%fused_computation.1 | loop fusion | flops 1572864 | bytes 5242884 | tf_op jit(solution)/shard_map/mul | solution.py:104
  114.7 0.7 fusion.14
  115.9 1.7 %add_convert_fusion = bf16[512,1024]{1,0:T(8,128)(2,1)} fusion(f32[512,1024]{1,0:T(8,128)S(1)} %fusion.14, bf16[512,1024]{1,0:T(8,128)(2,1)S(1)} %bitcast.33, bf16[1024,512]{1,0:T(8,128)(2,1)S(1)} %maximum_select_fusion), kind=kOutput, calls=%fused_computation.3 | convolution fusion | flops 537919488 | bytes 4718592 | tf_op jit(solution)/shard_map/dot_general | solution.py:116
  117.6 1.1 fusion.8
  (46 shorter events, 3.9 us)
Async XLA Ops:
  0.6 3.1 %collective-permute-start.10 = (bf16[512,1024]{1,0:T(8,128)(2,1)}, bf16[512,1024]{1,0:T(8,128)(2,1)}, u32[]{:S(2)}, u32[]{:S(2)}) collective-permute-start(bf16[512,1024]{1,0:T(8,128)(2,1)} %param.4), channel_id=1, source_target_pairs={{0,8},{8,0},{16,24},{24,16},{1,9},{9,1},{17,25},{25,17},{2,10},{10... | collective-permute-start | bytes 3145736 | tf_op jit(solution)/shard_map/ppermute | solution.py:25
  1.1 25.3 %collective-permute-start = (bf16[512,2048]{1,0:T(8,128)(2,1)}, bf16[512,2048]{1,0:T(8,128)(2,1)}, u32[]{:S(2)}, u32[]{:S(2)}) collective-permute-start(bf16[512,2048]{1,0:T(8,128)(2,1)} %param.7), channel_id=1, source_target_pairs={{0,8},{8,0},{16,24},{24,16},{1,9},{9,1},{17,25},{25,17},{2,10},{10... | collective-permute-start | bytes 6291464 | tf_op jit(solution)/shard_map/ppermute | solution.py:25
  1.2 1.9 %copy-start.5 = (bf16[1024,1024]{1,0:T(8,128)(2,1)S(1)}, bf16[1024,1024]{1,0:T(8,128)(2,1)}, u32[]{:S(2)}) copy-start(bf16[1024,1024]{1,0:T(8,128)(2,1)} %param.5) | copy-start | bytes 6291460
  3.3 3.1 %copy-start = (bf16[2,1,256,1024]{3,2,1,0:T(8,128)(2,1)}, bf16[2,1,256,1024]{3,2,1,0:T(8,128)(2,1)S(1)}, u32[]{:S(2)}) copy-start(bf16[2,1,256,1024]{3,2,1,0:T(8,128)(2,1)S(1)} %get-tuple-element.7) | copy-start | bytes 3145732
  5.1 4.4 %copy-start.6 = (bf16[512,2048]{1,0:T(8,128)(2,1)S(1)}, bf16[512,2048]{1,0:T(8,128)(2,1)}, u32[]{:S(2)}) copy-start(bf16[512,2048]{1,0:T(8,128)(2,1)} %param.7) | copy-start | bytes 6291460
  6.5 3.1 %copy-start.7 = (bf16[1024,2048]{1,0:T(8,128)(2,1)S(1)}, bf16[1024,2048]{1,0:T(8,128)(2,1)}, u32[]{:S(2)}) copy-start(bf16[1024,2048]{1,0:T(8,128)(2,1)} %param.6) | copy-start | bytes 12582916
  6.5 15.2 %collective-permute-start.12 = (bf16[512,512]{1,0:T(8,128)(2,1)S(1)}, bf16[512,512]{1,0:T(8,128)(2,1)S(1)}, u32[]{:S(2)}, u32[]{:S(2)}) collective-permute-start(bf16[512,512]{1,0:T(8,128)(2,1)S(1)} %dynamic-slice_convert_fusion.1), channel_id=1, source_target_pairs={{0,1},{1,0},{2,3},{3,2},{4,5},{5,4},{6,7},{7,6},{8,9},{9,8},{10,11... | collective-permute-start | bytes 1572872 | tf_op jit(solution)/shard_map/ppermute | solution.py:25
  21.9 10.5 %collective-permute-start.15 = (bf16[128,512]{1,0:T(8,128)(2,1)S(1)}, bf16[128,512]{1,0:T(8,128)(2,1)S(1)}, u32[]{:S(2)}, u32[]{:S(2)}) collective-permute-start(bf16[128,512]{1,0:T(8,128)(2,1)S(1)} %get-tuple-element.10), channel_id=1, source_target_pairs={{0,6},{1,7},{2,4},{3,5},{4,2},{5,3},{6,0},{7,1},{8,14},{9,15},{10,... | collective-permute-start | bytes 393224 | tf_op jit(solution)/shard_map/ppermute | solution.py:25
  25.8 10.5 %collective-permute-start.14 = (bf16[128,512]{1,0:T(8,128)(2,1)S(1)}, bf16[128,512]{1,0:T(8,128)(2,1)S(1)}, u32[]{:S(2)}, u32[]{:S(2)}) collective-permute-start(bf16[128,512]{1,0:T(8,128)(2,1)S(1)} %get-tuple-element.11), channel_id=1, source_target_pairs={{0,4},{1,5},{2,6},{3,7},{4,0},{5,1},{6,2},{7,3},{8,12},{9,13},{10,... | collective-permute-start | bytes 393224 | tf_op jit(solution)/shard_map/ppermute | solution.py:25
  25.8 10.5 %collective-permute-start.13 = (bf16[128,512]{1,0:T(8,128)(2,1)S(1)}, bf16[128,512]{1,0:T(8,128)(2,1)S(1)}, u32[]{:S(2)}, u32[]{:S(2)}) collective-permute-start(bf16[128,512]{1,0:T(8,128)(2,1)S(1)} %get-tuple-element.9), channel_id=1, source_target_pairs={{0,2},{1,3},{2,0},{3,1},{4,6},{5,7},{6,4},{7,5},{8,10},{9,11},{10,... | collective-permute-start | bytes 393224 | tf_op jit(solution)/shard_map/ppermute | solution.py:25
  28.2 2.4 %copy-start.8 = (bf16[1024,2048]{1,0:T(8,128)(2,1)}, bf16[1024,2048]{1,0:T(8,128)(2,1)S(1)}, u32[]{:S(2)}) copy-start(bf16[1024,2048]{1,0:T(8,128)(2,1)S(1)} %constant_dynamic-update-slice_fusion) | copy-start | bytes 12582916
  30.6 22.6 %collective-permute-start.1 = (bf16[512,512]{1,0:T(8,128)(2,1)S(1)}, bf16[512,512]{1,0:T(8,128)(2,1)S(1)}, u32[]{:S(2)}, u32[]{:S(2)}) collective-permute-start(bf16[512,512]{1,0:T(8,128)(2,1)S(1)} %dynamic-slice_convert_fusion.3), channel_id=1, source_target_pairs={{0,1},{1,0},{2,3},{3,2},{4,5},{5,4},{6,7},{7,6},{8,9},{9,8},{10,11... | collective-permute-start | bytes 1572872 | tf_op jit(solution)/shard_map/ppermute | solution.py:25
  37.9 6.3 %collective-permute-start.16 = (bf16[128,512]{1,0:T(8,128)(2,1)S(1)}, bf16[128,512]{1,0:T(8,128)(2,1)S(1)}, u32[]{:S(2)}, u32[]{:S(2)}) collective-permute-start(bf16[128,512]{1,0:T(8,128)(2,1)S(1)} %get-tuple-element.4), channel_id=1, source_target_pairs={{0,2},{1,3},{2,0},{3,1},{4,6},{5,7},{6,4},{7,5},{8,10},{9,11},{10,... | collective-permute-start | bytes 393224 | tf_op jit(solution)/shard_map/ppermute | solution.py:25
  37.9 12.4 %collective-permute-start.17 = (bf16[128,512]{1,0:T(8,128)(2,1)S(1)}, bf16[128,512]{1,0:T(8,128)(2,1)S(1)}, u32[]{:S(2)}, u32[]{:S(2)}) collective-permute-start(bf16[128,512]{1,0:T(8,128)(2,1)S(1)} %get-tuple-element.4), channel_id=1, source_target_pairs={{0,4},{1,5},{2,6},{3,7},{4,0},{5,1},{6,2},{7,3},{8,12},{9,13},{10,... | collective-permute-start | bytes 393224 | tf_op jit(solution)/shard_map/ppermute | solution.py:25
  41.0 10.1 %collective-permute-start.18 = (bf16[128,512]{1,0:T(8,128)(2,1)S(1)}, bf16[128,512]{1,0:T(8,128)(2,1)S(1)}, u32[]{:S(2)}, u32[]{:S(2)}) collective-permute-start(bf16[128,512]{1,0:T(8,128)(2,1)S(1)} %get-tuple-element.4), channel_id=1, source_target_pairs={{0,6},{1,7},{2,4},{3,5},{4,2},{5,3},{6,0},{7,1},{8,14},{9,15},{10,... | collective-permute-start | bytes 393224 | tf_op jit(solution)/shard_map/ppermute | solution.py:25
  51.7 19.2 %collective-permute-start.19 = (bf16[512,512]{1,0:T(8,128)(2,1)}, bf16[512,512]{1,0:T(8,128)(2,1)}, u32[]{:S(2)}, u32[]{:S(2)}) collective-permute-start(bf16[512,512]{1,0:T(8,128)(2,1)} %constant_dynamic-update-slice_fusion.4), channel_id=1, source_target_pairs={{0,1},{1,0},{2,3},{3,2},{4,5},{5,4},{6,7},{7,6},{8,9},{9,8},{10,11... | collective-permute-start | bytes 1572872 | tf_op jit(solution)/shard_map/ppermute | solution.py:25
  53.5 1.0 copy-start.2
  55.2 7.1 %collective-permute-start.4 = (bf16[128,512]{1,0:T(8,128)(2,1)}, bf16[128,512]{1,0:T(8,128)(2,1)S(1)}, u32[]{:S(2)}, u32[]{:S(2)}) collective-permute-start(bf16[128,512]{1,0:T(8,128)(2,1)} %get-tuple-element.13), channel_id=1, source_target_pairs={{0,6},{1,7},{2,4},{3,5},{4,2},{5,3},{6,0},{7,1},{8,14},{9,15},{10,... | collective-permute-start | bytes 393224 | tf_op jit(solution)/shard_map/ppermute | solution.py:25
  56.7 10.0 %collective-permute-start.3 = (bf16[128,512]{1,0:T(8,128)(2,1)}, bf16[128,512]{1,0:T(8,128)(2,1)S(1)}, u32[]{:S(2)}, u32[]{:S(2)}) collective-permute-start(bf16[128,512]{1,0:T(8,128)(2,1)} %get-tuple-element.14), channel_id=1, source_target_pairs={{0,4},{1,5},{2,6},{3,7},{4,0},{5,1},{6,2},{7,3},{8,12},{9,13},{10,... | collective-permute-start | bytes 393224 | tf_op jit(solution)/shard_map/ppermute | solution.py:25
  58.0 8.7 %collective-permute-start.2 = (bf16[128,512]{1,0:T(8,128)(2,1)}, bf16[128,512]{1,0:T(8,128)(2,1)S(1)}, u32[]{:S(2)}, u32[]{:S(2)}) collective-permute-start(bf16[128,512]{1,0:T(8,128)(2,1)} %get-tuple-element.12), channel_id=1, source_target_pairs={{0,2},{1,3},{2,0},{3,1},{4,6},{5,7},{6,4},{7,5},{8,10},{9,11},{10,... | collective-permute-start | bytes 393224 | tf_op jit(solution)/shard_map/ppermute | solution.py:25
  69.1 9.8 %collective-permute-start.5 = (bf16[128,512]{1,0:T(8,128)(2,1)S(1)}, bf16[128,512]{1,0:T(8,128)(2,1)S(1)}, u32[]{:S(2)}, u32[]{:S(2)}) collective-permute-start(bf16[128,512]{1,0:T(8,128)(2,1)S(1)} %get-tuple-element.6), channel_id=1, source_target_pairs={{0,2},{1,3},{2,0},{3,1},{4,6},{5,7},{6,4},{7,5},{8,10},{9,11},{10,... | collective-permute-start | bytes 393224 | tf_op jit(solution)/shard_map/ppermute | solution.py:25
  69.1 10.5 %collective-permute-start.6 = (bf16[128,512]{1,0:T(8,128)(2,1)S(1)}, bf16[128,512]{1,0:T(8,128)(2,1)S(1)}, u32[]{:S(2)}, u32[]{:S(2)}) collective-permute-start(bf16[128,512]{1,0:T(8,128)(2,1)S(1)} %get-tuple-element.6), channel_id=1, source_target_pairs={{0,4},{1,5},{2,6},{3,7},{4,0},{5,1},{6,2},{7,3},{8,12},{9,13},{10,... | collective-permute-start | bytes 393224 | tf_op jit(solution)/shard_map/ppermute | solution.py:25
  76.3 8.0 %copy-start.3 = (f32[512,2048]{1,0:T(8,128)}, f32[512,2048]{1,0:T(8,128)S(1)}, u32[]{:S(2)}) copy-start(f32[512,2048]{1,0:T(8,128)S(1)} %fusion.2) | copy-start | bytes 12582916
  76.3 6.8 %collective-permute-start.7 = (bf16[128,512]{1,0:T(8,128)(2,1)S(1)}, bf16[128,512]{1,0:T(8,128)(2,1)S(1)}, u32[]{:S(2)}, u32[]{:S(2)}) collective-permute-start(bf16[128,512]{1,0:T(8,128)(2,1)S(1)} %get-tuple-element.6), channel_id=1, source_target_pairs={{0,6},{1,7},{2,4},{3,5},{4,2},{5,3},{6,0},{7,1},{8,14},{9,15},{10,... | collective-permute-start | bytes 393224 | tf_op jit(solution)/shard_map/ppermute | solution.py:25
  83.8 9.8 %collective-permute-start.8 = (bf16[512,512]{1,0:T(8,128)(2,1)}, bf16[512,512]{1,0:T(8,128)(2,1)}, u32[]{:S(2)}, u32[]{:S(2)}) collective-permute-start(bf16[512,512]{1,0:T(8,128)(2,1)} %constant_dynamic-update-slice_fusion.8), channel_id=1, source_target_pairs={{0,1},{1,0},{2,3},{3,2},{4,5},{5,4},{6,7},{7,6},{8,9},{9,8},{10,11... | collective-permute-start | bytes 1572872 | tf_op jit(solution)/shard_map/ppermute | solution.py:25
  85.4 26.4 %collective-permute-start.20 = (bf16[256,2048]{1,0:T(8,128)(2,1)}, bf16[256,2048]{1,0:T(8,128)(2,1)}, u32[]{:S(2)}, u32[]{:S(2)}) collective-permute-start(bf16[256,2048]{1,0:T(8,128)(2,1)} %fusion.1), channel_id=1, source_target_pairs={{0,16},{8,24},{16,0},{24,8},{1,17},{9,25},{17,1},{25,9},{2,18},{10... | collective-permute-start | bytes 3145736 | tf_op jit(solution)/shard_map/ppermute | solution.py:25
  95.6 16.2 %copy-start.4 = (f32[512,2048]{1,0:T(8,128)S(1)}, f32[512,2048]{1,0:T(8,128)}, u32[]{:S(2)}) copy-start(f32[512,2048]{1,0:T(8,128)} %copy-done.3) | copy-start | bytes 12582916
  95.6 19.1 %collective-permute-start.9 = (bf16[512,512]{1,0:T(8,128)(2,1)S(1)}, bf16[512,512]{1,0:T(8,128)(2,1)S(1)}, u32[]{:S(2)}, u32[]{:S(2)}) collective-permute-start(bf16[512,512]{1,0:T(8,128)(2,1)S(1)} %slice.9), channel_id=1, source_target_pairs={{0,8},{8,0},{16,24},{24,16},{1,9},{9,1},{17,25},{25,17},{2,10},{10... | collective-permute-start | bytes 1572872 | tf_op jit(solution)/shard_map/ppermute | solution.py:25
  97.0 20.6 %collective-permute-start.11 = (bf16[256,1024]{1,0:T(8,128)(2,1)S(1)}, bf16[256,1024]{1,0:T(8,128)(2,1)S(1)}, u32[]{:S(2)}, u32[]{:S(2)}) collective-permute-start(bf16[256,1024]{1,0:T(8,128)(2,1)S(1)} %fusion.10), channel_id=1, source_target_pairs={{0,16},{8,24},{16,0},{24,8},{1,17},{9,25},{17,1},{25,9},{2,18},{10... | collective-permute-start | bytes 1572872 | tf_op jit(solution)/shard_map/ppermute | solution.py:25
  114.7 1.2 %copy-start.1 = (bf16[2,1,256,1024]{3,2,1,0:T(8,128)(2,1)S(1)}, bf16[2,1,256,1024]{3,2,1,0:T(8,128)(2,1)}, u32[]{:S(2)}) copy-start(bf16[2,1,256,1024]{3,2,1,0:T(8,128)(2,1)} %copy-done) | copy-start | bytes 3145732

commit v2 on v0

v2 whole, which is shorter than its diff:
```python
import functools
import math

import jax
import jax.numpy as jnp
from jax import lax
from jax.experimental import pallas as pl
from jax.experimental.pallas import tpu as pltpu
from jax.sharding import PartitionSpec as P

CHUNKS = 2
NAMES = {"G": "latent_grad", "L": "latent", "x": "far", "c": "core"}
ORDER = (
    "G0S", "G1S", "LS", "own", "GK", "G0near", "LK", "G1near", "G0far", "L0near", "G1far",
    "L1near", "L0far", "G0last", "G1last", "L1far", "G0join", "L0last", "G1join", "L0stack",
    "L1last", "G0halves", "L0join", "og", "L1stack", "G1halves", "G0left", "L1join", "G1left",
    "input", "Lrn", "Lrf", "final",
)
HALVES = {"G": (True, True), "L": (True, False)}
BF16 = jnp.bfloat16
F32 = jnp.float32
MIB = 1 << 20
COLS = (((1,), (1,)), ((), ()))
ROWS = (((0,), (0,)), ((), ()))


def dot(first, second, dims):
    return lax.dot_general(first, second, dims, preferred_element_type=F32)


def cost(flops, *arrays):
    sizes = []
    for array in arrays:
        shape, dtype = array if isinstance(array, tuple) else (array.shape, array.dtype)
        sizes.append(math.prod(shape) * jnp.dtype(dtype).itemsize)
    return pl.CostEstimate(flops=flops, bytes_accessed=sum(sizes), transcendentals=0)


def whole_call(kernel, where, values, outs, scratch=(), flops=0):
    return pl.pallas_call(
        kernel,
        out_shape=[jax.ShapeDtypeStruct(s, t) for s, t in outs],
        in_specs=[pl.BlockSpec(memory_space=pltpu.SMEM)]
        + [pl.BlockSpec(memory_space=pltpu.VMEM)] * len(values),
        out_specs=[pl.BlockSpec(memory_space=pltpu.VMEM)] * len(outs),
        scratch_shapes=list(scratch),
        compiler_params=pltpu.CompilerParams(vmem_limit_bytes=24 * MIB),
        cost_estimate=cost(flops, *values, *outs),
    )(where, *values)


def swap(value, axis, mask):
    size = lax.axis_size(axis)
    return lax.ppermute(value, axis, [(i, i ^ mask) for i in range(size)])


def tied(value, run):
    return lax.optimization_barrier((value, run.last))[0]


class InOrder:
    def __init__(self):
        self.last = ()

    def __call__(self, step, *values):
        values, _ = lax.optimization_barrier((values, self.last))
        result = step(*values)
        self.last = result
        return result


def product_kernel(chunks, where, *refs):
    values, factor, outs = refs[:-chunks - 1], refs[-chunks - 1], refs[-chunks:]
    count, width = outs[0].shape[0], outs[0].shape[2]
    flat = factor[...].reshape(count * chunks * width, factor.shape[-1])
    rows = values[0].shape[0]
    for i, value in enumerate(values):
        result = dot(value[...], flat, COLS)
        for j in range(count):
            for c in range(chunks):
                lane = (j * chunks + c) * width
                part = result[:, lane : lane + width]
                outs[c][j, i * rows : (i + 1) * rows, :] = part.astype(outs[c].dtype)


def products(where, which, values, factor, block, place, dtype, batch, chunks, limit):
    rows, depth = values[0].shape
    half = rows // 2
    width = block[-2]
    count = math.prod(block[:-3])
    total = half * len(values)

    def half_of(i, where):
        return (where[0] if which else 1 - where[0], 0)

    return pl.pallas_call(
        functools.partial(product_kernel, chunks),
        out_shape=[jax.ShapeDtypeStruct((count, total, width), dtype)] * chunks,
        grid_spec=pltpu.PrefetchScalarGridSpec(
            num_scalar_prefetch=1,
            grid=(count // batch,),
            in_specs=[pl.BlockSpec((half, depth), half_of)] * len(values)
            + [pl.BlockSpec((batch,) + block[1:], place)],
            out_specs=[pl.BlockSpec((batch, total, width), lambda i, where: (i, 0, 0))] * chunks,
        ),
        compiler_params=pltpu.CompilerParams(vmem_limit_bytes=limit * MIB),
        cost_estimate=cost(
            2 * total * depth * count * chunks * width,
            *values,
            ((count, chunks, width, depth), BF16),
        ),
    )(where, *values, factor)


def split_kernel(where, kept, sent, mine, away):
    rows = mine.shape[1]
    if rows == kept.shape[1]:
        total = kept[...] + sent[...].astype(F32)
        mine[...] = total
        away[...] = total.astype(BF16)
        return
    for out, at in ((mine, where[4]), (away, 1 - where[4])):
        span = pl.ds(pl.multiple_of(at * rows, rows), rows)
        out[...] = (kept[:, span, :] + sent[:, span, :].astype(F32)).astype(out.dtype)


def split(where, parts, kept, sent):
    count, rows, width = kept.shape
    shape = (count, rows // parts, width)
    return whole_call(split_kernel, where, [kept, sent], [(shape, F32), (shape, BF16)])


def added_kernel(where, mine, other, out, away):
    total = mine[...] + other[...].astype(F32)
    out[...] = total
    away[...] = total.astype(BF16)


def added(where, mine, other):
    return whole_call(
        added_kernel, where, [mine, other], [(mine.shape, F32), (mine.shape, BF16)]
    )


def summed_kernel(where, mine, other, out):
    out[...] = (mine[...] + other[...].astype(F32)).astype(BF16)


def summed(where, mine, other):
    return whole_call(summed_kernel, where, [mine, other], [(mine.shape, BF16)])[0]


def summed_by_owner_kernel(where, mine, other, *outs):
    for step, out in enumerate(outs):
        at = where[3] ^ step
        out[...] = (mine[at] + other[at].astype(F32)).astype(BF16)


def summed_by_owner(where, mine, other):
    owners = mine.shape[0]
    return whole_call(
        summed_by_owner_kernel, where, [mine, other], [(mine.shape[1:], BF16)] * owners
    )


def stacked_kernel(where, *refs):
    *pieces, out = refs
    for i, piece in enumerate(pieces):
        out[i] = piece[...]


def stacked(where, *pieces):
    return whole_call(
        stacked_kernel, where, list(pieces), [((len(pieces),) + pieces[0].shape, BF16)]
    )[0]


def joined_kernel(where, mine, other, out):
    rows = mine.shape[1]
    for part, at in ((mine, where[4]), (other, 1 - where[4])):
        out[:, pl.ds(pl.multiple_of(at * rows, rows), rows), :] = part[...]


def joined(where, mine, other):
    count, rows, width = mine.shape
    return whole_call(joined_kernel, where, [mine, other], [((count, 2 * rows, width), BF16)])[0]


def halves_kernel(owners, where, near, far, out):
    for i, part in enumerate((near, far)):
        for owner in range(owners):
            out[i, owner] = part[owner * 2 + 1 - where[2]]


def halves(where, owners, near, far):
    return whole_call(
        functools.partial(halves_kernel, owners),
        where,
        [near, far],
        [((2, owners) + near.shape[1:], BF16)],
    )[0]


def left_kernel(owners, where, near, far, theirs, acts, acts_other, mine, *rest):
    blocks, (ordered, result) = rest[: owners - 1], rest[owners - 1 :]
    _, share, width = near.shape
    for i, part in enumerate((near, far)):
        low = where[0] if i == 0 else 1 - where[0]
        span = pl.ds(pl.multiple_of(low * share, share), share)
        for owner in range(owners):
            lanes = slice(owner * width, (owner + 1) * width)
            ordered[0, span, lanes] = part[owner * 2 + where[2]]
            ordered[1, span, lanes] = theirs[i, owner]
    result[...] = dot(ordered[0], acts[...], ROWS) + dot(ordered[1], acts_other[...], ROWS)
    for step in range(owners):
        rows = pl.ds(pl.multiple_of((where[3] ^ step) * width, width), width)
        if step:
            blocks[step - 1][...] = result[rows, :].astype(BF16)
        else:
            mine[...] = result[rows, :]


def left_parts(where, owners, near, far, theirs, acts, acts_other):
    width = near.shape[-1]
    tokens, depth = acts.shape
    mine, *blocks = whole_call(
        functools.partial(left_kernel, owners),
        where,
        [near, far, theirs, acts, acts_other],
        [((width, depth), F32)] + [((width, depth), BF16)] * (owners - 1),
        [
            pltpu.VMEM((2, tokens, owners * width), BF16),
            pltpu.VMEM((owners * width, depth), F32),
        ],
        4 * tokens * owners * width * depth,
    )
    return mine, blocks


def input_kernel(count, where, *refs):
    parts, (factor, out, ordered) = refs[: 2 * count], refs[2 * count :]
    groups, share, width = parts[0].shape
    block = out.shape[1]

    @pl.when(pl.program_id(0) == 0)
    def _():
        for chunk in range(count):
            for i in range(2):
                low = where[0] if i == 0 else 1 - where[0]
                span = pl.ds(pl.multiple_of(low * share, share), share)
                for group in range(groups):
                    lane = (group * count + chunk) * width
                    ordered[span, lane : lane + width] = parts[2 * chunk + i][group]

    columns = pl.ds(pl.multiple_of(pl.program_id(0) * block, block), block)
    out[...] = jnp.dot(
        ordered[...], factor[:, columns], preferred_element_type=F32
    ).astype(BF16)


def input_product(where, parts, factor, tokens):
    rank, depth = factor.shape
    block = min(depth, 512)
    values = [*parts, factor]
    return pl.pallas_call(
        functools.partial(input_kernel, len(parts) // 2),
        out_shape=jax.ShapeDtypeStruct((tokens, depth), BF16),
        grid=(depth // block,),
        in_specs=[pl.BlockSpec(memory_space=pltpu.SMEM)]
        + [pl.BlockSpec(memory_space=pltpu.VMEM)] * len(values),
        out_specs=pl.BlockSpec((tokens, block), lambda i: (0, i)),
        scratch_shapes=[pltpu.VMEM((tokens, rank), BF16)],
        compiler_params=pltpu.CompilerParams(vmem_limit_bytes=24 * MIB),
        cost_estimate=cost(2 * tokens * rank * depth, *values),
    )(where, *values)


def right_kernel(owners, near, scale, where, *refs):
    parts, refs = refs[:CHUNKS], refs[CHUNKS:]
    grads, refs = refs[: 2 * owners], refs[2 * owners :]
    done, (out, ordered) = refs[:-2], refs[-2:]
    share, width = parts[0].shape[1] // 2, parts[0].shape[2]
    block = out.shape[1]
    blocks = len(grads) * share

    @pl.when(pl.program_id(0) == 0)
    def _():
        for c, part in enumerate(parts):
            lanes = slice(c * width, (c + 1) * width)
            ordered[:, lanes] = part[...].reshape(blocks, width)

    low = where[0] if near else 1 - where[0]
    span = pl.ds(pl.multiple_of(low * share, share), share)
    columns = pl.ds(pl.multiple_of(pl.program_id(0) * block, block), block)
    total = None
    for i, grad in enumerate(grads):
        term = dot(ordered[i * share : (i + 1) * share, :], grad[span, columns], ROWS)
        total = term if total is None else total + term
    if done:
        total = (done[0][:, columns] + total) * scale
    out[...] = total


def right_rows(where, near, scale, parts, grads, done):
    owners, rows, width = parts[0].shape
    columns = grads[0].shape[1]
    block = min(columns, 512)
    values = [*parts, *grads, *done]
    return pl.pallas_call(
        functools.partial(right_kernel, owners, near, scale),
        out_shape=jax.ShapeDtypeStruct((CHUNKS * width, columns), F32),
        grid=(columns // block,),
        in_specs=[pl.BlockSpec(memory_space=pltpu.SMEM)]
        + [pl.BlockSpec(memory_space=pltpu.VMEM)] * len(values),
        out_specs=pl.BlockSpec((CHUNKS * width, block), lambda i: (0, i)),
        scratch_shapes=[pltpu.VMEM((owners * rows, CHUNKS * width), BF16)],
        compiler_params=pltpu.CompilerParams(vmem_limit_bytes=32 * MIB),
        cost_estimate=cost(2 * owners * rows * CHUNKS * width * columns, *parts, *grads),
    )(where, *values)


def final_kernel(scale, count, where, *refs):
    out = refs[-1]
    per = (len(refs) - 1) // count
    width = refs[0].shape[0]
    for chunk in range(count):
        total = refs[chunk * per][...]
        for other in refs[chunk * per + 1 : (chunk + 1) * per]:
            total = total + other[...].astype(F32)
        out[chunk * width : (chunk + 1) * width, :] = total * scale


def shards(activations, left_factor, right_factor, out_grad):
    groups = lax.axis_size("dp")
    width = lax.axis_size("tensor")
    tokens, depth = activations.shape
    rank = left_factor.shape[0]
    owners, peers = groups // 2, width // 2
    rows = rank // groups
    step = rows // CHUNKS
    scale = 1.0 / math.sqrt(tokens * groups)
    place, spot = lax.axis_index("tensor"), lax.axis_index("dp")
    where = jnp.stack([place % 2, place // 2, spot % 2, spot // 2, place // 2 % 2])
    where = where.astype(jnp.int32)
    run = InOrder()

    left_blocks = left_factor.reshape(owners, 2, CHUNKS, step, depth)
    right_blocks = right_factor.reshape(groups, CHUNKS, step, out_grad.shape[1])

    features = out_grad.shape[1]

    def grad_product(which, dtype, first, chunks, limit):
        return lambda *values: products(
            where,
            which,
            values,
            right_blocks,
            (groups, chunks, step, features),
            lambda i, where: (i, first, 0, 0),
            dtype,
            2,
            chunks,
            limit,
        )

    def latent_product(which, dtype):
        return lambda *values: products(
            where,
            which,
            values,
            left_blocks,
            (owners, 1, CHUNKS, step, depth),
            lambda i, where: (i, where[2], 0, 0, 0),
            dtype,
            owners,
            CHUNKS,
            24,
        )

    def halve(which, c):
        return 2 if HALVES[which][c] and peers > 1 else 1

    kept, piece, comes, near, far, latest = ({} for _ in range(6))
    theirs, left_mine, left_in = {}, {}, {}
    first_mask, masks = 2, []
    mask = 4
    while mask < width:
        masks.append(mask)
        mask *= 2

    def scoped(name, c, stage):
        return jax.named_scope(f"{NAMES[name]}{c}_{stage}")

    def grad_send(c, limit):
        with scoped("G", c, "S"):
            (away,) = run(grad_product(0, BF16, c, 1, limit), out_grad)
            comes["G", c] = latest["G", c] = swap(away, "tensor", 1)

    def grad_keep():
        with scoped("G", "", "K"):
            for c, value in enumerate(run(grad_product(1, F32, 0, CHUNKS, 24), out_grad)):
                kept["G", c] = value

    def latent_send():
        with scoped("L", "", "S"):
            for c, value in enumerate(run(latent_product(0, BF16), *acts)):
                comes["L", c] = latest["L", c] = swap(value, "tensor", 1)

    def latent_keep():
        with scoped("L", "", "K"):
            for c, value in enumerate(run(latent_product(1, F32), *acts)):
                kept["L", c] = value

    def near_sum(name, c):
        parts = halve(name, c)
        with scoped(name, c, "near"):
            piece[name, c], away = run(
                lambda a, b: split(where, parts, a, b), kept[name, c], comes[name, c]
            )
            comes[name, c] = latest[name, c] = swap(away, "tensor", first_mask)

    def far_sum(name, c):
        for mask in masks:
            with scoped(name, c, "far"):
                piece[name, c], away = run(
                    functools.partial(added, where), piece[name, c], comes[name, c]
                )
                comes[name, c] = latest[name, c] = swap(away, "tensor", mask)

    def last_sum(name, c):
        with scoped(name, c, "last"):
            if name == "G":
                piece[name, c] = run(
                    functools.partial(summed, where), piece[name, c], comes[name, c]
                )
                forward(name, c)
            else:
                own, *others = run(
                    functools.partial(summed_by_owner, where), piece[name, c], comes[name, c]
                )
                others = [swap(v, "dp", 2 * s) for s, v in enumerate(others, 1)]
                piece[name, c], latest[name, c] = [own, *others], others

    def forward(name, c):
        if halve(name, c) == 2:
            comes[name, c] = latest[name, c] = swap(piece[name, c], "tensor", first_mask)
        else:
            spread(name, c, piece[name, c])

    def spread(name, c, value):
        near[name, c] = value
        far[name, c] = latest[name, c] = swap(value, "tensor", 1)

    def stack(name, c):
        with scoped(name, c, "stack"):
            piece[name, c] = run(functools.partial(stacked, where), *piece[name, c])
            forward(name, c)

    def join(name, c):
        if halve(name, c) == 2:
            with scoped(name, c, "join"):
                spread(
                    name, c, run(functools.partial(joined, where), piece[name, c], comes[name, c])
                )

    def core_halves(c):
        with scoped("G", c, "halves"):
            theirs[c] = latest["G", c] = swap(
                run(lambda a, b: halves(where, owners, a, b), near["G", c], far["G", c]), "dp", 1
            )

    def left(c):
        with scoped("G", c, "left"):
            left_mine[c], out = run(
                lambda *v: left_parts(where, owners, *v),
                near["G", c],
                far["G", c],
                theirs[c],
                *acts,
            )
            left_in[c] = latest["G", c] = [swap(v, "dp", 2 * s) for s, v in enumerate(out, 1)]

    def inputs():
        with scoped("G", "", "input"):
            return run(
                lambda f, *v: input_product(where, v, f, tokens),
                left_factor,
                *(v for c in range(CHUNKS) for v in [near["G", c], far["G", c]]),
            )

    def rights(stage, *done):
        parts = near if stage == "rn" else far
        with scoped("L", "", stage):
            return run(
                lambda *v: right_rows(
                    where, stage == "rn", scale, v[:CHUNKS], v[CHUNKS : CHUNKS + 2 * owners], v[CHUNKS + 2 * owners :]
                ),
                *(parts["L", c] for c in range(CHUNKS)),
                *grads,
                *done,
            )

    def final():
        with scoped("G", "", "final"):
            return run(
                lambda *v: whole_call(
                    functools.partial(final_kernel, scale, CHUNKS), where, v, [((rows, depth), F32)]
                )[0],
                *(v for c in range(CHUNKS) for v in [left_mine[c], *left_in[c]]),
            )

    def settle(*values):
        run.last = (run.last, values)

    with scoped("x", "", "og"):
        far_grads = [swap(out_grad, "dp", 2 * s) for s in range(1, owners)]
    with scoped("c", "", "acts"):
        acts = (activations, swap(activations, "dp", 1))
    with scoped("c", "", "own"):
        grads = [out_grad, swap(out_grad, "dp", 1)]

    def far_swaps():
        with scoped("c", "", "far"):
            for block in far_grads:
                grads.extend([block, swap(tied(block, run), "dp", 1)])
    input_grad = right_grad = left_grad = None
    actions = {
        "near": near_sum,
        "far": far_sum,
        "last": last_sum,
        "join": join,
        "stack": stack,
    }
    for entry in ORDER:
        if entry == "GK":
            grad_keep()
        elif entry == "LS":
            latent_send()
        elif entry == "LK":
            latent_keep()
        elif entry == "Lrn":
            right_near = rights("rn")
        elif entry == "Lrf":
            right_grad = rights("rf", right_near)
        elif entry == "input":
            input_grad = inputs()
        elif entry == "final":
            left_grad = final()
        elif entry == "own":
            settle(grads[1])
        elif entry == "og":
            far_swaps()
        elif entry == "@og":
            settle(*grads)
        elif entry[0] == "@":
            settle(latest[entry[1], int(entry[2])])
        else:
            name, c, stage = entry[0], int(entry[1]), entry[2:]
            if stage == "S":
                grad_send(c, 24)
            elif stage == "halves":
                core_halves(c)
            elif stage == "left":
                left(c)
            else:
                actions[stage](name, c)
    return input_grad, left_grad, right_grad


def solution(mesh):
    placed = (P("dp", "tensor"), P(None, "tensor"), P(None, "tensor"), P("dp", "tensor"))
    return jax.shard_map(
        shards,
        mesh=mesh,
        in_specs=placed,
        out_specs=(P("dp", "tensor"), P("dp", "tensor"), P("dp", "tensor")),
        check_vma=False,
    )
```

time: 319 us -> 97.9 us (0.31)
  blocking collectives: 169 us -> 0 us
  waiting for transfers between devices: 104 us -> 23.8 us
  Pallas kernels: 0 us -> 35 us
  starting transfers between devices: 0.08 us -> 34 us
  matrix products: 24.7 us -> 0 us
  between operations: 14.1 us -> 0.95 us
  other arithmetic: 5.55 us -> 0 us
    psum x1 -> x0, blocking collectives: 169 us -> none  [shards(): latent_grad = lax.psum(grad_part, 'tensor').astype(jnp.bfloat16)]
    reduce_scatter x2 -> x0, waiting for transfers between devices: 104 us -> none  [the longest x1 72.2 us: shards(): lax.psum_scatter(contract_rows(columns, out_grad), 'dp', scatter_dimensio...]
    pallas_call x0 -> x30, Pallas kernels: none -> 35 us  [the longest x22 15.4 us: whole_call(): pl.pallas_call(kernel, out_shape=[jax.ShapeDtypeStruct(s, t) for s, t in...]
    ppermute x0 -> x29, starting transfers between devices: none -> 34 us  [swap(): return lax.ppermute(value, axis, [(i, i ^ mask) for i in range(size)])]
    dot_general x5 -> x0, matrix products: 24.7 us -> none  [the longest x2 12.1 us: contract_rows(): lax.dot_general(first, second, (((0,), (0,)), ((), ())), preferred_elemen...]
    ppermute x0 -> x29, waiting for transfers between devices: none -> 23.8 us  [swap(): return lax.ppermute(value, axis, [(i, i ^ mask) for i in range(size)])]
    mul x2 -> x0, other arithmetic: 5.55 us -> none  [shards(): return (input_grad, left_sum * scale, right_sum * scale)]
  transfers between devices with their start and end apart: 2 -> 29, of which waited for: 2 -> 11; matrix products, arithmetic and copies ran while one was open for 4% -> 0% of each run, Pallas kernels for 0% -> 34%
where the time goes in v2:
time: 97.9 us; the launch traced here: 97.6 us
  Pallas kernels  35 us (36%)
  starting transfers between devices  34 us (35%)
  waiting for transfers between devices  23.8 us (24%)
  local copies, waits for them, and re-layouts  3.88 us (4%)
    ppermute x29, starting transfers between devices, swap(): return lax.ppermute(value, axis, [(i, i ^ mask) for i in range(size)])  34 us
    ppermute x29, waiting for transfers between devices, swap(): return lax.ppermute(value, axis, [(i, i ^ mask) for i in range(size)])  23.8 us
    pallas_call x22, Pallas kernels, whole_call(): pl.pallas_call(kernel, out_shape=[jax.ShapeDtypeStruct(s, t) for s, t in...  15.4 us
    pallas_call x2, Pallas kernels, right_rows(): pl.pallas_call(functools.partial(right_kernel, owners, near, scale), out_...  8.49 us
    pallas_call x5, Pallas kernels, products(): pl.pallas_call(functools.partial(product_kernel, chunks), out_shape=[jax....  8 us
    unnamed x12, local copies, waits for them, and re-layouts  3.8 us
    pallas_call x1, Pallas kernels, input_product(): pl.pallas_call(functools.partial(input_kernel, len(parts) // 2), out_shap...  3.1 us
  transfers between devices with their start and end apart: 29, of which 11 were waited for; matrix products, arithmetic and copies ran while one was open for 0% of the time, Pallas kernels for 34%

profile of v2, /device:TPU:0, one launch (start us, length us, event | category | flops | bytes accessed | tf_op | source)
XLA Modules:
  0.0 97.6 jit_solution(3574099568942828610)
XLA Ops:
  1.1 2.6 %collective-permute-start.27 = (bf16[512,2048]{1,0:T(8,128)(2,1)}, bf16[512,2048]{1,0:T(8,128)(2,1)}, u32[]{:S(2)}, u32[]{:S(2)}) collective-permute-start(bf16[512,2048]{1,0:T(8,128)(2,1)} %refs_2_.1), channel_id=1, source_target_pairs={{0,16},{8,24},{16,0},{24,8},{1,17},{9,25},{17,1},{25,9},{2,18},{10... | collective-permute-start | bytes 6291464 | tf_op jit(solution)/shard_map/far_og/ppermute | solution.py:54
  4.0 1.6 %copy-done = bf16[512,2048]{1,0:T(8,128)(2,1)S(1)} copy-done((bf16[512,2048]{1,0:T(8,128)(2,1)S(1)}, bf16[512,2048]{1,0:T(8,128)(2,1)}, u32[]{:S(2)}) %copy-start) | copy-done | bytes 2097176
  5.6 2.2 %copy-done.2 = bf16[1024,2048]{1,0:T(8,128)(2,1)S(1)} copy-done((bf16[1024,2048]{1,0:T(8,128)(2,1)S(1)}, bf16[1024,2048]{1,0:T(8,128)(2,1)}, u32[]{:S(2)}) %copy-start.2) | copy-done | bytes 4194328
  7.7 1.7 %latent_grad0_S.1 = bf16[4,256,128]{2,1,0:T(8,128)(2,1)S(1)} custom-call(s32[5]{0:T(128)S(1)} %stack.23.where, bf16[512,2048]{1,0:T(8,128)(2,1)S(1)} %copy-done, bf16[4,2,128,2048]{3,2,1,0:T(8,128)(2,1)S(1)} %bitcast.7), custom_call_target="tpu_custom_call" | custom-call | flops 536870912 | bytes 4194304 | tf_op jit(solution)/shard_map/latent_grad0_S/pallas_call | solution.py:96
  9.5 1.6 %collective-permute-start.2 = (bf16[4,256,128]{2,1,0:T(8,128)(2,1)S(1)}, bf16[4,256,128]{2,1,0:T(8,128)(2,1)S(1)}, u32[]{:S(2)}, u32[]{:S(2)}) collective-permute-start(bf16[4,256,128]{2,1,0:T(8,128)(2,1)S(1)} %latent_grad0_S.1), channel_id=1, source_target_pairs={{0,1},{1,0},{2,3},{3,2},{4,5},{5,4},{6,7},{7,6},{8,9},{9,8},{10,11... | collective-permute-start | bytes 786440 | tf_op jit(solution)/shard_map/latent_grad0_S/ppermute | solution.py:54
  11.0 1.7 %latent_grad1_S.1 = bf16[4,256,128]{2,1,0:T(8,128)(2,1)S(1)} custom-call(s32[5]{0:T(128)S(1)} %stack.23.where, bf16[512,2048]{1,0:T(8,128)(2,1)S(1)} %copy-done, bf16[4,2,128,2048]{3,2,1,0:T(8,128)(2,1)S(1)} %bitcast.8), custom_call_target="tpu_custom_call" | custom-call | flops 536870912 | bytes 4194304 | tf_op jit(solution)/shard_map/latent_grad1_S/pallas_call | solution.py:96
  13.3 1.3 %latent_S.1 = (bf16[2,512,128]{2,1,0:T(8,128)(2,1)S(1)}, bf16[2,512,128]{2,1,0:T(8,128)(2,1)S(1)}) custom-call(s32[5]{0:T(128)S(1)} %stack.23.where, bf16[512,1024]{1,0:T(8,128)(2,1)S(1)} %copy-done.5, bf16[512,1024]{1,0:T(8,128)(2,1)S(1)} %collective-permute-done.refs_1_.acts_other, bf16[2,2,2,128,1024]{4,3,2,1,0:T(8,128)(2,1)S(1)} %bitcast.10), custom_call_target="tpu_custom_call" | custom-call | flops 536870912 | bytes 3145728 | tf_op jit(solution)/shard_map/latent_S/pallas_call | solution.py:96
  14.6 1.6 %collective-permute-start.6 = (bf16[2,512,128]{2,1,0:T(8,128)(2,1)S(1)}, bf16[2,512,128]{2,1,0:T(8,128)(2,1)S(1)}, u32[]{:S(2)}, u32[]{:S(2)}) collective-permute-start(bf16[2,512,128]{2,1,0:T(8,128)(2,1)S(1)} %get-tuple-element.113), channel_id=1, source_target_pairs={{0,1},{1,0},{2,3},{3,2},{4,5},{5,4},{6,7},{7,6},{8,9},{9,8},{10,11... | collective-permute-start | bytes 786440 | tf_op jit(solution)/shard_map/latent_S/ppermute | solution.py:54
  16.7 2.1 %latent_grad_K.1 = (f32[4,256,128]{2,1,0:T(8,128)S(1)}, f32[4,256,128]{2,1,0:T(8,128)S(1)}) custom-call(s32[5]{0:T(128)S(1)} %stack.23.where, bf16[512,2048]{1,0:T(8,128)(2,1)S(1)} %copy-done.1, bf16[4,2,128,2048]{3,2,1,0:T(8,128)(2,1)S(1)} %bitcast.9), custom_call_target="tpu_custom_call" | custom-call | flops 1073741824 | bytes 6291456 | tf_op jit(solution)/shard_map/latent_grad_K/pallas_call | solution.py:96
  18.8 0.6 latent_grad0_near.1
  19.4 1.6 %collective-permute-start.3 = (bf16[4,128,128]{2,1,0:T(8,128)(2,1)S(1)}, bf16[4,128,128]{2,1,0:T(8,128)(2,1)S(1)}, u32[]{:S(2)}, u32[]{:S(2)}) collective-permute-start(bf16[4,128,128]{2,1,0:T(8,128)(2,1)S(1)} %get-tuple-element.121), channel_id=1, source_target_pairs={{0,2},{1,3},{2,0},{3,1},{4,6},{5,7},{6,4},{7,5},{8,10},{9,11},{10,... | collective-permute-start | bytes 393224 | tf_op jit(solution)/shard_map/latent_grad0_near/ppermute | solution.py:54
  21.1 1.3 %latent_K.1 = (f32[2,512,128]{2,1,0:T(8,128)S(1)}, f32[2,512,128]{2,1,0:T(8,128)S(1)}) custom-call(s32[5]{0:T(128)S(1)} %stack.23.where, bf16[512,1024]{1,0:T(8,128)(2,1)S(1)} %copy-done.5, bf16[512,1024]{1,0:T(8,128)(2,1)S(1)} %collective-permute-done.refs_1_.acts_other, bf16[2,2,2,128,1024]{4,3,2,1,0:T(8,128)(2,1)S(1)} %bitcast.11), custom_call_target="tpu_custom_call" | custom-call | flops 536870912 | bytes 3145728 | tf_op jit(solution)/shard_map/latent_K/pallas_call | solution.py:96
  22.3 1.9 %collective-permute-done.4.sent = bf16[4,256,128]{2,1,0:T(8,128)(2,1)S(1)} collective-permute-done((bf16[4,256,128]{2,1,0:T(8,128)(2,1)S(1)}, bf16[4,256,128]{2,1,0:T(8,128)(2,1)S(1)}, u32[]{:S(2)}, u32[]{:S(2)}) %collective-permute-start.4) | collective-permute-done | bytes 262176 | tf_op jit(solution)/shard_map/latent_grad1_S/ppermute | solution.py:54
  24.3 0.6 latent_grad1_near.1
  24.9 1.6 %collective-permute-start.9 = (bf16[4,128,128]{2,1,0:T(8,128)(2,1)S(1)}, bf16[4,128,128]{2,1,0:T(8,128)(2,1)S(1)}, u32[]{:S(2)}, u32[]{:S(2)}) collective-permute-start(bf16[4,128,128]{2,1,0:T(8,128)(2,1)S(1)} %get-tuple-element.129), channel_id=1, source_target_pairs={{0,2},{1,3},{2,0},{3,1},{4,6},{5,7},{6,4},{7,5},{8,10},{9,11},{10,... | collective-permute-start | bytes 393224 | tf_op jit(solution)/shard_map/latent_grad1_near/ppermute | solution.py:54
  27.1 2.7 %collective-permute-start.5 = (bf16[4,128,128]{2,1,0:T(8,128)(2,1)S(1)}, bf16[4,128,128]{2,1,0:T(8,128)(2,1)S(1)}, u32[]{:S(2)}, u32[]{:S(2)}) collective-permute-start(bf16[4,128,128]{2,1,0:T(8,128)(2,1)S(1)} %get-tuple-element.133), channel_id=1, source_target_pairs={{0,4},{1,5},{2,6},{3,7},{4,0},{5,1},{6,2},{7,3},{8,12},{9,13},{10,... | collective-permute-start | bytes 393224 | tf_op jit(solution)/shard_map/latent_grad0_far/ppermute | solution.py:54
  29.9 0.6 latent0_near.1
  30.5 1.6 %collective-permute-start.7 = (bf16[2,256,128]{2,1,0:T(8,128)(2,1)S(1)}, bf16[2,256,128]{2,1,0:T(8,128)(2,1)S(1)}, u32[]{:S(2)}, u32[]{:S(2)}) collective-permute-start(bf16[2,256,128]{2,1,0:T(8,128)(2,1)S(1)} %get-tuple-element.137), channel_id=1, source_target_pairs={{0,2},{1,3},{2,0},{3,1},{4,6},{5,7},{6,4},{7,5},{8,10},{9,11},{10,... | collective-permute-start | bytes 393224 | tf_op jit(solution)/shard_map/latent0_near/ppermute | solution.py:54
  32.7 2.2 %collective-permute-done.8.sent = bf16[2,512,128]{2,1,0:T(8,128)(2,1)S(1)} collective-permute-done((bf16[2,512,128]{2,1,0:T(8,128)(2,1)S(1)}, bf16[2,512,128]{2,1,0:T(8,128)(2,1)S(1)}, u32[]{:S(2)}, u32[]{:S(2)}) %collective-permute-start.8) | collective-permute-done | bytes 262176 | tf_op jit(solution)/shard_map/latent_S/ppermute | solution.py:54
  34.9 0.6 latent1_near.1
  35.6 1.6 %collective-permute-start.11 = (bf16[2,512,128]{2,1,0:T(8,128)(2,1)S(1)}, bf16[2,512,128]{2,1,0:T(8,128)(2,1)S(1)}, u32[]{:S(2)}, u32[]{:S(2)}) collective-permute-start(bf16[2,512,128]{2,1,0:T(8,128)(2,1)S(1)} %get-tuple-element.145), channel_id=1, source_target_pairs={{0,2},{1,3},{2,0},{3,1},{4,6},{5,7},{6,4},{7,5},{8,10},{9,11},{10,... | collective-permute-start | bytes 786440 | tf_op jit(solution)/shard_map/latent1_near/ppermute | solution.py:54
  37.2 2.6 %collective-permute-start.12 = (bf16[4,128,128]{2,1,0:T(8,128)(2,1)S(1)}, bf16[4,128,128]{2,1,0:T(8,128)(2,1)S(1)}, u32[]{:S(2)}, u32[]{:S(2)}) collective-permute-start(bf16[4,128,128]{2,1,0:T(8,128)(2,1)S(1)} %get-tuple-element.141), channel_id=1, source_target_pairs={{0,4},{1,5},{2,6},{3,7},{4,0},{5,1},{6,2},{7,3},{8,12},{9,13},{10,... | collective-permute-start | bytes 393224 | tf_op jit(solution)/shard_map/latent_grad1_far/ppermute | solution.py:54
  39.8 0.6 latent0_far.1
  41.8 4.9 %collective-permute-done.12.other = bf16[4,128,128]{2,1,0:T(8,128)(2,1)S(1)} collective-permute-done((bf16[4,128,128]{2,1,0:T(8,128)(2,1)S(1)}, bf16[4,128,128]{2,1,0:T(8,128)(2,1)S(1)}, u32[]{:S(2)}, u32[]{:S(2)}) %collective-permute-start.12) | collective-permute-done | bytes 131104 | tf_op jit(solution)/shard_map/latent_grad1_far/ppermute | solution.py:54
  47.3 3.6 %collective-permute-start.14 = (bf16[4,128,128]{2,1,0:T(8,128)(2,1)S(1)}, bf16[4,128,128]{2,1,0:T(8,128)(2,1)S(1)}, u32[]{:S(2)}, u32[]{:S(2)}) collective-permute-start(bf16[4,128,128]{2,1,0:T(8,128)(2,1)S(1)} %latent_grad1_last.1.mine), channel_id=1, source_target_pairs={{0,2},{1,3},{2,0},{3,1},{4,6},{5,7},{6,4},{7,5},{8,10},{9,11},{10,... | collective-permute-start | bytes 393224 | tf_op jit(solution)/shard_map/latent_grad1_last/ppermute | solution.py:54
  50.9 0.6 latent1_far.1
  51.5 1.2 %collective-permute-start.17 = (bf16[2,512,128]{2,1,0:T(8,128)(2,1)S(1)}, bf16[2,512,128]{2,1,0:T(8,128)(2,1)S(1)}, u32[]{:S(2)}, u32[]{:S(2)}) collective-permute-start(bf16[2,512,128]{2,1,0:T(8,128)(2,1)S(1)} %get-tuple-element.157), channel_id=1, source_target_pairs={{0,4},{1,5},{2,6},{3,7},{4,0},{5,1},{6,2},{7,3},{8,12},{9,13},{10,... | collective-permute-start | bytes 786440 | tf_op jit(solution)/shard_map/latent1_far/ppermute | solution.py:54
  52.7 1.6 %collective-permute-done.10.other = bf16[4,128,128]{2,1,0:T(8,128)(2,1)S(1)} collective-permute-done((bf16[4,128,128]{2,1,0:T(8,128)(2,1)S(1)}, bf16[4,128,128]{2,1,0:T(8,128)(2,1)S(1)}, u32[]{:S(2)}, u32[]{:S(2)}) %collective-permute-start.10) | collective-permute-done | bytes 131104 | tf_op jit(solution)/shard_map/latent_grad0_last/ppermute | solution.py:54
  54.9 1.5 %collective-permute-start.13 = (bf16[4,256,128]{2,1,0:T(8,128)(2,1)S(1)}, bf16[4,256,128]{2,1,0:T(8,128)(2,1)S(1)}, u32[]{:S(2)}, u32[]{:S(2)}) collective-permute-start(bf16[4,256,128]{2,1,0:T(8,128)(2,1)S(1)} %latent_grad0_join.1.near.refs_0_), channel_id=1, source_target_pairs={{0,1},{1,0},{2,3},{3,2},{4,5},{5,4},{6,7},{7,6},{8,9},{9,8},{10,11... | collective-permute-start | bytes 786440 | tf_op jit(solution)/shard_map/latent_grad0_join/ppermute | solution.py:54
  57.0 0.6 collective-permute-start.18
  58.2 3.1 %collective-permute-done.18.refs_1_ = bf16[256,128]{1,0:T(8,128)(2,1)S(1)} collective-permute-done((bf16[256,128]{1,0:T(8,128)(2,1)S(1)}, bf16[256,128]{1,0:T(8,128)(2,1)S(1)}, u32[]{:S(2)}, u32[]{:S(2)}) %collective-permute-start.18) | collective-permute-done | bytes 65568 | tf_op jit(solution)/shard_map/latent0_last/ppermute | solution.py:54
  61.9 1.0 %collective-permute-start.20 = (bf16[2,256,128]{2,1,0:T(8,128)(2,1)S(1)}, bf16[2,256,128]{2,1,0:T(8,128)(2,1)S(1)}, u32[]{:S(2)}, u32[]{:S(2)}) collective-permute-start(bf16[2,256,128]{2,1,0:T(8,128)(2,1)S(1)} %latent0_stack.1.mine), channel_id=1, source_target_pairs={{0,2},{1,3},{2,0},{3,1},{4,6},{5,7},{6,4},{7,5},{8,10},{9,11},{10,... | collective-permute-start | bytes 393224 | tf_op jit(solution)/shard_map/latent0_stack/ppermute | solution.py:54
  62.9 2.1 %collective-permute-done.17.other = bf16[2,512,128]{2,1,0:T(8,128)(2,1)S(1)} collective-permute-done((bf16[2,512,128]{2,1,0:T(8,128)(2,1)S(1)}, bf16[2,512,128]{2,1,0:T(8,128)(2,1)S(1)}, u32[]{:S(2)}, u32[]{:S(2)}) %collective-permute-start.17) | collective-permute-done | bytes 262176 | tf_op jit(solution)/shard_map/latent1_far/ppermute | solution.py:54
  65.0 0.6 latent1_last.1
  66.2 0.7 collective-permute-done.20.other
  67.6 1.1 %collective-permute-start.16 = (bf16[4,256,128]{2,1,0:T(8,128)(2,1)S(1)}, bf16[4,256,128]{2,1,0:T(8,128)(2,1)S(1)}, u32[]{:S(2)}, u32[]{:S(2)}) collective-permute-start(bf16[4,256,128]{2,1,0:T(8,128)(2,1)S(1)} %latent_grad1_join.1.near.refs_2_), channel_id=1, source_target_pairs={{0,1},{1,0},{2,3},{3,2},{4,5},{5,4},{6,7},{7,6},{8,9},{9,8},{10,11... | collective-permute-start | bytes 786440 | tf_op jit(solution)/shard_map/latent_grad1_join/ppermute | solution.py:54
  69.2 5.1 %collective-permute-done.19.refs_1_ = bf16[512,128]{1,0:T(8,128)(2,1)S(1)} collective-permute-done((bf16[512,128]{1,0:T(8,128)(2,1)S(1)}, bf16[512,128]{1,0:T(8,128)(2,1)S(1)}, u32[]{:S(2)}, u32[]{:S(2)}) %collective-permute-start.19) | collective-permute-done | bytes 131104 | tf_op jit(solution)/shard_map/latent1_last/ppermute | solution.py:54
  74.8 1.5 %collective-permute-done.16.far.refs_3_ = bf16[4,256,128]{2,1,0:T(8,128)(2,1)S(1)} collective-permute-done((bf16[4,256,128]{2,1,0:T(8,128)(2,1)S(1)}, bf16[4,256,128]{2,1,0:T(8,128)(2,1)S(1)}, u32[]{:S(2)}, u32[]{:S(2)}) %collective-permute-start.16) | collective-permute-done | bytes 262176 | tf_op jit(solution)/shard_map/latent_grad1_join/ppermute | solution.py:54
  77.0 1.1 %collective-permute-start.25 = (bf16[2,512,128]{2,1,0:T(8,128)(2,1)S(1)}, bf16[2,512,128]{2,1,0:T(8,128)(2,1)S(1)}, u32[]{:S(2)}, u32[]{:S(2)}) collective-permute-start(bf16[2,512,128]{2,1,0:T(8,128)(2,1)S(1)} %latent0_join.1.refs_0_), channel_id=1, source_target_pairs={{0,1},{1,0},{2,3},{3,2},{4,5},{5,4},{6,7},{7,6},{8,9},{9,8},{10,11... | collective-permute-start | bytes 786440 | tf_op jit(solution)/shard_map/latent0_join/ppermute | solution.py:54
  78.0 1.0 %collective-permute-start.26 = (bf16[2,512,128]{2,1,0:T(8,128)(2,1)S(1)}, bf16[2,512,128]{2,1,0:T(8,128)(2,1)S(1)}, u32[]{:S(2)}, u32[]{:S(2)}) collective-permute-start(bf16[2,512,128]{2,1,0:T(8,128)(2,1)S(1)} %latent1_stack.1.refs_1_), channel_id=1, source_target_pairs={{0,1},{1,0},{2,3},{3,2},{4,5},{5,4},{6,7},{7,6},{8,9},{9,8},{10,11... | collective-permute-start | bytes 786440 | tf_op jit(solution)/shard_map/latent1_stack/ppermute | solution.py:54
  79.0 1.4 %latent_grad0_left.1 = (f32[128,1024]{1,0:T(8,128)S(1)}, bf16[128,1024]{1,0:T(8,128)(2,1)S(1)}) custom-call(s32[5]{0:T(128)S(1)} %stack.23.where, bf16[4,256,128]{2,1,0:T(8,128)(2,1)S(1)} %latent_grad0_join.1.near.refs_0_, bf16[4,256,128]{2,1,0:T(8,128)(2,1)S(1)} %collective-permute-done.13.far.refs_1_, ...), custom_call_target="tpu_custom_call" | custom-call | flops 536870912 | bytes 3670016 | tf_op jit(solution)/shard_map/latent_grad0_left/pallas_call | solution.py:40
  80.5 0.6 collective-permute-start.23
  81.1 1.4 %latent_grad1_left.1 = (f32[128,1024]{1,0:T(8,128)S(1)}, bf16[128,1024]{1,0:T(8,128)(2,1)S(1)}) custom-call(s32[5]{0:T(128)S(1)} %stack.23.where, bf16[4,256,128]{2,1,0:T(8,128)(2,1)S(1)} %latent_grad1_join.1.near.refs_2_, bf16[4,256,128]{2,1,0:T(8,128)(2,1)S(1)} %collective-permute-done.16.far.refs_3_, ...), custom_call_target="tpu_custom_call" | custom-call | flops 536870912 | bytes 3670016 | tf_op jit(solution)/shard_map/latent_grad1_left/pallas_call | solution.py:40
  82.5 1.5 %collective-permute-start.24 = (bf16[128,1024]{1,0:T(8,128)(2,1)S(1)}, bf16[128,1024]{1,0:T(8,128)(2,1)S(1)}, u32[]{:S(2)}, u32[]{:S(2)}) collective-permute-start(bf16[128,1024]{1,0:T(8,128)(2,1)S(1)} %get-tuple-element.193), channel_id=1, source_target_pairs={{0,16},{8,24},{16,0},{24,8},{1,17},{9,25},{17,1},{25,9},{2,18},{10... | collective-permute-start | bytes 786440 | tf_op jit(solution)/shard_map/latent_grad1_left/ppermute | solution.py:54
  84.1 3.1 %latent_grad_input.1 = bf16[512,1024]{1,0:T(8,128)(2,1)} custom-call(s32[5]{0:T(128)S(1)} %stack.23.where, bf16[4,256,128]{2,1,0:T(8,128)(2,1)S(1)} %latent_grad0_join.1.near.refs_0_, bf16[4,256,128]{2,1,0:T(8,128)(2,1)S(1)} %collective-permute-done.13.far.refs_1_, bf16[4,256,128]{2,1,0:T(8,128)(2,1)S(1)} %latent_grad1_join.1.near.refs_2_, ...), custom_call_target="tpu_custom_call" | custom-call | flops 1073741824 | bytes 3145728 | tf_op jit(solution)/shard_map/latent_grad_input/pallas_call | solution.py:265
  87.2 3.8 %latent_rn.1.refs_6_ = f32[256,2048]{1,0:T(8,128)S(1)} custom-call(s32[5]{0:T(128)S(1)} %stack.23.where, bf16[2,512,128]{2,1,0:T(8,128)(2,1)S(1)} %latent0_join.1.refs_0_, bf16[2,512,128]{2,1,0:T(8,128)(2,1)S(1)} %latent1_stack.1.refs_1_, bf16[512,2048]{1,0:T(8,128)(2,1)S(1)} %copy-done.1, bf16[512,2048]{1,0:T(8,128)(2,1)S(1)} %collective-permute-done.1.refs_3_, ...), custom_call_target="tpu_custom_call" | custom-call | flops 1073741824 | bytes 8912896 | tf_op jit(solution)/shard_map/latent_rn/pallas_call | solution.py:309
  91.3 4.7 %latent_rf.1 = f32[256,2048]{1,0:T(8,128)} custom-call(s32[5]{0:T(128)S(1)} %stack.23.where, bf16[2,512,128]{2,1,0:T(8,128)(2,1)S(1)} %collective-permute-done.25.refs_0_, bf16[2,512,128]{2,1,0:T(8,128)(2,1)S(1)} %collective-permute-done.26.refs_1_, bf16[512,2048]{1,0:T(8,128)(2,1)S(1)} %copy-done.1, bf16[512,2048]{1,0:T(8,128)(2,1)S(1)} %collective-permute-done.1.refs_3_, ...), custom_call_target="tpu_custom_call" | custom-call | flops 1073741824 | bytes 8912896 | tf_op jit(solution)/shard_map/latent_rf/pallas_call | solution.py:309
  96.0 1.6 %latent_grad_final.1 = f32[256,1024]{1,0:T(8,128)} custom-call(s32[5]{0:T(128)S(1)} %stack.23.where, f32[128,1024]{1,0:T(8,128)S(1)} %get-tuple-element.213.refs_0_, bf16[128,1024]{1,0:T(8,128)(2,1)S(1)} %collective-permute-done.23.refs_1_, f32[128,1024]{1,0:T(8,128)S(1)} %get-tuple-element.215.refs_2_, bf16[128,1024]{1,0:T(8,128)(2,1)S(1)} %collective-permute-done.24.refs_3_), custom_call_target="tpu_custom_call" | custom-call | bytes 2621440 | tf_op jit(solution)/shard_map/latent_grad_final/pallas_call | solution.py:40
  (53 shorter events, 10.7 us)
Async XLA Ops:
  0.6 15.6 %collective-permute-start.1 = (bf16[512,2048]{1,0:T(8,128)(2,1)}, bf16[512,2048]{1,0:T(8,128)(2,1)S(1)}, u32[]{:S(2)}, u32[]{:S(2)}) collective-permute-start(bf16[512,2048]{1,0:T(8,128)(2,1)} %refs_2_.1), channel_id=1, source_target_pairs={{0,8},{8,0},{16,24},{24,16},{1,9},{9,1},{17,25},{25,17},{2,10},{10... | collective-permute-start | bytes 6291464 | tf_op jit(solution)/shard_map/core_own/ppermute | solution.py:54
  1.1 66.3 %collective-permute-start.27 = (bf16[512,2048]{1,0:T(8,128)(2,1)}, bf16[512,2048]{1,0:T(8,128)(2,1)}, u32[]{:S(2)}, u32[]{:S(2)}) collective-permute-start(bf16[512,2048]{1,0:T(8,128)(2,1)} %refs_2_.1), channel_id=1, source_target_pairs={{0,16},{8,24},{16,0},{24,8},{1,17},{9,25},{17,1},{25,9},{2,18},{10... | collective-permute-start | bytes 6291464 | tf_op jit(solution)/shard_map/far_og/ppermute | solution.py:54
  3.7 9.6 %collective-permute-start = (bf16[512,1024]{1,0:T(8,128)(2,1)}, bf16[512,1024]{1,0:T(8,128)(2,1)S(1)}, u32[]{:S(2)}, u32[]{:S(2)}) collective-permute-start(bf16[512,1024]{1,0:T(8,128)(2,1)} %acts.1), channel_id=1, source_target_pairs={{0,8},{8,0},{16,24},{24,16},{1,9},{9,1},{17,25},{25,17},{2,10},{10... | collective-permute-start | bytes 3145736 | tf_op jit(solution)/shard_map/core_acts/ppermute | solution.py:54
  4.0 1.6 %copy-start = (bf16[512,2048]{1,0:T(8,128)(2,1)S(1)}, bf16[512,2048]{1,0:T(8,128)(2,1)}, u32[]{:S(2)}) copy-start(bf16[512,2048]{1,0:T(8,128)(2,1)} %refs_2_.1) | copy-start | bytes 6291460
  5.6 2.2 %copy-start.2 = (bf16[1024,2048]{1,0:T(8,128)(2,1)S(1)}, bf16[1024,2048]{1,0:T(8,128)(2,1)}, u32[]{:S(2)}) copy-start(bf16[1024,2048]{1,0:T(8,128)(2,1)} %param.6) | copy-start | bytes 12582916
  9.4 3.9 %copy-start.4 = (bf16[1024,1024]{1,0:T(8,128)(2,1)S(1)}, bf16[1024,1024]{1,0:T(8,128)(2,1)}, u32[]{:S(2)}) copy-start(bf16[1024,1024]{1,0:T(8,128)(2,1)} %refs_4_) | copy-start | bytes 6291460
  9.4 3.9 %copy-start.5 = (bf16[512,1024]{1,0:T(8,128)(2,1)S(1)}, bf16[512,1024]{1,0:T(8,128)(2,1)}, u32[]{:S(2)}) copy-start(bf16[512,1024]{1,0:T(8,128)(2,1)} %acts.1) | copy-start | bytes 3145732
  9.5 9.3 %collective-permute-start.2 = (bf16[4,256,128]{2,1,0:T(8,128)(2,1)S(1)}, bf16[4,256,128]{2,1,0:T(8,128)(2,1)S(1)}, u32[]{:S(2)}, u32[]{:S(2)}) collective-permute-start(bf16[4,256,128]{2,1,0:T(8,128)(2,1)S(1)} %latent_grad0_S.1), channel_id=1, source_target_pairs={{0,1},{1,0},{2,3},{3,2},{4,5},{5,4},{6,7},{7,6},{8,9},{9,8},{10,11... | collective-permute-start | bytes 786440 | tf_op jit(solution)/shard_map/latent_grad0_S/ppermute | solution.py:54
  11.0 5.7 %copy-start.3 = (bf16[1024,2048]{1,0:T(8,128)(2,1)S(1)}, bf16[1024,2048]{1,0:T(8,128)(2,1)}, u32[]{:S(2)}) copy-start(bf16[1024,2048]{1,0:T(8,128)(2,1)} %param.6) | copy-start | bytes 12582916
  12.7 11.5 %collective-permute-start.4 = (bf16[4,256,128]{2,1,0:T(8,128)(2,1)S(1)}, bf16[4,256,128]{2,1,0:T(8,128)(2,1)S(1)}, u32[]{:S(2)}, u32[]{:S(2)}) collective-permute-start(bf16[4,256,128]{2,1,0:T(8,128)(2,1)S(1)} %latent_grad1_S.1), channel_id=1, source_target_pairs={{0,1},{1,0},{2,3},{3,2},{4,5},{5,4},{6,7},{7,6},{8,9},{9,8},{10,11... | collective-permute-start | bytes 786440 | tf_op jit(solution)/shard_map/latent_grad1_S/ppermute | solution.py:54
  13.3 3.4 %copy-start.1 = (bf16[512,2048]{1,0:T(8,128)(2,1)S(1)}, bf16[512,2048]{1,0:T(8,128)(2,1)}, u32[]{:S(2)}) copy-start(bf16[512,2048]{1,0:T(8,128)(2,1)} %refs_2_.1) | copy-start | bytes 6291460
  14.6 15.2 %collective-permute-start.6 = (bf16[2,512,128]{2,1,0:T(8,128)(2,1)S(1)}, bf16[2,512,128]{2,1,0:T(8,128)(2,1)S(1)}, u32[]{:S(2)}, u32[]{:S(2)}) collective-permute-start(bf16[2,512,128]{2,1,0:T(8,128)(2,1)S(1)} %get-tuple-element.113), channel_id=1, source_target_pairs={{0,1},{1,0},{2,3},{3,2},{4,5},{5,4},{6,7},{7,6},{8,9},{9,8},{10,11... | collective-permute-start | bytes 786440 | tf_op jit(solution)/shard_map/latent_S/ppermute | solution.py:54
  16.2 18.7 %collective-permute-start.8 = (bf16[2,512,128]{2,1,0:T(8,128)(2,1)S(1)}, bf16[2,512,128]{2,1,0:T(8,128)(2,1)S(1)}, u32[]{:S(2)}, u32[]{:S(2)}) collective-permute-start(bf16[2,512,128]{2,1,0:T(8,128)(2,1)S(1)} %get-tuple-element.114), channel_id=1, source_target_pairs={{0,1},{1,0},{2,3},{3,2},{4,5},{5,4},{6,7},{7,6},{8,9},{9,8},{10,11... | collective-permute-start | bytes 786440 | tf_op jit(solution)/shard_map/latent_S/ppermute | solution.py:54
  19.4 7.1 %collective-permute-start.3 = (bf16[4,128,128]{2,1,0:T(8,128)(2,1)S(1)}, bf16[4,128,128]{2,1,0:T(8,128)(2,1)S(1)}, u32[]{:S(2)}, u32[]{:S(2)}) collective-permute-start(bf16[4,128,128]{2,1,0:T(8,128)(2,1)S(1)} %get-tuple-element.121), channel_id=1, source_target_pairs={{0,2},{1,3},{2,0},{3,1},{4,6},{5,7},{6,4},{7,5},{8,10},{9,11},{10,... | collective-permute-start | bytes 393224 | tf_op jit(solution)/shard_map/latent_grad0_near/ppermute | solution.py:54
  24.9 7.3 %collective-permute-start.9 = (bf16[4,128,128]{2,1,0:T(8,128)(2,1)S(1)}, bf16[4,128,128]{2,1,0:T(8,128)(2,1)S(1)}, u32[]{:S(2)}, u32[]{:S(2)}) collective-permute-start(bf16[4,128,128]{2,1,0:T(8,128)(2,1)S(1)} %get-tuple-element.129), channel_id=1, source_target_pairs={{0,2},{1,3},{2,0},{3,1},{4,6},{5,7},{6,4},{7,5},{8,10},{9,11},{10,... | collective-permute-start | bytes 393224 | tf_op jit(solution)/shard_map/latent_grad1_near/ppermute | solution.py:54
  27.1 13.3 %collective-permute-start.5 = (bf16[4,128,128]{2,1,0:T(8,128)(2,1)S(1)}, bf16[4,128,128]{2,1,0:T(8,128)(2,1)S(1)}, u32[]{:S(2)}, u32[]{:S(2)}) collective-permute-start(bf16[4,128,128]{2,1,0:T(8,128)(2,1)S(1)} %get-tuple-element.133), channel_id=1, source_target_pairs={{0,4},{1,5},{2,6},{3,7},{4,0},{5,1},{6,2},{7,3},{8,12},{9,13},{10,... | collective-permute-start | bytes 393224 | tf_op jit(solution)/shard_map/latent_grad0_far/ppermute | solution.py:54
  30.5 9.3 %collective-permute-start.7 = (bf16[2,256,128]{2,1,0:T(8,128)(2,1)S(1)}, bf16[2,256,128]{2,1,0:T(8,128)(2,1)S(1)}, u32[]{:S(2)}, u32[]{:S(2)}) collective-permute-start(bf16[2,256,128]{2,1,0:T(8,128)(2,1)S(1)} %get-tuple-element.137), channel_id=1, source_target_pairs={{0,2},{1,3},{2,0},{3,1},{4,6},{5,7},{6,4},{7,5},{8,10},{9,11},{10,... | collective-permute-start | bytes 393224 | tf_op jit(solution)/shard_map/latent0_near/ppermute | solution.py:54
  35.6 15.3 %collective-permute-start.11 = (bf16[2,512,128]{2,1,0:T(8,128)(2,1)S(1)}, bf16[2,512,128]{2,1,0:T(8,128)(2,1)S(1)}, u32[]{:S(2)}, u32[]{:S(2)}) collective-permute-start(bf16[2,512,128]{2,1,0:T(8,128)(2,1)S(1)} %get-tuple-element.145), channel_id=1, source_target_pairs={{0,2},{1,3},{2,0},{3,1},{4,6},{5,7},{6,4},{7,5},{8,10},{9,11},{10,... | collective-permute-start | bytes 786440 | tf_op jit(solution)/shard_map/latent1_near/ppermute | solution.py:54
  37.2 9.5 %collective-permute-start.12 = (bf16[4,128,128]{2,1,0:T(8,128)(2,1)S(1)}, bf16[4,128,128]{2,1,0:T(8,128)(2,1)S(1)}, u32[]{:S(2)}, u32[]{:S(2)}) collective-permute-start(bf16[4,128,128]{2,1,0:T(8,128)(2,1)S(1)} %get-tuple-element.141), channel_id=1, source_target_pairs={{0,4},{1,5},{2,6},{3,7},{4,0},{5,1},{6,2},{7,3},{8,12},{9,13},{10,... | collective-permute-start | bytes 393224 | tf_op jit(solution)/shard_map/latent_grad1_far/ppermute | solution.py:54
  41.0 13.4 %collective-permute-start.10 = (bf16[4,128,128]{2,1,0:T(8,128)(2,1)S(1)}, bf16[4,128,128]{2,1,0:T(8,128)(2,1)S(1)}, u32[]{:S(2)}, u32[]{:S(2)}) collective-permute-start(bf16[4,128,128]{2,1,0:T(8,128)(2,1)S(1)} %latent_grad0_last.1.mine), channel_id=1, source_target_pairs={{0,2},{1,3},{2,0},{3,1},{4,6},{5,7},{6,4},{7,5},{8,10},{9,11},{10,... | collective-permute-start | bytes 393224 | tf_op jit(solution)/shard_map/latent_grad0_last/ppermute | solution.py:54
  41.5 14.9 %collective-permute-start.15 = (bf16[2,256,128]{2,1,0:T(8,128)(2,1)S(1)}, bf16[2,256,128]{2,1,0:T(8,128)(2,1)S(1)}, u32[]{:S(2)}, u32[]{:S(2)}) collective-permute-start(bf16[2,256,128]{2,1,0:T(8,128)(2,1)S(1)} %get-tuple-element.149), channel_id=1, source_target_pairs={{0,4},{1,5},{2,6},{3,7},{4,0},{5,1},{6,2},{7,3},{8,12},{9,13},{10,... | collective-permute-start | bytes 393224 | tf_op jit(solution)/shard_map/latent0_far/ppermute | solution.py:54
  47.3 10.3 %collective-permute-start.14 = (bf16[4,128,128]{2,1,0:T(8,128)(2,1)S(1)}, bf16[4,128,128]{2,1,0:T(8,128)(2,1)S(1)}, u32[]{:S(2)}, u32[]{:S(2)}) collective-permute-start(bf16[4,128,128]{2,1,0:T(8,128)(2,1)S(1)} %latent_grad1_last.1.mine), channel_id=1, source_target_pairs={{0,2},{1,3},{2,0},{3,1},{4,6},{5,7},{6,4},{7,5},{8,10},{9,11},{10,... | collective-permute-start | bytes 393224 | tf_op jit(solution)/shard_map/latent_grad1_last/ppermute | solution.py:54
  51.5 13.5 %collective-permute-start.17 = (bf16[2,512,128]{2,1,0:T(8,128)(2,1)S(1)}, bf16[2,512,128]{2,1,0:T(8,128)(2,1)S(1)}, u32[]{:S(2)}, u32[]{:S(2)}) collective-permute-start(bf16[2,512,128]{2,1,0:T(8,128)(2,1)S(1)} %get-tuple-element.157), channel_id=1, source_target_pairs={{0,4},{1,5},{2,6},{3,7},{4,0},{5,1},{6,2},{7,3},{8,12},{9,13},{10,... | collective-permute-start | bytes 786440 | tf_op jit(solution)/shard_map/latent1_far/ppermute | solution.py:54
  54.9 10.7 %collective-permute-start.13 = (bf16[4,256,128]{2,1,0:T(8,128)(2,1)S(1)}, bf16[4,256,128]{2,1,0:T(8,128)(2,1)S(1)}, u32[]{:S(2)}, u32[]{:S(2)}) collective-permute-start(bf16[4,256,128]{2,1,0:T(8,128)(2,1)S(1)} %latent_grad0_join.1.near.refs_0_), channel_id=1, source_target_pairs={{0,1},{1,0},{2,3},{3,2},{4,5},{5,4},{6,7},{7,6},{8,9},{9,8},{10,11... | collective-permute-start | bytes 786440 | tf_op jit(solution)/shard_map/latent_grad0_join/ppermute | solution.py:54
  57.0 4.3 %collective-permute-start.18 = (bf16[256,128]{1,0:T(8,128)(2,1)S(1)}, bf16[256,128]{1,0:T(8,128)(2,1)S(1)}, u32[]{:S(2)}, u32[]{:S(2)}) collective-permute-start(bf16[256,128]{1,0:T(8,128)(2,1)S(1)} %get-tuple-element.163), channel_id=1, source_target_pairs={{0,16},{8,24},{16,0},{24,8},{1,17},{9,25},{17,1},{25,9},{2,18},{10... | collective-permute-start | bytes 196616 | tf_op jit(solution)/shard_map/latent0_last/ppermute | solution.py:54
  61.9 5.0 %collective-permute-start.20 = (bf16[2,256,128]{2,1,0:T(8,128)(2,1)S(1)}, bf16[2,256,128]{2,1,0:T(8,128)(2,1)S(1)}, u32[]{:S(2)}, u32[]{:S(2)}) collective-permute-start(bf16[2,256,128]{2,1,0:T(8,128)(2,1)S(1)} %latent0_stack.1.mine), channel_id=1, source_target_pairs={{0,2},{1,3},{2,0},{3,1},{4,6},{5,7},{6,4},{7,5},{8,10},{9,11},{10,... | collective-permute-start | bytes 393224 | tf_op jit(solution)/shard_map/latent0_stack/ppermute | solution.py:54
  67.5 19.7 %collective-permute-start.28 = (bf16[512,2048]{1,0:T(8,128)(2,1)}, bf16[512,2048]{1,0:T(8,128)(2,1)S(1)}, u32[]{:S(2)}, u32[]{:S(2)}) collective-permute-start(bf16[512,2048]{1,0:T(8,128)(2,1)} %collective-permute-done.27.refs_4_), channel_id=1, source_target_pairs={{0,8},{8,0},{16,24},{24,16},{1,9},{9,1},{17,25},{25,17},{2,10},{10... | collective-permute-start | bytes 6291464 | tf_op jit(solution)/shard_map/core_far/ppermute | solution.py:54
  67.6 8.7 %collective-permute-start.16 = (bf16[4,256,128]{2,1,0:T(8,128)(2,1)S(1)}, bf16[4,256,128]{2,1,0:T(8,128)(2,1)S(1)}, u32[]{:S(2)}, u32[]{:S(2)}) collective-permute-start(bf16[4,256,128]{2,1,0:T(8,128)(2,1)S(1)} %latent_grad1_join.1.near.refs_2_), channel_id=1, source_target_pairs={{0,1},{1,0},{2,3},{3,2},{4,5},{5,4},{6,7},{7,6},{8,9},{9,8},{10,11... | collective-permute-start | bytes 786440 | tf_op jit(solution)/shard_map/latent_grad1_join/ppermute | solution.py:54
  68.7 5.6 %collective-permute-start.19 = (bf16[512,128]{1,0:T(8,128)(2,1)S(1)}, bf16[512,128]{1,0:T(8,128)(2,1)S(1)}, u32[]{:S(2)}, u32[]{:S(2)}) collective-permute-start(bf16[512,128]{1,0:T(8,128)(2,1)S(1)} %get-tuple-element.171), channel_id=1, source_target_pairs={{0,16},{8,24},{16,0},{24,8},{1,17},{9,25},{17,1},{25,9},{2,18},{10... | collective-permute-start | bytes 393224 | tf_op jit(solution)/shard_map/latent1_last/ppermute | solution.py:54
  69.2 9.9 %collective-permute-start.22 = (bf16[2,2,256,128]{3,2,1,0:T(8,128)(2,1)S(1)}, bf16[2,2,256,128]{3,2,1,0:T(8,128)(2,1)S(1)}, u32[]{:S(2)}, u32[]{:S(2)}) collective-permute-start(bf16[2,2,256,128]{3,2,1,0:T(8,128)(2,1)S(1)} %latent_grad0_halves.1), channel_id=1, source_target_pairs={{0,8},{8,0},{16,24},{24,16},{1,9},{9,1},{17,25},{25,17},{2,10},{10... | collective-permute-start | bytes 786440 | tf_op jit(solution)/shard_map/latent_grad0_halves/ppermute | solution.py:54
  76.9 4.2 %collective-permute-start.21 = (bf16[2,2,256,128]{3,2,1,0:T(8,128)(2,1)S(1)}, bf16[2,2,256,128]{3,2,1,0:T(8,128)(2,1)S(1)}, u32[]{:S(2)}, u32[]{:S(2)}) collective-permute-start(bf16[2,2,256,128]{3,2,1,0:T(8,128)(2,1)S(1)} %latent_grad1_halves.1), channel_id=1, source_target_pairs={{0,8},{8,0},{16,24},{24,16},{1,9},{9,1},{17,25},{25,17},{2,10},{10... | collective-permute-start | bytes 786440 | tf_op jit(solution)/shard_map/latent_grad1_halves/ppermute | solution.py:54
  77.0 14.0 %collective-permute-start.25 = (bf16[2,512,128]{2,1,0:T(8,128)(2,1)S(1)}, bf16[2,512,128]{2,1,0:T(8,128)(2,1)S(1)}, u32[]{:S(2)}, u32[]{:S(2)}) collective-permute-start(bf16[2,512,128]{2,1,0:T(8,128)(2,1)S(1)} %latent0_join.1.refs_0_), channel_id=1, source_target_pairs={{0,1},{1,0},{2,3},{3,2},{4,5},{5,4},{6,7},{7,6},{8,9},{9,8},{10,11... | collective-permute-start | bytes 786440 | tf_op jit(solution)/shard_map/latent0_join/ppermute | solution.py:54
  78.0 13.2 %collective-permute-start.26 = (bf16[2,512,128]{2,1,0:T(8,128)(2,1)S(1)}, bf16[2,512,128]{2,1,0:T(8,128)(2,1)S(1)}, u32[]{:S(2)}, u32[]{:S(2)}) collective-permute-start(bf16[2,512,128]{2,1,0:T(8,128)(2,1)S(1)} %latent1_stack.1.refs_1_), channel_id=1, source_target_pairs={{0,1},{1,0},{2,3},{3,2},{4,5},{5,4},{6,7},{7,6},{8,9},{9,8},{10,11... | collective-permute-start | bytes 786440 | tf_op jit(solution)/shard_map/latent1_stack/ppermute | solution.py:54
  80.5 15.5 %collective-permute-start.23 = (bf16[128,1024]{1,0:T(8,128)(2,1)S(1)}, bf16[128,1024]{1,0:T(8,128)(2,1)S(1)}, u32[]{:S(2)}, u32[]{:S(2)}) collective-permute-start(bf16[128,1024]{1,0:T(8,128)(2,1)S(1)} %get-tuple-element.186), channel_id=1, source_target_pairs={{0,16},{8,24},{16,0},{24,8},{1,17},{9,25},{17,1},{25,9},{2,18},{10... | collective-permute-start | bytes 786440 | tf_op jit(solution)/shard_map/latent_grad0_left/ppermute | solution.py:54
  82.5 13.5 %collective-permute-start.24 = (bf16[128,1024]{1,0:T(8,128)(2,1)S(1)}, bf16[128,1024]{1,0:T(8,128)(2,1)S(1)}, u32[]{:S(2)}, u32[]{:S(2)}) collective-permute-start(bf16[128,1024]{1,0:T(8,128)(2,1)S(1)} %get-tuple-element.193), channel_id=1, source_target_pairs={{0,16},{8,24},{16,0},{24,8},{1,17},{9,25},{17,1},{25,9},{2,18},{10... | collective-permute-start | bytes 786440 | tf_op jit(solution)/shard_map/latent_grad1_left/ppermute | solution.py:54

commit v3 on v2

--- a/solution.py
+++ b/solution.py
@@ -10,13 +10,14 @@
 
 CHUNKS = 2
 NAMES = {"G": "latent_grad", "L": "latent", "x": "far", "c": "core"}
+PIECES = 4
 ORDER = (
-    "G0S", "G1S", "LS", "own", "GK", "G0near", "LK", "G1near", "G0far", "L0near", "G1far",
-    "L1near", "L0far", "G0last", "G1last", "L1far", "G0join", "L0last", "G1join", "L0stack",
-    "L1last", "G0halves", "L0join", "og", "L1stack", "G1halves", "G0left", "L1join", "G1left",
-    "input", "Lrn", "Lrf", "final",
+    "own", "acts", "far", "G1S", "G0S", "GK", "LS", "@own", "LK", "G0near", "G1near", "G0far",
+    "L0near", "G1far", "L1near", "L0far", "G0last", "@G1", "G1last", "L1far", "G0join",
+    "L0last", "G1join", "L0stack", "L1last", "G0halves", "L0join", "og", "L1stack", "G1halves",
+    "G0left", "L1join", "G1left", "input", "Lrn", "Lrf", "final",
 )
-HALVES = {"G": (True, True), "L": (True, False)}
+HALVES = {"G": (True, True), "L": (True, True)}
 BF16 = jnp.bfloat16
 F32 = jnp.float32
 MIB = 1 << 20
@@ -237,97 +238,165 @@
     return mine, blocks
 
 
-def input_kernel(count, where, *refs):
-    parts, (factor, out, ordered) = refs[: 2 * count], refs[2 * count :]
+def written_call(kernel, where, values, out, blocks, scratch, flops, limit):
+    shape, dtype = out
+    return pl.pallas_call(
+        kernel,
+        out_shape=jax.ShapeDtypeStruct(shape, dtype),
+        in_specs=[pl.BlockSpec(memory_space=pltpu.SMEM)]
+        + [pl.BlockSpec(memory_space=pltpu.VMEM)] * len(values),
+        out_specs=pl.BlockSpec(memory_space=pltpu.HBM),
+        scratch_shapes=[
+            pltpu.VMEM(shape, dtype),
+            pltpu.SemaphoreType.DMA((blocks,)),
+            *scratch,
+        ],
+        compiler_params=pltpu.CompilerParams(vmem_limit_bytes=limit * MIB),
+        cost_estimate=cost(flops, *values),
+    )(where, *values)
+
+
+def write(held, out, sems, i, index):
+    copy = pltpu.make_async_copy(held.at[index], out.at[index], sems.at[i])
+    copy.start()
+    return copy
+
+
+def input_kernel(count, blocks, where, *refs):
+    parts, (factor, out, held, sems, ordered) = refs[: 2 * count], refs[2 * count :]
     groups, share, width = parts[0].shape
-    block = out.shape[1]
-
-    @pl.when(pl.program_id(0) == 0)
-    def _():
-        for chunk in range(count):
-            for i in range(2):
-                low = where[0] if i == 0 else 1 - where[0]
-                span = pl.ds(pl.multiple_of(low * share, share), share)
-                for group in range(groups):
-                    lane = (group * count + chunk) * width
-                    ordered[span, lane : lane + width] = parts[2 * chunk + i][group]
-
-    columns = pl.ds(pl.multiple_of(pl.program_id(0) * block, block), block)
-    out[...] = jnp.dot(
-        ordered[...], factor[:, columns], preferred_element_type=F32
-    ).astype(BF16)
+    block = held.shape[1] // blocks
+    for chunk in range(count):
+        for i in range(2):
+            low = where[0] if i == 0 else 1 - where[0]
+            span = pl.ds(pl.multiple_of(low * share, share), share)
+            for group in range(groups):
+                lane = (group * count + chunk) * width
+                ordered[span, lane : lane + width] = parts[2 * chunk + i][group]
+    copies = []
+    for i in range(blocks):
+        columns = slice(i * block, (i + 1) * block)
+        held[:, columns] = jnp.dot(
+            ordered[...], factor[:, columns], preferred_element_type=F32
+        ).astype(BF16)
+        copies.append(write(held, out, sems, i, (slice(None), columns)))
+    for copy in copies:
+        copy.wait()
 
 
 def input_product(where, parts, factor, tokens):
     rank, depth = factor.shape
-    block = min(depth, 512)
-    values = [*parts, factor]
-    return pl.pallas_call(
-        functools.partial(input_kernel, len(parts) // 2),
-        out_shape=jax.ShapeDtypeStruct((tokens, depth), BF16),
-        grid=(depth // block,),
-        in_specs=[pl.BlockSpec(memory_space=pltpu.SMEM)]
-        + [pl.BlockSpec(memory_space=pltpu.VMEM)] * len(values),
-        out_specs=pl.BlockSpec((tokens, block), lambda i: (0, i)),
-        scratch_shapes=[pltpu.VMEM((tokens, rank), BF16)],
-        compiler_params=pltpu.CompilerParams(vmem_limit_bytes=24 * MIB),
-        cost_estimate=cost(2 * tokens * rank * depth, *values),
-    )(where, *values)
-
-
-def right_kernel(owners, near, scale, where, *refs):
-    parts, refs = refs[:CHUNKS], refs[CHUNKS:]
-    grads, refs = refs[: 2 * owners], refs[2 * owners :]
-    done, (out, ordered) = refs[:-2], refs[-2:]
-    share, width = parts[0].shape[1] // 2, parts[0].shape[2]
-    block = out.shape[1]
-    blocks = len(grads) * share
-
-    @pl.when(pl.program_id(0) == 0)
-    def _():
-        for c, part in enumerate(parts):
-            lanes = slice(c * width, (c + 1) * width)
-            ordered[:, lanes] = part[...].reshape(blocks, width)
-
-    low = where[0] if near else 1 - where[0]
+    blocks = max(depth // 256, 1)
+    return written_call(
+        functools.partial(input_kernel, len(parts) // 2, blocks),
+        where,
+        [*parts, factor],
+        ((tokens, depth), BF16),
+        blocks,
+        [pltpu.VMEM((tokens, rank), BF16)],
+        2 * tokens * rank * depth,
+        16,
+    )
+
+
+def right_sum(low, parts, grads, ordered, columns):
+    share = parts[0].shape[1] // 2
     span = pl.ds(pl.multiple_of(low * share, share), share)
-    columns = pl.ds(pl.multiple_of(pl.program_id(0) * block, block), block)
     total = None
-    for i, grad in enumerate(grads):
-        term = dot(ordered[i * share : (i + 1) * share, :], grad[span, columns], ROWS)
+    refs = list(grads)
+    for i in range(ordered.shape[0] // share):
+        pieces = [refs.pop(0) for _ in range(pieces_of(i))]
+        width = pieces[0].shape[1]
+        at, start = divmod(columns.start, width)
+        grad = pieces[at][span, start : start + columns.stop - columns.start]
+        term = dot(ordered[i * share : (i + 1) * share, :], grad, ROWS)
         total = term if total is None else total + term
-    if done:
-        total = (done[0][:, columns] + total) * scale
-    out[...] = total
-
-
-def right_rows(where, near, scale, parts, grads, done):
+    return total
+
+
+def pieces_of(i):
+    return PIECES if i >= 2 and i % 2 else 1
+
+
+def order_parts(parts, ordered):
+    width = parts[0].shape[2]
+    for c, part in enumerate(parts):
+        ordered[:, c * width : (c + 1) * width] = part[...].reshape(ordered.shape[0], width)
+
+
+def right_near_kernel(blocks, where, *refs):
+    parts, grads, (out, ordered) = refs[:CHUNKS], refs[CHUNKS:-2], refs[-2:]
+    block = out.shape[1] // blocks
+    order_parts(parts, ordered)
+    for i in range(blocks):
+        columns = slice(i * block, (i + 1) * block)
+        out[:, columns] = right_sum(where[0], parts, grads, ordered, columns)
+
+
+def right_near(where, parts, grads):
     owners, rows, width = parts[0].shape
     columns = grads[0].shape[1]
-    block = min(columns, 512)
-    values = [*parts, *grads, *done]
-    return pl.pallas_call(
-        functools.partial(right_kernel, owners, near, scale),
-        out_shape=jax.ShapeDtypeStruct((CHUNKS * width, columns), F32),
-        grid=(columns // block,),
-        in_specs=[pl.BlockSpec(memory_space=pltpu.SMEM)]
-        + [pl.BlockSpec(memory_space=pltpu.VMEM)] * len(values),
-        out_specs=pl.BlockSpec((CHUNKS * width, block), lambda i: (0, i)),
-        scratch_shapes=[pltpu.VMEM((owners * rows, CHUNKS * width), BF16)],
-        compiler_params=pltpu.CompilerParams(vmem_limit_bytes=32 * MIB),
-        cost_estimate=cost(2 * owners * rows * CHUNKS * width * columns, *parts, *grads),
-    )(where, *values)
+    return whole_call(
+        functools.partial(right_near_kernel, max(columns // 512, PIECES)),
+        where,
+        [*parts, *grads],
+        [((CHUNKS * width, columns), F32)],
+        [pltpu.VMEM((owners * rows, CHUNKS * width), BF16)],
+        2 * owners * rows * CHUNKS * width * columns,
+    )[0]
+
+
+def right_far_kernel(blocks, scale, where, *refs):
+    parts, refs = refs[:CHUNKS], refs[CHUNKS:]
+    grads, (done, out, held, sems, ordered) = refs[:-5], refs[-5:]
+    block = held.shape[1] // blocks
+    order_parts(parts, ordered)
+    copies = []
+    for i in range(blocks):
+        columns = slice(i * block, (i + 1) * block)
+        total = done[:, columns] + right_sum(1 - where[0], parts, grads, ordered, columns)
+        held[:, columns] = total * scale
+        copies.append(write(held, out, sems, i, (slice(None), columns)))
+    for copy in copies:
+        copy.wait()
+
+
+def right_far(where, scale, parts, grads, done):
+    owners, rows, width = parts[0].shape
+    columns = grads[0].shape[1]
+    blocks = max(columns // 256, PIECES)
+    return written_call(
+        functools.partial(right_far_kernel, blocks, scale),
+        where,
+        [*parts, *grads, done],
+        (done.shape, F32),
+        blocks,
+        [pltpu.VMEM((owners * rows, CHUNKS * width), BF16)],
+        2 * owners * rows * CHUNKS * width * columns,
+        24,
+    )
 
 
 def final_kernel(scale, count, where, *refs):
-    out = refs[-1]
-    per = (len(refs) - 1) // count
+    refs, (out, held, sems) = refs[:-3], refs[-3:]
+    per = len(refs) // count
     width = refs[0].shape[0]
+    copies = []
     for chunk in range(count):
         total = refs[chunk * per][...]
         for other in refs[chunk * per + 1 : (chunk + 1) * per]:
             total = total + other[...].astype(F32)
-        out[chunk * width : (chunk + 1) * width, :] = total * scale
+        rows = slice(chunk * width, (chunk + 1) * width)
+        held[rows, :] = total * scale
+        copies.append(write(held, out, sems, chunk, (rows, slice(None))))
+    for copy in copies:
+        copy.wait()
+
+
+def left_final(where, scale, values, shape):
+    return written_call(
+        functools.partial(final_kernel, scale, CHUNKS), where, values, (shape, F32), CHUNKS, [], 0, 16
+    )
 
 
 def shards(activations, left_factor, right_factor, out_grad):
@@ -391,9 +460,9 @@
     def scoped(name, c, stage):
         return jax.named_scope(f"{NAMES[name]}{c}_{stage}")
 
-    def grad_send(c, limit):
+    def grad_send(c):
         with scoped("G", c, "S"):
-            (away,) = run(grad_product(0, BF16, c, 1, limit), out_grad)
+            (away,) = run(grad_product(0, BF16, c, 1, 24), out_grad)
             comes["G", c] = latest["G", c] = swap(away, "tensor", 1)
 
     def grad_keep():
@@ -488,41 +557,55 @@
                 *(v for c in range(CHUNKS) for v in [near["G", c], far["G", c]]),
             )
 
-    def rights(stage, *done):
-        parts = near if stage == "rn" else far
-        with scoped("L", "", stage):
+    def rights_near():
+        with scoped("L", "", "rn"):
             return run(
-                lambda *v: right_rows(
-                    where, stage == "rn", scale, v[:CHUNKS], v[CHUNKS : CHUNKS + 2 * owners], v[CHUNKS + 2 * owners :]
-                ),
-                *(parts["L", c] for c in range(CHUNKS)),
+                lambda *v: right_near(where, v[:CHUNKS], v[CHUNKS:]),
+                *(near["L", c] for c in range(CHUNKS)),
                 *grads,
-                *done,
+            )
+
+    def rights_far(done):
+        with scoped("L", "", "rf"):
+            return run(
+                lambda d, *v: right_far(where, scale, v[:CHUNKS], v[CHUNKS:], d),
+                done,
+                *(far["L", c] for c in range(CHUNKS)),
+                *grads,
             )
 
     def final():
         with scoped("G", "", "final"):
             return run(
-                lambda *v: whole_call(
-                    functools.partial(final_kernel, scale, CHUNKS), where, v, [((rows, depth), F32)]
-                )[0],
+                lambda *v: left_final(where, scale, v, (rows, depth)),
                 *(v for c in range(CHUNKS) for v in [left_mine[c], *left_in[c]]),
             )
 
     def settle(*values):
         run.last = (run.last, values)
 
-    with scoped("x", "", "og"):
-        far_grads = [swap(out_grad, "dp", 2 * s) for s in range(1, owners)]
-    with scoped("c", "", "acts"):
-        acts = (activations, swap(activations, "dp", 1))
-    with scoped("c", "", "own"):
-        grads = [out_grad, swap(out_grad, "dp", 1)]
+    far_grads, acts, grads = [], [activations], [out_grad]
+
+    def far_start():
+        with scoped("x", "", "og"):
+            for s in range(1, owners):
+                far_grads.append(swap(tied(out_grad, run), "dp", 2 * s))
+
+    def acts_swap():
+        with scoped("c", "", "acts"):
+            acts.append(swap(tied(activations, run), "dp", 1))
+
+    def own_swap():
+        with scoped("c", "", "own"):
+            grads.append(swap(tied(out_grad, run), "dp", 1))
 
     def far_swaps():
         with scoped("c", "", "far"):
             for block in far_grads:
-                grads.extend([block, swap(tied(block, run), "dp", 1)])
+                width = block.shape[1] // PIECES
+                grads.append(block)
+                for i in range(PIECES):
+                    grads.append(swap(block[:, i * width : (i + 1) * width], "dp", 1))
     input_grad = right_grad = left_grad = None
     actions = {
         "near": near_sum,
@@ -539,14 +622,20 @@
         elif entry == "LK":
             latent_keep()
         elif entry == "Lrn":
-            right_near = rights("rn")
+            right_near_sum = rights_near()
         elif entry == "Lrf":
-            right_grad = rights("rf", right_near)
+            right_grad = rights_far(right_near_sum)
         elif entry == "input":
             input_grad = inputs()
         elif entry == "final":
             left_grad = final()
         elif entry == "own":
+            own_swap()
+        elif entry == "acts":
+            acts_swap()
+        elif entry == "far":
+            far_start()
+        elif entry == "@own":
             settle(grads[1])
         elif entry == "og":
             far_swaps()
@@ -557,7 +646,7 @@
         else:
             name, c, stage = entry[0], int(entry[1]), entry[2:]
             if stage == "S":
-                grad_send(c, 24)
+                grad_send(c)
             elif stage == "halves":
                 core_halves(c)
             elif stage == "left":

time: 97.9 us -> 94.1 us (0.961)
  waiting for transfers between devices: 23.8 us -> 21.3 us
  Pallas kernels: 35 us -> 33.6 us
    pallas_call x3, Pallas kernels: 11.6 us -> 8.41 us  [written_call(): pl.pallas_call(kernel, out_shape=jax.ShapeDtypeStruct(shape, dtype), in_s...]
    ppermute x29 -> x33, waiting for transfers between devices: 23.8 us -> 21.3 us  [swap(): return lax.ppermute(value, axis, [(i, i ^ mask) for i in range(size)])]
    pallas_call x22 -> x23, Pallas kernels: 15.4 us -> 17.2 us  [whole_call(): pl.pallas_call(kernel, out_shape=[jax.ShapeDtypeStruct(s, t) for s, t in...]
    ppermute x29 -> x33, starting transfers between devices: 34 us -> 33.9 us  [swap(): return lax.ppermute(value, axis, [(i, i ^ mask) for i in range(size)])]
    unnamed x12 -> x10, local copies, waits for them, and re-layouts: 3.8 us -> 3.8 us
  transfers between devices with their start and end apart: 29 -> 33, of which waited for: 11 -> 9; matrix products, arithmetic and copies ran while one was open for 0% -> 0% of each run, Pallas kernels for 34% -> 34%
where the time goes in v3:
time: 94.1 us; the launch traced here: 93.9 us
  starting transfers between devices  33.9 us (36%)
  Pallas kernels  33.6 us (36%)
  waiting for transfers between devices  21.3 us (23%)
  local copies, waits for them, and re-layouts  4.04 us (4%)
  between operations  1.05 us (1%)
    ppermute x33, starting transfers between devices, swap(): return lax.ppermute(value, axis, [(i, i ^ mask) for i in range(size)])  33.9 us
    ppermute x33, waiting for transfers between devices, swap(): return lax.ppermute(value, axis, [(i, i ^ mask) for i in range(size)])  21.3 us
    pallas_call x23, Pallas kernels, whole_call(): pl.pallas_call(kernel, out_shape=[jax.ShapeDtypeStruct(s, t) for s, t in...  17.2 us
    pallas_call x3, Pallas kernels, written_call(): pl.pallas_call(kernel, out_shape=jax.ShapeDtypeStruct(shape, dtype), in_s...  8.41 us
    pallas_call x5, Pallas kernels, products(): pl.pallas_call(functools.partial(product_kernel, chunks), out_shape=[jax....  7.99 us
    unnamed x10, local copies, waits for them, and re-layouts  3.8 us
  transfers between devices with their start and end apart: 33, of which 9 were waited for; matrix products, arithmetic and copies ran while one was open for 0% of the time, Pallas kernels for 34%

profile of v3, /device:TPU:0, one launch (start us, length us, event | category | flops | bytes accessed | tf_op | source)
XLA Modules:
  0.0 93.9 jit_solution(7398028624200149014)
XLA Ops:
  1.1 2.6 %collective-permute-start.26 = (bf16[512,2048]{1,0:T(8,128)(2,1)}, bf16[512,2048]{1,0:T(8,128)(2,1)S(1)}, u32[]{:S(2)}, u32[]{:S(2)}) collective-permute-start(bf16[512,2048]{1,0:T(8,128)(2,1)} %refs_2_.1), channel_id=1, source_target_pairs={{0,16},{8,24},{16,0},{24,8},{1,17},{9,25},{17,1},{25,9},{2,18},{10... | collective-permute-start | bytes 6291464 | tf_op jit(solution)/shard_map/far_og/ppermute | solution.py:55
  4.0 1.6 %copy-done = bf16[512,2048]{1,0:T(8,128)(2,1)S(1)} copy-done((bf16[512,2048]{1,0:T(8,128)(2,1)S(1)}, bf16[512,2048]{1,0:T(8,128)(2,1)}, u32[]{:S(2)}) %copy-start) | copy-done | bytes 2097176
  5.6 2.2 %copy-done.2 = bf16[1024,2048]{1,0:T(8,128)(2,1)S(1)} copy-done((bf16[1024,2048]{1,0:T(8,128)(2,1)S(1)}, bf16[1024,2048]{1,0:T(8,128)(2,1)}, u32[]{:S(2)}) %copy-start.2) | copy-done | bytes 4194328
  7.7 1.7 %latent_grad1_S.1 = bf16[4,256,128]{2,1,0:T(8,128)(2,1)S(1)} custom-call(s32[5]{0:T(128)S(1)} %stack.23.where, bf16[512,2048]{1,0:T(8,128)(2,1)S(1)} %copy-done, bf16[4,2,128,2048]{3,2,1,0:T(8,128)(2,1)S(1)} %bitcast.7), custom_call_target="tpu_custom_call" | custom-call | flops 536870912 | bytes 4194304 | tf_op jit(solution)/shard_map/latent_grad1_S/pallas_call | solution.py:97
  9.4 1.6 %collective-permute-start.4 = (bf16[4,256,128]{2,1,0:T(8,128)(2,1)S(1)}, bf16[4,256,128]{2,1,0:T(8,128)(2,1)S(1)}, u32[]{:S(2)}, u32[]{:S(2)}) collective-permute-start(bf16[4,256,128]{2,1,0:T(8,128)(2,1)S(1)} %latent_grad1_S.1), channel_id=1, source_target_pairs={{0,1},{1,0},{2,3},{3,2},{4,5},{5,4},{6,7},{7,6},{8,9},{9,8},{10,11... | collective-permute-start | bytes 786440 | tf_op jit(solution)/shard_map/latent_grad1_S/ppermute | solution.py:55
  11.0 1.7 %latent_grad0_S.1 = bf16[4,256,128]{2,1,0:T(8,128)(2,1)S(1)} custom-call(s32[5]{0:T(128)S(1)} %stack.23.where, bf16[512,2048]{1,0:T(8,128)(2,1)S(1)} %copy-done, bf16[4,2,128,2048]{3,2,1,0:T(8,128)(2,1)S(1)} %bitcast.8), custom_call_target="tpu_custom_call" | custom-call | flops 536870912 | bytes 4194304 | tf_op jit(solution)/shard_map/latent_grad0_S/pallas_call | solution.py:97
  12.7 0.6 collective-permute-start
  13.3 2.1 %latent_grad_K.1 = (f32[4,256,128]{2,1,0:T(8,128)S(1)}, f32[4,256,128]{2,1,0:T(8,128)S(1)}) custom-call(s32[5]{0:T(128)S(1)} %stack.23.where, bf16[512,2048]{1,0:T(8,128)(2,1)S(1)} %copy-done, bf16[4,2,128,2048]{3,2,1,0:T(8,128)(2,1)S(1)} %bitcast.9), custom_call_target="tpu_custom_call" | custom-call | flops 1073741824 | bytes 6291456 | tf_op jit(solution)/shard_map/latent_grad_K/pallas_call | solution.py:97
  15.4 1.3 %latent_S.1 = (bf16[2,512,128]{2,1,0:T(8,128)(2,1)S(1)}, bf16[2,512,128]{2,1,0:T(8,128)(2,1)S(1)}) custom-call(s32[5]{0:T(128)S(1)} %stack.23.where, bf16[512,1024]{1,0:T(8,128)(2,1)S(1)} %copy-done.4, bf16[512,1024]{1,0:T(8,128)(2,1)S(1)} %collective-permute-done.1.refs_1_.acts_other, bf16[2,2,2,128,1024]{4,3,2,1,0:T(8,128)(2,1)S(1)} %bitcast.10), custom_call_target="tpu_custom_call" | custom-call | flops 536870912 | bytes 3145728 | tf_op jit(solution)/shard_map/latent_S/pallas_call | solution.py:97
  16.7 1.6 %collective-permute-start.6 = (bf16[2,512,128]{2,1,0:T(8,128)(2,1)S(1)}, bf16[2,512,128]{2,1,0:T(8,128)(2,1)S(1)}, u32[]{:S(2)}, u32[]{:S(2)}) collective-permute-start(bf16[2,512,128]{2,1,0:T(8,128)(2,1)S(1)} %get-tuple-element.123), channel_id=1, source_target_pairs={{0,1},{1,0},{2,3},{3,2},{4,5},{5,4},{6,7},{7,6},{8,9},{9,8},{10,11... | collective-permute-start | bytes 786440 | tf_op jit(solution)/shard_map/latent_S/ppermute | solution.py:55
  18.8 1.3 %latent_K.1 = (f32[2,512,128]{2,1,0:T(8,128)S(1)}, f32[2,512,128]{2,1,0:T(8,128)S(1)}) custom-call(s32[5]{0:T(128)S(1)} %stack.23.where, bf16[512,1024]{1,0:T(8,128)(2,1)S(1)} %copy-done.4, bf16[512,1024]{1,0:T(8,128)(2,1)S(1)} %collective-permute-done.1.refs_1_.acts_other, bf16[2,2,2,128,1024]{4,3,2,1,0:T(8,128)(2,1)S(1)} %bitcast.11), custom_call_target="tpu_custom_call" | custom-call | flops 536870912 | bytes 3145728 | tf_op jit(solution)/shard_map/latent_K/pallas_call | solution.py:97
  20.1 4.2 %collective-permute-done.sent = bf16[4,256,128]{2,1,0:T(8,128)(2,1)S(1)} collective-permute-done((bf16[4,256,128]{2,1,0:T(8,128)(2,1)S(1)}, bf16[4,256,128]{2,1,0:T(8,128)(2,1)S(1)}, u32[]{:S(2)}, u32[]{:S(2)}) %collective-permute-start) | collective-permute-done | bytes 262176 | tf_op jit(solution)/shard_map/latent_grad0_S/ppermute | solution.py:55
  24.2 0.6 latent_grad0_near.1
  24.8 1.6 %collective-permute-start.3 = (bf16[4,128,128]{2,1,0:T(8,128)(2,1)S(1)}, bf16[4,128,128]{2,1,0:T(8,128)(2,1)S(1)}, u32[]{:S(2)}, u32[]{:S(2)}) collective-permute-start(bf16[4,128,128]{2,1,0:T(8,128)(2,1)S(1)} %get-tuple-element.132), channel_id=1, source_target_pairs={{0,2},{1,3},{2,0},{3,1},{4,6},{5,7},{6,4},{7,5},{8,10},{9,11},{10,... | collective-permute-start | bytes 393224 | tf_op jit(solution)/shard_map/latent_grad0_near/ppermute | solution.py:55
  26.5 0.6 latent_grad1_near.1
  27.6 3.7 %collective-permute-done.3.other = bf16[4,128,128]{2,1,0:T(8,128)(2,1)S(1)} collective-permute-done((bf16[4,128,128]{2,1,0:T(8,128)(2,1)S(1)}, bf16[4,128,128]{2,1,0:T(8,128)(2,1)S(1)}, u32[]{:S(2)}, u32[]{:S(2)}) %collective-permute-start.3) | collective-permute-done | bytes 131104 | tf_op jit(solution)/shard_map/latent_grad0_near/ppermute | solution.py:55
  31.3 0.6 latent_grad0_far.1
  31.9 0.6 latent0_near.1
  32.5 1.1 %collective-permute-start.7 = (bf16[2,256,128]{2,1,0:T(8,128)(2,1)S(1)}, bf16[2,256,128]{2,1,0:T(8,128)(2,1)S(1)}, u32[]{:S(2)}, u32[]{:S(2)}) collective-permute-start(bf16[2,256,128]{2,1,0:T(8,128)(2,1)S(1)} %get-tuple-element.144), channel_id=1, source_target_pairs={{0,2},{1,3},{2,0},{3,1},{4,6},{5,7},{6,4},{7,5},{8,10},{9,11},{10,... | collective-permute-start | bytes 393224 | tf_op jit(solution)/shard_map/latent0_near/ppermute | solution.py:55
  33.5 2.6 %collective-permute-start.5 = (bf16[4,128,128]{2,1,0:T(8,128)(2,1)S(1)}, bf16[4,128,128]{2,1,0:T(8,128)(2,1)S(1)}, u32[]{:S(2)}, u32[]{:S(2)}) collective-permute-start(bf16[4,128,128]{2,1,0:T(8,128)(2,1)S(1)} %get-tuple-element.140), channel_id=1, source_target_pairs={{0,4},{1,5},{2,6},{3,7},{4,0},{5,1},{6,2},{7,3},{8,12},{9,13},{10,... | collective-permute-start | bytes 393224 | tf_op jit(solution)/shard_map/latent_grad0_far/ppermute | solution.py:55
  36.1 0.6 latent_grad1_far.1
  37.1 0.6 latent1_near.1
  37.7 1.1 %collective-permute-start.11 = (bf16[2,256,128]{2,1,0:T(8,128)(2,1)S(1)}, bf16[2,256,128]{2,1,0:T(8,128)(2,1)S(1)}, u32[]{:S(2)}, u32[]{:S(2)}) collective-permute-start(bf16[2,256,128]{2,1,0:T(8,128)(2,1)S(1)} %get-tuple-element.152), channel_id=1, source_target_pairs={{0,2},{1,3},{2,0},{3,1},{4,6},{5,7},{6,4},{7,5},{8,10},{9,11},{10,... | collective-permute-start | bytes 393224 | tf_op jit(solution)/shard_map/latent1_near/ppermute | solution.py:55
  38.8 0.6 latent0_far.1
  39.4 3.5 %collective-permute-done.5.other = bf16[4,128,128]{2,1,0:T(8,128)(2,1)S(1)} collective-permute-done((bf16[4,128,128]{2,1,0:T(8,128)(2,1)S(1)}, bf16[4,128,128]{2,1,0:T(8,128)(2,1)S(1)}, u32[]{:S(2)}, u32[]{:S(2)}) %collective-permute-start.5) | collective-permute-done | bytes 131104 | tf_op jit(solution)/shard_map/latent_grad0_far/ppermute | solution.py:55
  43.4 1.3 %collective-permute-start.10 = (bf16[4,128,128]{2,1,0:T(8,128)(2,1)S(1)}, bf16[4,128,128]{2,1,0:T(8,128)(2,1)S(1)}, u32[]{:S(2)}, u32[]{:S(2)}) collective-permute-start(bf16[4,128,128]{2,1,0:T(8,128)(2,1)S(1)} %latent_grad0_last.1.mine), channel_id=1, source_target_pairs={{0,2},{1,3},{2,0},{3,1},{4,6},{5,7},{6,4},{7,5},{8,10},{9,11},{10,... | collective-permute-start | bytes 393224 | tf_op jit(solution)/shard_map/latent_grad0_last/ppermute | solution.py:55
  44.8 3.2 %collective-permute-start.15 = (bf16[2,256,128]{2,1,0:T(8,128)(2,1)S(1)}, bf16[2,256,128]{2,1,0:T(8,128)(2,1)S(1)}, u32[]{:S(2)}, u32[]{:S(2)}) collective-permute-start(bf16[2,256,128]{2,1,0:T(8,128)(2,1)S(1)} %get-tuple-element.156), channel_id=1, source_target_pairs={{0,4},{1,5},{2,6},{3,7},{4,0},{5,1},{6,2},{7,3},{8,12},{9,13},{10,... | collective-permute-start | bytes 393224 | tf_op jit(solution)/shard_map/latent0_far/ppermute | solution.py:55
  48.0 0.9 collective-permute-done.12.other
  49.6 0.6 latent1_far.1
  50.2 3.0 %collective-permute-start.17 = (bf16[2,256,128]{2,1,0:T(8,128)(2,1)S(1)}, bf16[2,256,128]{2,1,0:T(8,128)(2,1)S(1)}, u32[]{:S(2)}, u32[]{:S(2)}) collective-permute-start(bf16[2,256,128]{2,1,0:T(8,128)(2,1)S(1)} %get-tuple-element.164), channel_id=1, source_target_pairs={{0,4},{1,5},{2,6},{3,7},{4,0},{5,1},{6,2},{7,3},{8,12},{9,13},{10,... | collective-permute-start | bytes 393224 | tf_op jit(solution)/shard_map/latent1_far/ppermute | solution.py:55
  54.4 0.6 collective-permute-start.18
  55.0 1.5 %collective-permute-start.13 = (bf16[4,256,128]{2,1,0:T(8,128)(2,1)S(1)}, bf16[4,256,128]{2,1,0:T(8,128)(2,1)S(1)}, u32[]{:S(2)}, u32[]{:S(2)}) collective-permute-start(bf16[4,256,128]{2,1,0:T(8,128)(2,1)S(1)} %latent_grad0_join.1.near.refs_0_), channel_id=1, source_target_pairs={{0,1},{1,0},{2,3},{3,2},{4,5},{5,4},{6,7},{7,6},{8,9},{9,8},{10,11... | collective-permute-start | bytes 786440 | tf_op jit(solution)/shard_map/latent_grad0_join/ppermute | solution.py:55
  57.6 1.4 %collective-permute-done.18.refs_1_ = bf16[256,128]{1,0:T(8,128)(2,1)S(1)} collective-permute-done((bf16[256,128]{1,0:T(8,128)(2,1)S(1)}, bf16[256,128]{1,0:T(8,128)(2,1)S(1)}, u32[]{:S(2)}, u32[]{:S(2)}) %collective-permute-start.18) | collective-permute-done | bytes 65568 | tf_op jit(solution)/shard_map/latent0_last/ppermute | solution.py:55
  59.6 0.9 collective-permute-start.20
  61.1 0.6 collective-permute-start.19
  63.1 1.6 %collective-permute-done.20.other = bf16[2,256,128]{2,1,0:T(8,128)(2,1)S(1)} collective-permute-done((bf16[2,256,128]{2,1,0:T(8,128)(2,1)S(1)}, bf16[2,256,128]{2,1,0:T(8,128)(2,1)S(1)}, u32[]{:S(2)}, u32[]{:S(2)}) %collective-permute-start.20) | collective-permute-done | bytes 131104 | tf_op jit(solution)/shard_map/latent0_stack/ppermute | solution.py:55
  66.0 1.3 %collective-permute-start.22 = (bf16[2,256,128]{2,1,0:T(8,128)(2,1)S(1)}, bf16[2,256,128]{2,1,0:T(8,128)(2,1)S(1)}, u32[]{:S(2)}, u32[]{:S(2)}) collective-permute-start(bf16[2,256,128]{2,1,0:T(8,128)(2,1)S(1)} %latent1_stack.1.mine), channel_id=1, source_target_pairs={{0,2},{1,3},{2,0},{3,1},{4,6},{5,7},{6,4},{7,5},{8,10},{9,11},{10,... | collective-permute-start | bytes 393224 | tf_op jit(solution)/shard_map/latent1_stack/ppermute | solution.py:55
  67.8 3.2 %collective-permute-done.22.other = bf16[2,256,128]{2,1,0:T(8,128)(2,1)S(1)} collective-permute-done((bf16[2,256,128]{2,1,0:T(8,128)(2,1)S(1)}, bf16[2,256,128]{2,1,0:T(8,128)(2,1)S(1)}, u32[]{:S(2)}, u32[]{:S(2)}) %collective-permute-start.22) | collective-permute-done | bytes 131104 | tf_op jit(solution)/shard_map/latent1_stack/ppermute | solution.py:55
  71.6 0.6 collective-permute-start.21
  72.2 1.4 %latent_grad0_left.1 = (f32[128,1024]{1,0:T(8,128)S(1)}, bf16[128,1024]{1,0:T(8,128)(2,1)S(1)}) custom-call(s32[5]{0:T(128)S(1)} %stack.23.where, bf16[4,256,128]{2,1,0:T(8,128)(2,1)S(1)} %latent_grad0_join.1.near.refs_0_, bf16[4,256,128]{2,1,0:T(8,128)(2,1)S(1)} %collective-permute-done.13.far.refs_1_, ...), custom_call_target="tpu_custom_call" | custom-call | flops 536870912 | bytes 3670016 | tf_op jit(solution)/shard_map/latent_grad0_left/pallas_call | solution.py:41
  74.2 2.1 %collective-permute-start.31 = (bf16[2,512,128]{2,1,0:T(8,128)(2,1)S(1)}, bf16[2,512,128]{2,1,0:T(8,128)(2,1)S(1)}, u32[]{:S(2)}, u32[]{:S(2)}) collective-permute-start(bf16[2,512,128]{2,1,0:T(8,128)(2,1)S(1)} %latent0_join.1.refs_0_), channel_id=1, source_target_pairs={{0,1},{1,0},{2,3},{3,2},{4,5},{5,4},{6,7},{7,6},{8,9},{9,8},{10,11... | collective-permute-start | bytes 786440 | tf_op jit(solution)/shard_map/latent0_join/ppermute | solution.py:55
  76.4 1.4 %latent_grad1_left.1 = (f32[128,1024]{1,0:T(8,128)S(1)}, bf16[128,1024]{1,0:T(8,128)(2,1)S(1)}) custom-call(s32[5]{0:T(128)S(1)} %stack.23.where, bf16[4,256,128]{2,1,0:T(8,128)(2,1)S(1)} %latent_grad1_join.1.near.refs_2_, bf16[4,256,128]{2,1,0:T(8,128)(2,1)S(1)} %collective-permute-done.16.far.refs_3_, ...), custom_call_target="tpu_custom_call" | custom-call | flops 536870912 | bytes 3670016 | tf_op jit(solution)/shard_map/latent_grad1_left/pallas_call | solution.py:41
  78.3 1.6 %collective-permute-start.24 = (bf16[128,1024]{1,0:T(8,128)(2,1)S(1)}, bf16[128,1024]{1,0:T(8,128)(2,1)S(1)}, u32[]{:S(2)}, u32[]{:S(2)}) collective-permute-start(bf16[128,1024]{1,0:T(8,128)(2,1)S(1)} %get-tuple-element.193), channel_id=1, source_target_pairs={{0,16},{8,24},{16,0},{24,8},{1,17},{9,25},{17,1},{25,9},{2,18},{10... | collective-permute-start | bytes 786440 | tf_op jit(solution)/shard_map/latent_grad0_left/ppermute | solution.py:55
  79.9 2.9 %latent_grad_input.1 = bf16[512,1024]{1,0:T(8,128)(2,1)} custom-call(s32[5]{0:T(128)S(1)} %stack.23.where, bf16[4,256,128]{2,1,0:T(8,128)(2,1)S(1)} %latent_grad0_join.1.near.refs_0_, bf16[4,256,128]{2,1,0:T(8,128)(2,1)S(1)} %collective-permute-done.13.far.refs_1_, bf16[4,256,128]{2,1,0:T(8,128)(2,1)S(1)} %latent_grad1_join.1.near.refs_2_, ...), custom_call_target="tpu_custom_call" | custom-call | flops 1073741824 | bytes 3145728 | tf_op jit(solution)/shard_map/latent_grad_input/pallas_call | solution.py:243
  82.9 2.9 %latent_rn.1.refs_9_ = f32[256,2048]{1,0:T(8,128)S(1)} custom-call(s32[5]{0:T(128)S(1)} %stack.23.where, bf16[2,512,128]{2,1,0:T(8,128)(2,1)S(1)} %latent0_join.1.refs_0_, bf16[2,512,128]{2,1,0:T(8,128)(2,1)S(1)} %latent1_join.1.refs_1_, bf16[512,2048]{1,0:T(8,128)(2,1)S(1)} %copy-done.1, bf16[512,2048]{1,0:T(8,128)(2,1)} %collective-permute-done.2.refs_3_, ...), custom_call_target="tpu_custom_call" | custom-call | flops 1073741824 | bytes 11010048 | tf_op jit(solution)/shard_map/latent_rn/pallas_call | solution.py:41
  85.8 2.6 %collective-permute-done.32.refs_1_ = bf16[2,512,128]{2,1,0:T(8,128)(2,1)S(1)} collective-permute-done((bf16[2,512,128]{2,1,0:T(8,128)(2,1)S(1)}, bf16[2,512,128]{2,1,0:T(8,128)(2,1)S(1)}, u32[]{:S(2)}, u32[]{:S(2)}) %collective-permute-start.32) | collective-permute-done | bytes 262176 | tf_op jit(solution)/shard_map/latent1_join/ppermute | solution.py:55
  88.4 3.9 %latent_rf.1 = f32[256,2048]{1,0:T(8,128)} custom-call(s32[5]{0:T(128)S(1)} %stack.23.where, bf16[2,512,128]{2,1,0:T(8,128)(2,1)S(1)} %collective-permute-done.31.refs_0_, bf16[2,512,128]{2,1,0:T(8,128)(2,1)S(1)} %collective-permute-done.32.refs_1_, bf16[512,2048]{1,0:T(8,128)(2,1)S(1)} %copy-done.1, bf16[512,2048]{1,0:T(8,128)(2,1)} %collective-permute-done.2.refs_3_, ...), custom_call_target="tpu_custom_call" | custom-call | flops 1073741824 | bytes 11010048 | tf_op jit(solution)/shard_map/latent_rf/pallas_call | solution.py:243
  92.3 1.6 %latent_grad_final.1 = f32[256,1024]{1,0:T(8,128)} custom-call(s32[5]{0:T(128)S(1)} %stack.23.where, f32[128,1024]{1,0:T(8,128)S(1)} %get-tuple-element.227.refs_0_, bf16[128,1024]{1,0:T(8,128)(2,1)S(1)} %collective-permute-done.24.refs_1_, f32[128,1024]{1,0:T(8,128)S(1)} %get-tuple-element.229.refs_2_, bf16[128,1024]{1,0:T(8,128)(2,1)S(1)} %collective-permute-done.25.refs_3_), custom_call_target="tpu_custom_call" | custom-call | bytes 1572864 | tf_op jit(solution)/shard_map/latent_grad_final/pallas_call | solution.py:243
  (61 shorter events, 11.7 us)
Async XLA Ops:
  0.6 17.7 %collective-permute-start.2 = (bf16[512,2048]{1,0:T(8,128)(2,1)}, bf16[512,2048]{1,0:T(8,128)(2,1)}, u32[]{:S(2)}, u32[]{:S(2)}) collective-permute-start(bf16[512,2048]{1,0:T(8,128)(2,1)} %refs_2_.1), channel_id=1, source_target_pairs={{0,8},{8,0},{16,24},{24,16},{1,9},{9,1},{17,25},{25,17},{2,10},{10... | collective-permute-start | bytes 6291464 | tf_op jit(solution)/shard_map/core_own/ppermute | solution.py:55
  1.1 60.5 %collective-permute-start.26 = (bf16[512,2048]{1,0:T(8,128)(2,1)}, bf16[512,2048]{1,0:T(8,128)(2,1)S(1)}, u32[]{:S(2)}, u32[]{:S(2)}) collective-permute-start(bf16[512,2048]{1,0:T(8,128)(2,1)} %refs_2_.1), channel_id=1, source_target_pairs={{0,16},{8,24},{16,0},{24,8},{1,17},{9,25},{17,1},{25,9},{2,18},{10... | collective-permute-start | bytes 6291464 | tf_op jit(solution)/shard_map/far_og/ppermute | solution.py:55
  3.7 11.7 %collective-permute-start.1 = (bf16[512,1024]{1,0:T(8,128)(2,1)}, bf16[512,1024]{1,0:T(8,128)(2,1)S(1)}, u32[]{:S(2)}, u32[]{:S(2)}) collective-permute-start(bf16[512,1024]{1,0:T(8,128)(2,1)} %acts.1), channel_id=1, source_target_pairs={{0,8},{8,0},{16,24},{24,16},{1,9},{9,1},{17,25},{25,17},{2,10},{10... | collective-permute-start | bytes 3145736 | tf_op jit(solution)/shard_map/core_acts/ppermute | solution.py:55
  4.0 1.6 %copy-start = (bf16[512,2048]{1,0:T(8,128)(2,1)S(1)}, bf16[512,2048]{1,0:T(8,128)(2,1)}, u32[]{:S(2)}) copy-start(bf16[512,2048]{1,0:T(8,128)(2,1)} %refs_2_.1) | copy-start | bytes 6291460
  5.6 2.2 %copy-start.2 = (bf16[1024,2048]{1,0:T(8,128)(2,1)S(1)}, bf16[1024,2048]{1,0:T(8,128)(2,1)}, u32[]{:S(2)}) copy-start(bf16[1024,2048]{1,0:T(8,128)(2,1)} %param.6) | copy-start | bytes 12582916
  9.4 17.0 %collective-permute-start.4 = (bf16[4,256,128]{2,1,0:T(8,128)(2,1)S(1)}, bf16[4,256,128]{2,1,0:T(8,128)(2,1)S(1)}, u32[]{:S(2)}, u32[]{:S(2)}) collective-permute-start(bf16[4,256,128]{2,1,0:T(8,128)(2,1)S(1)} %latent_grad1_S.1), channel_id=1, source_target_pairs={{0,1},{1,0},{2,3},{3,2},{4,5},{5,4},{6,7},{7,6},{8,9},{9,8},{10,11... | collective-permute-start | bytes 786440 | tf_op jit(solution)/shard_map/latent_grad1_S/ppermute | solution.py:55
  12.7 2.7 %copy-start.3 = (bf16[1024,1024]{1,0:T(8,128)(2,1)S(1)}, bf16[1024,1024]{1,0:T(8,128)(2,1)}, u32[]{:S(2)}) copy-start(bf16[1024,1024]{1,0:T(8,128)(2,1)} %refs_4_) | copy-start | bytes 6291460
  12.7 2.7 %copy-start.4 = (bf16[512,1024]{1,0:T(8,128)(2,1)S(1)}, bf16[512,1024]{1,0:T(8,128)(2,1)}, u32[]{:S(2)}) copy-start(bf16[512,1024]{1,0:T(8,128)(2,1)} %acts.1) | copy-start | bytes 3145732
  12.7 11.5 %collective-permute-start = (bf16[4,256,128]{2,1,0:T(8,128)(2,1)S(1)}, bf16[4,256,128]{2,1,0:T(8,128)(2,1)S(1)}, u32[]{:S(2)}, u32[]{:S(2)}) collective-permute-start(bf16[4,256,128]{2,1,0:T(8,128)(2,1)S(1)} %latent_grad0_S.1), channel_id=1, source_target_pairs={{0,1},{1,0},{2,3},{3,2},{4,5},{5,4},{6,7},{7,6},{8,9},{9,8},{10,11... | collective-permute-start | bytes 786440 | tf_op jit(solution)/shard_map/latent_grad0_S/ppermute | solution.py:55
  16.7 15.1 %collective-permute-start.6 = (bf16[2,512,128]{2,1,0:T(8,128)(2,1)S(1)}, bf16[2,512,128]{2,1,0:T(8,128)(2,1)S(1)}, u32[]{:S(2)}, u32[]{:S(2)}) collective-permute-start(bf16[2,512,128]{2,1,0:T(8,128)(2,1)S(1)} %get-tuple-element.123), channel_id=1, source_target_pairs={{0,1},{1,0},{2,3},{3,2},{4,5},{5,4},{6,7},{7,6},{8,9},{9,8},{10,11... | collective-permute-start | bytes 786440 | tf_op jit(solution)/shard_map/latent_S/ppermute | solution.py:55
  18.3 18.8 %collective-permute-start.8 = (bf16[2,512,128]{2,1,0:T(8,128)(2,1)S(1)}, bf16[2,512,128]{2,1,0:T(8,128)(2,1)S(1)}, u32[]{:S(2)}, u32[]{:S(2)}) collective-permute-start(bf16[2,512,128]{2,1,0:T(8,128)(2,1)S(1)} %get-tuple-element.124), channel_id=1, source_target_pairs={{0,1},{1,0},{2,3},{3,2},{4,5},{5,4},{6,7},{7,6},{8,9},{9,8},{10,11... | collective-permute-start | bytes 786440 | tf_op jit(solution)/shard_map/latent_S/ppermute | solution.py:55
  24.8 6.4 %collective-permute-start.3 = (bf16[4,128,128]{2,1,0:T(8,128)(2,1)S(1)}, bf16[4,128,128]{2,1,0:T(8,128)(2,1)S(1)}, u32[]{:S(2)}, u32[]{:S(2)}) collective-permute-start(bf16[4,128,128]{2,1,0:T(8,128)(2,1)S(1)} %get-tuple-element.132), channel_id=1, source_target_pairs={{0,2},{1,3},{2,0},{3,1},{4,6},{5,7},{6,4},{7,5},{8,10},{9,11},{10,... | collective-permute-start | bytes 393224 | tf_op jit(solution)/shard_map/latent_grad0_near/ppermute | solution.py:55
  27.1 9.0 %collective-permute-start.9 = (bf16[4,128,128]{2,1,0:T(8,128)(2,1)S(1)}, bf16[4,128,128]{2,1,0:T(8,128)(2,1)S(1)}, u32[]{:S(2)}, u32[]{:S(2)}) collective-permute-start(bf16[4,128,128]{2,1,0:T(8,128)(2,1)S(1)} %get-tuple-element.136), channel_id=1, source_target_pairs={{0,2},{1,3},{2,0},{3,1},{4,6},{5,7},{6,4},{7,5},{8,10},{9,11},{10,... | collective-permute-start | bytes 393224 | tf_op jit(solution)/shard_map/latent_grad1_near/ppermute | solution.py:55
  32.5 6.3 %collective-permute-start.7 = (bf16[2,256,128]{2,1,0:T(8,128)(2,1)S(1)}, bf16[2,256,128]{2,1,0:T(8,128)(2,1)S(1)}, u32[]{:S(2)}, u32[]{:S(2)}) collective-permute-start(bf16[2,256,128]{2,1,0:T(8,128)(2,1)S(1)} %get-tuple-element.144), channel_id=1, source_target_pairs={{0,2},{1,3},{2,0},{3,1},{4,6},{5,7},{6,4},{7,5},{8,10},{9,11},{10,... | collective-permute-start | bytes 393224 | tf_op jit(solution)/shard_map/latent0_near/ppermute | solution.py:55
  33.5 9.3 %collective-permute-start.5 = (bf16[4,128,128]{2,1,0:T(8,128)(2,1)S(1)}, bf16[4,128,128]{2,1,0:T(8,128)(2,1)S(1)}, u32[]{:S(2)}, u32[]{:S(2)}) collective-permute-start(bf16[4,128,128]{2,1,0:T(8,128)(2,1)S(1)} %get-tuple-element.140), channel_id=1, source_target_pairs={{0,4},{1,5},{2,6},{3,7},{4,0},{5,1},{6,2},{7,3},{8,12},{9,13},{10,... | collective-permute-start | bytes 393224 | tf_op jit(solution)/shard_map/latent_grad0_far/ppermute | solution.py:55
  36.7 12.2 %collective-permute-start.12 = (bf16[4,128,128]{2,1,0:T(8,128)(2,1)S(1)}, bf16[4,128,128]{2,1,0:T(8,128)(2,1)S(1)}, u32[]{:S(2)}, u32[]{:S(2)}) collective-permute-start(bf16[4,128,128]{2,1,0:T(8,128)(2,1)S(1)} %get-tuple-element.148), channel_id=1, source_target_pairs={{0,4},{1,5},{2,6},{3,7},{4,0},{5,1},{6,2},{7,3},{8,12},{9,13},{10,... | collective-permute-start | bytes 393224 | tf_op jit(solution)/shard_map/latent_grad1_far/ppermute | solution.py:55
  37.7 11.9 %collective-permute-start.11 = (bf16[2,256,128]{2,1,0:T(8,128)(2,1)S(1)}, bf16[2,256,128]{2,1,0:T(8,128)(2,1)S(1)}, u32[]{:S(2)}, u32[]{:S(2)}) collective-permute-start(bf16[2,256,128]{2,1,0:T(8,128)(2,1)S(1)} %get-tuple-element.152), channel_id=1, source_target_pairs={{0,2},{1,3},{2,0},{3,1},{4,6},{5,7},{6,4},{7,5},{8,10},{9,11},{10,... | collective-permute-start | bytes 393224 | tf_op jit(solution)/shard_map/latent1_near/ppermute | solution.py:55
  43.4 9.8 %collective-permute-start.10 = (bf16[4,128,128]{2,1,0:T(8,128)(2,1)S(1)}, bf16[4,128,128]{2,1,0:T(8,128)(2,1)S(1)}, u32[]{:S(2)}, u32[]{:S(2)}) collective-permute-start(bf16[4,128,128]{2,1,0:T(8,128)(2,1)S(1)} %latent_grad0_last.1.mine), channel_id=1, source_target_pairs={{0,2},{1,3},{2,0},{3,1},{4,6},{5,7},{6,4},{7,5},{8,10},{9,11},{10,... | collective-permute-start | bytes 393224 | tf_op jit(solution)/shard_map/latent_grad0_last/ppermute | solution.py:55
  44.8 9.0 %collective-permute-start.15 = (bf16[2,256,128]{2,1,0:T(8,128)(2,1)S(1)}, bf16[2,256,128]{2,1,0:T(8,128)(2,1)S(1)}, u32[]{:S(2)}, u32[]{:S(2)}) collective-permute-start(bf16[2,256,128]{2,1,0:T(8,128)(2,1)S(1)} %get-tuple-element.156), channel_id=1, source_target_pairs={{0,4},{1,5},{2,6},{3,7},{4,0},{5,1},{6,2},{7,3},{8,12},{9,13},{10,... | collective-permute-start | bytes 393224 | tf_op jit(solution)/shard_map/latent0_far/ppermute | solution.py:55
  49.5 7.0 %collective-permute-start.14 = (bf16[4,128,128]{2,1,0:T(8,128)(2,1)S(1)}, bf16[4,128,128]{2,1,0:T(8,128)(2,1)S(1)}, u32[]{:S(2)}, u32[]{:S(2)}) collective-permute-start(bf16[4,128,128]{2,1,0:T(8,128)(2,1)S(1)} %latent_grad1_last.1.mine), channel_id=1, source_target_pairs={{0,2},{1,3},{2,0},{3,1},{4,6},{5,7},{6,4},{7,5},{8,10},{9,11},{10,... | collective-permute-start | bytes 393224 | tf_op jit(solution)/shard_map/latent_grad1_last/ppermute | solution.py:55
  50.2 10.3 %collective-permute-start.17 = (bf16[2,256,128]{2,1,0:T(8,128)(2,1)S(1)}, bf16[2,256,128]{2,1,0:T(8,128)(2,1)S(1)}, u32[]{:S(2)}, u32[]{:S(2)}) collective-permute-start(bf16[2,256,128]{2,1,0:T(8,128)(2,1)S(1)} %get-tuple-element.164), channel_id=1, source_target_pairs={{0,4},{1,5},{2,6},{3,7},{4,0},{5,1},{6,2},{7,3},{8,12},{9,13},{10,... | collective-permute-start | bytes 393224 | tf_op jit(solution)/shard_map/latent1_far/ppermute | solution.py:55
  54.4 4.7 %collective-permute-start.18 = (bf16[256,128]{1,0:T(8,128)(2,1)S(1)}, bf16[256,128]{1,0:T(8,128)(2,1)S(1)}, u32[]{:S(2)}, u32[]{:S(2)}) collective-permute-start(bf16[256,128]{1,0:T(8,128)(2,1)S(1)} %get-tuple-element.170), channel_id=1, source_target_pairs={{0,16},{8,24},{16,0},{24,8},{1,17},{9,25},{17,1},{25,9},{2,18},{10... | collective-permute-start | bytes 196616 | tf_op jit(solution)/shard_map/latent0_last/ppermute | solution.py:55
  55.0 7.0 %collective-permute-start.13 = (bf16[4,256,128]{2,1,0:T(8,128)(2,1)S(1)}, bf16[4,256,128]{2,1,0:T(8,128)(2,1)S(1)}, u32[]{:S(2)}, u32[]{:S(2)}) collective-permute-start(bf16[4,256,128]{2,1,0:T(8,128)(2,1)S(1)} %latent_grad0_join.1.near.refs_0_), channel_id=1, source_target_pairs={{0,1},{1,0},{2,3},{3,2},{4,5},{5,4},{6,7},{7,6},{8,9},{9,8},{10,11... | collective-permute-start | bytes 786440 | tf_op jit(solution)/shard_map/latent_grad0_join/ppermute | solution.py:55
  57.1 10.2 %collective-permute-start.16 = (bf16[4,256,128]{2,1,0:T(8,128)(2,1)S(1)}, bf16[4,256,128]{2,1,0:T(8,128)(2,1)S(1)}, u32[]{:S(2)}, u32[]{:S(2)}) collective-permute-start(bf16[4,256,128]{2,1,0:T(8,128)(2,1)S(1)} %latent_grad1_join.1.near.refs_2_), channel_id=1, source_target_pairs={{0,1},{1,0},{2,3},{3,2},{4,5},{5,4},{6,7},{7,6},{8,9},{9,8},{10,11... | collective-permute-start | bytes 786440 | tf_op jit(solution)/shard_map/latent_grad1_join/ppermute | solution.py:55
  59.6 5.0 %collective-permute-start.20 = (bf16[2,256,128]{2,1,0:T(8,128)(2,1)S(1)}, bf16[2,256,128]{2,1,0:T(8,128)(2,1)S(1)}, u32[]{:S(2)}, u32[]{:S(2)}) collective-permute-start(bf16[2,256,128]{2,1,0:T(8,128)(2,1)S(1)} %latent0_stack.1.mine), channel_id=1, source_target_pairs={{0,2},{1,3},{2,0},{3,1},{4,6},{5,7},{6,4},{7,5},{8,10},{9,11},{10,... | collective-permute-start | bytes 393224 | tf_op jit(solution)/shard_map/latent0_stack/ppermute | solution.py:55
  61.1 4.3 %collective-permute-start.19 = (bf16[256,128]{1,0:T(8,128)(2,1)S(1)}, bf16[256,128]{1,0:T(8,128)(2,1)S(1)}, u32[]{:S(2)}, u32[]{:S(2)}) collective-permute-start(bf16[256,128]{1,0:T(8,128)(2,1)S(1)} %get-tuple-element.178), channel_id=1, source_target_pairs={{0,16},{8,24},{16,0},{24,8},{1,17},{9,25},{17,1},{25,9},{2,18},{10... | collective-permute-start | bytes 196616 | tf_op jit(solution)/shard_map/latent1_last/ppermute | solution.py:55
  61.8 12.3 %collective-permute-start.30 = (bf16[512,512]{1,0:T(8,128)(2,1)S(1)}, bf16[512,512]{1,0:T(8,128)(2,1)S(1)}, u32[]{:S(2)}, u32[]{:S(2)}) collective-permute-start(bf16[512,512]{1,0:T(8,128)(2,1)S(1)} %get-tuple-element.231), channel_id=1, source_target_pairs={{0,8},{8,0},{16,24},{24,16},{1,9},{9,1},{17,25},{25,17},{2,10},{10... | collective-permute-start | bytes 1572872 | tf_op jit(solution)/shard_map/core_far/ppermute | solution.py:55
  62.5 9.1 %collective-permute-start.23 = (bf16[2,2,256,128]{3,2,1,0:T(8,128)(2,1)S(1)}, bf16[2,2,256,128]{3,2,1,0:T(8,128)(2,1)S(1)}, u32[]{:S(2)}, u32[]{:S(2)}) collective-permute-start(bf16[2,2,256,128]{3,2,1,0:T(8,128)(2,1)S(1)} %latent_grad0_halves.1), channel_id=1, source_target_pairs={{0,8},{8,0},{16,24},{24,16},{1,9},{9,1},{17,25},{25,17},{2,10},{10... | collective-permute-start | bytes 786440 | tf_op jit(solution)/shard_map/latent_grad0_halves/ppermute | solution.py:55
  66.0 5.0 %collective-permute-start.22 = (bf16[2,256,128]{2,1,0:T(8,128)(2,1)S(1)}, bf16[2,256,128]{2,1,0:T(8,128)(2,1)S(1)}, u32[]{:S(2)}, u32[]{:S(2)}) collective-permute-start(bf16[2,256,128]{2,1,0:T(8,128)(2,1)S(1)} %latent1_stack.1.mine), channel_id=1, source_target_pairs={{0,2},{1,3},{2,0},{3,1},{4,6},{5,7},{6,4},{7,5},{8,10},{9,11},{10,... | collective-permute-start | bytes 393224 | tf_op jit(solution)/shard_map/latent1_stack/ppermute | solution.py:55
  67.3 10.6 %collective-permute-start.29 = (bf16[512,512]{1,0:T(8,128)(2,1)S(1)}, bf16[512,512]{1,0:T(8,128)(2,1)S(1)}, u32[]{:S(2)}, u32[]{:S(2)}) collective-permute-start(bf16[512,512]{1,0:T(8,128)(2,1)S(1)} %get-tuple-element.232), channel_id=1, source_target_pairs={{0,8},{8,0},{16,24},{24,16},{1,9},{9,1},{17,25},{25,17},{2,10},{10... | collective-permute-start | bytes 1572872 | tf_op jit(solution)/shard_map/core_far/ppermute | solution.py:55
  67.3 11.1 %collective-permute-start.28 = (bf16[512,512]{1,0:T(8,128)(2,1)S(1)}, bf16[512,512]{1,0:T(8,128)(2,1)S(1)}, u32[]{:S(2)}, u32[]{:S(2)}) collective-permute-start(bf16[512,512]{1,0:T(8,128)(2,1)S(1)} %get-tuple-element.233), channel_id=1, source_target_pairs={{0,8},{8,0},{16,24},{24,16},{1,9},{9,1},{17,25},{25,17},{2,10},{10... | collective-permute-start | bytes 1572872 | tf_op jit(solution)/shard_map/core_far/ppermute | solution.py:55
  71.0 11.9 %collective-permute-start.27 = (bf16[512,512]{1,0:T(8,128)(2,1)S(1)}, bf16[512,512]{1,0:T(8,128)(2,1)S(1)}, u32[]{:S(2)}, u32[]{:S(2)}) collective-permute-start(bf16[512,512]{1,0:T(8,128)(2,1)S(1)} %get-tuple-element.234), channel_id=1, source_target_pairs={{0,8},{8,0},{16,24},{24,16},{1,9},{9,1},{17,25},{25,17},{2,10},{10... | collective-permute-start | bytes 1572872 | tf_op jit(solution)/shard_map/core_far/ppermute | solution.py:55
  71.6 4.7 %collective-permute-start.21 = (bf16[2,2,256,128]{3,2,1,0:T(8,128)(2,1)S(1)}, bf16[2,2,256,128]{3,2,1,0:T(8,128)(2,1)S(1)}, u32[]{:S(2)}, u32[]{:S(2)}) collective-permute-start(bf16[2,2,256,128]{3,2,1,0:T(8,128)(2,1)S(1)} %latent_grad1_halves.1), channel_id=1, source_target_pairs={{0,8},{8,0},{16,24},{24,16},{1,9},{9,1},{17,25},{25,17},{2,10},{10... | collective-permute-start | bytes 786440 | tf_op jit(solution)/shard_map/latent_grad1_halves/ppermute | solution.py:55
  74.2 11.6 %collective-permute-start.31 = (bf16[2,512,128]{2,1,0:T(8,128)(2,1)S(1)}, bf16[2,512,128]{2,1,0:T(8,128)(2,1)S(1)}, u32[]{:S(2)}, u32[]{:S(2)}) collective-permute-start(bf16[2,512,128]{2,1,0:T(8,128)(2,1)S(1)} %latent0_join.1.refs_0_), channel_id=1, source_target_pairs={{0,1},{1,0},{2,3},{3,2},{4,5},{5,4},{6,7},{7,6},{8,9},{9,8},{10,11... | collective-permute-start | bytes 786440 | tf_op jit(solution)/shard_map/latent0_join/ppermute | solution.py:55
  76.3 12.1 %collective-permute-start.32 = (bf16[2,512,128]{2,1,0:T(8,128)(2,1)S(1)}, bf16[2,512,128]{2,1,0:T(8,128)(2,1)S(1)}, u32[]{:S(2)}, u32[]{:S(2)}) collective-permute-start(bf16[2,512,128]{2,1,0:T(8,128)(2,1)S(1)} %latent1_join.1.refs_1_), channel_id=1, source_target_pairs={{0,1},{1,0},{2,3},{3,2},{4,5},{5,4},{6,7},{7,6},{8,9},{9,8},{10,11... | collective-permute-start | bytes 786440 | tf_op jit(solution)/shard_map/latent1_join/ppermute | solution.py:55
  77.8 5.1 %copy-start.1 = (bf16[512,2048]{1,0:T(8,128)(2,1)S(1)}, bf16[512,2048]{1,0:T(8,128)(2,1)}, u32[]{:S(2)}) copy-start(bf16[512,2048]{1,0:T(8,128)(2,1)} %refs_2_.1) | copy-start | bytes 6291460
  77.8 14.5 %collective-permute-start.25 = (bf16[128,1024]{1,0:T(8,128)(2,1)S(1)}, bf16[128,1024]{1,0:T(8,128)(2,1)S(1)}, u32[]{:S(2)}, u32[]{:S(2)}) collective-permute-start(bf16[128,1024]{1,0:T(8,128)(2,1)S(1)} %get-tuple-element.202), channel_id=1, source_target_pairs={{0,16},{8,24},{16,0},{24,8},{1,17},{9,25},{17,1},{25,9},{2,18},{10... | collective-permute-start | bytes 786440 | tf_op jit(solution)/shard_map/latent_grad1_left/ppermute | solution.py:55
  78.3 14.0 %collective-permute-start.24 = (bf16[128,1024]{1,0:T(8,128)(2,1)S(1)}, bf16[128,1024]{1,0:T(8,128)(2,1)S(1)}, u32[]{:S(2)}, u32[]{:S(2)}) collective-permute-start(bf16[128,1024]{1,0:T(8,128)(2,1)S(1)} %get-tuple-element.193), channel_id=1, source_target_pairs={{0,16},{8,24},{16,0},{24,8},{1,17},{9,25},{17,1},{25,9},{2,18},{10... | collective-permute-start | bytes 786440 | tf_op jit(solution)/shard_map/latent_grad0_left/ppermute | solution.py:55

commit v4 on v3

--- a/solution.py
+++ b/solution.py
@@ -12,10 +12,10 @@
 NAMES = {"G": "latent_grad", "L": "latent", "x": "far", "c": "core"}
 PIECES = 4
 ORDER = (
-    "own", "acts", "far", "G1S", "G0S", "GK", "LS", "@own", "LK", "G0near", "G1near", "G0far",
-    "L0near", "G1far", "L1near", "L0far", "G0last", "@G1", "G1last", "L1far", "G0join",
-    "L0last", "G1join", "L0stack", "L1last", "G0halves", "L0join", "og", "L1stack", "G1halves",
-    "G0left", "L1join", "G1left", "input", "Lrn", "Lrf", "final",
+    "own", "acts", "far", "G0S", "G1S", "GK", "LS", "@own", "LK", "G0near", "G1near", "G0far",
+    "L0near", "G1far", "L1near", "G0last", "L0far", "G1last", "L1far", "G0join", "L0last",
+    "G1join", "L0stack", "L1last", "G0halves", "L0join", "og", "L1stack", "G1halves", "G0left",
+    "L1join", "G1left", "input", "Lrn", "Lrf", "final",
 )
 HALVES = {"G": (True, True), "L": (True, True)}
 BF16 = jnp.bfloat16
@@ -62,8 +62,11 @@
 class InOrder:
     def __init__(self):
         self.last = ()
+        self.free = False
 
     def __call__(self, step, *values):
+        if self.free:
+            return step(*values)
         values, _ = lax.optimization_barrier((values, self.last))
         result = step(*values)
         self.last = result
@@ -615,6 +618,8 @@
         "stack": stack,
     }
     for entry in ORDER:
+        run.free = entry[0] == "~"
+        entry = entry.lstrip("~")
         if entry == "GK":
             grad_keep()
         elif entry == "LS":

time: 94.1 us -> 90.3 us (0.960)
  waiting for transfers between devices: 21.3 us -> 17.3 us
    ppermute x33, waiting for transfers between devices: 21.3 us -> 17.3 us  [swap(): return lax.ppermute(value, axis, [(i, i ^ mask) for i in range(size)])]
  transfers between devices with their start and end apart: 33 -> 33, of which waited for: 9 -> 9; matrix products, arithmetic and copies ran while one was open for 0% -> 0% of each run, Pallas kernels for 34% -> 36%
where the time goes in v4:
time: 90.3 us; the launch traced here: 90 us
  starting transfers between devices  34 us (38%)
  Pallas kernels  33.6 us (37%)
  waiting for transfers between devices  17.3 us (19%)
  local copies, waits for them, and re-layouts  4.04 us (4%)
  between operations  1.06 us (1%)
    ppermute x33, starting transfers between devices, swap(): return lax.ppermute(value, axis, [(i, i ^ mask) for i in range(size)])  34 us
    ppermute x33, waiting for transfers between devices, swap(): return lax.ppermute(value, axis, [(i, i ^ mask) for i in range(size)])  17.3 us
    pallas_call x23, Pallas kernels, whole_call(): pl.pallas_call(kernel, out_shape=[jax.ShapeDtypeStruct(s, t) for s, t in...  17.2 us
    pallas_call x3, Pallas kernels, written_call(): pl.pallas_call(kernel, out_shape=jax.ShapeDtypeStruct(shape, dtype), in_s...  8.41 us
    pallas_call x5, Pallas kernels, products(): pl.pallas_call(functools.partial(product_kernel, chunks), out_shape=[jax....  7.99 us
    unnamed x10, local copies, waits for them, and re-layouts  3.8 us
  transfers between devices with their start and end apart: 33, of which 9 were waited for; matrix products, arithmetic and copies ran while one was open for 0% of the time, Pallas kernels for 36%

profile of v4, /device:TPU:0, one launch (start us, length us, event | category | flops | bytes accessed | tf_op | source)
XLA Modules:
  0.0 90.0 jit_solution(4366797187897236106)
XLA Ops:
  1.1 2.6 %collective-permute-start.26 = (bf16[512,2048]{1,0:T(8,128)(2,1)}, bf16[512,2048]{1,0:T(8,128)(2,1)S(1)}, u32[]{:S(2)}, u32[]{:S(2)}) collective-permute-start(bf16[512,2048]{1,0:T(8,128)(2,1)} %refs_2_.1), channel_id=1, source_target_pairs={{0,16},{8,24},{16,0},{24,8},{1,17},{9,25},{17,1},{25,9},{2,18},{10... | collective-permute-start | bytes 6291464 | tf_op jit(solution)/shard_map/far_og/ppermute | solution.py:55
  4.0 1.6 %copy-done = bf16[512,2048]{1,0:T(8,128)(2,1)S(1)} copy-done((bf16[512,2048]{1,0:T(8,128)(2,1)S(1)}, bf16[512,2048]{1,0:T(8,128)(2,1)}, u32[]{:S(2)}) %copy-start) | copy-done | bytes 2097176
  5.6 2.2 %copy-done.2 = bf16[1024,2048]{1,0:T(8,128)(2,1)S(1)} copy-done((bf16[1024,2048]{1,0:T(8,128)(2,1)S(1)}, bf16[1024,2048]{1,0:T(8,128)(2,1)}, u32[]{:S(2)}) %copy-start.2) | copy-done | bytes 4194328
  7.7 1.7 %latent_grad0_S.1 = bf16[4,256,128]{2,1,0:T(8,128)(2,1)S(1)} custom-call(s32[5]{0:T(128)S(1)} %stack.23.where, bf16[512,2048]{1,0:T(8,128)(2,1)S(1)} %copy-done, bf16[4,2,128,2048]{3,2,1,0:T(8,128)(2,1)S(1)} %bitcast.7), custom_call_target="tpu_custom_call" | custom-call | flops 536870912 | bytes 4194304 | tf_op jit(solution)/shard_map/latent_grad0_S/pallas_call | solution.py:100
  9.4 1.6 %collective-permute-start = (bf16[4,256,128]{2,1,0:T(8,128)(2,1)S(1)}, bf16[4,256,128]{2,1,0:T(8,128)(2,1)S(1)}, u32[]{:S(2)}, u32[]{:S(2)}) collective-permute-start(bf16[4,256,128]{2,1,0:T(8,128)(2,1)S(1)} %latent_grad0_S.1), channel_id=1, source_target_pairs={{0,1},{1,0},{2,3},{3,2},{4,5},{5,4},{6,7},{7,6},{8,9},{9,8},{10,11... | collective-permute-start | bytes 786440 | tf_op jit(solution)/shard_map/latent_grad0_S/ppermute | solution.py:55
  11.0 1.7 %latent_grad1_S.1 = bf16[4,256,128]{2,1,0:T(8,128)(2,1)S(1)} custom-call(s32[5]{0:T(128)S(1)} %stack.23.where, bf16[512,2048]{1,0:T(8,128)(2,1)S(1)} %copy-done, bf16[4,2,128,2048]{3,2,1,0:T(8,128)(2,1)S(1)} %bitcast.8), custom_call_target="tpu_custom_call" | custom-call | flops 536870912 | bytes 4194304 | tf_op jit(solution)/shard_map/latent_grad1_S/pallas_call | solution.py:100
  12.7 0.6 collective-permute-start.4
  13.3 2.1 %latent_grad_K.1 = (f32[4,256,128]{2,1,0:T(8,128)S(1)}, f32[4,256,128]{2,1,0:T(8,128)S(1)}) custom-call(s32[5]{0:T(128)S(1)} %stack.23.where, bf16[512,2048]{1,0:T(8,128)(2,1)S(1)} %copy-done, bf16[4,2,128,2048]{3,2,1,0:T(8,128)(2,1)S(1)} %bitcast.9), custom_call_target="tpu_custom_call" | custom-call | flops 1073741824 | bytes 6291456 | tf_op jit(solution)/shard_map/latent_grad_K/pallas_call | solution.py:100
  15.4 1.3 %latent_S.1 = (bf16[2,512,128]{2,1,0:T(8,128)(2,1)S(1)}, bf16[2,512,128]{2,1,0:T(8,128)(2,1)S(1)}) custom-call(s32[5]{0:T(128)S(1)} %stack.23.where, bf16[512,1024]{1,0:T(8,128)(2,1)S(1)} %copy-done.4, bf16[512,1024]{1,0:T(8,128)(2,1)S(1)} %collective-permute-done.1.refs_1_.acts_other, bf16[2,2,2,128,1024]{4,3,2,1,0:T(8,128)(2,1)S(1)} %bitcast.10), custom_call_target="tpu_custom_call" | custom-call | flops 536870912 | bytes 3145728 | tf_op jit(solution)/shard_map/latent_S/pallas_call | solution.py:100
  16.7 1.6 %collective-permute-start.8 = (bf16[2,512,128]{2,1,0:T(8,128)(2,1)S(1)}, bf16[2,512,128]{2,1,0:T(8,128)(2,1)S(1)}, u32[]{:S(2)}, u32[]{:S(2)}) collective-permute-start(bf16[2,512,128]{2,1,0:T(8,128)(2,1)S(1)} %get-tuple-element.123), channel_id=1, source_target_pairs={{0,1},{1,0},{2,3},{3,2},{4,5},{5,4},{6,7},{7,6},{8,9},{9,8},{10,11... | collective-permute-start | bytes 786440 | tf_op jit(solution)/shard_map/latent_S/ppermute | solution.py:55
  18.8 1.3 %latent_K.1 = (f32[2,512,128]{2,1,0:T(8,128)S(1)}, f32[2,512,128]{2,1,0:T(8,128)S(1)}) custom-call(s32[5]{0:T(128)S(1)} %stack.23.where, bf16[512,1024]{1,0:T(8,128)(2,1)S(1)} %copy-done.4, bf16[512,1024]{1,0:T(8,128)(2,1)S(1)} %collective-permute-done.1.refs_1_.acts_other, bf16[2,2,2,128,1024]{4,3,2,1,0:T(8,128)(2,1)S(1)} %bitcast.11), custom_call_target="tpu_custom_call" | custom-call | flops 536870912 | bytes 3145728 | tf_op jit(solution)/shard_map/latent_K/pallas_call | solution.py:100
  20.1 0.6 latent_grad0_near.1
  20.7 1.6 %collective-permute-start.3 = (bf16[4,128,128]{2,1,0:T(8,128)(2,1)S(1)}, bf16[4,128,128]{2,1,0:T(8,128)(2,1)S(1)}, u32[]{:S(2)}, u32[]{:S(2)}) collective-permute-start(bf16[4,128,128]{2,1,0:T(8,128)(2,1)S(1)} %get-tuple-element.132), channel_id=1, source_target_pairs={{0,2},{1,3},{2,0},{3,1},{4,6},{5,7},{6,4},{7,5},{8,10},{9,11},{10,... | collective-permute-start | bytes 393224 | tf_op jit(solution)/shard_map/latent_grad0_near/ppermute | solution.py:55
  22.3 1.9 %collective-permute-done.4.sent = bf16[4,256,128]{2,1,0:T(8,128)(2,1)S(1)} collective-permute-done((bf16[4,256,128]{2,1,0:T(8,128)(2,1)S(1)}, bf16[4,256,128]{2,1,0:T(8,128)(2,1)S(1)}, u32[]{:S(2)}, u32[]{:S(2)}) %collective-permute-start.4) | collective-permute-done | bytes 262176 | tf_op jit(solution)/shard_map/latent_grad1_S/ppermute | solution.py:55
  24.2 0.6 latent_grad1_near.1
  24.8 1.6 %collective-permute-start.7 = (bf16[4,128,128]{2,1,0:T(8,128)(2,1)S(1)}, bf16[4,128,128]{2,1,0:T(8,128)(2,1)S(1)}, u32[]{:S(2)}, u32[]{:S(2)}) collective-permute-start(bf16[4,128,128]{2,1,0:T(8,128)(2,1)S(1)} %get-tuple-element.136), channel_id=1, source_target_pairs={{0,2},{1,3},{2,0},{3,1},{4,6},{5,7},{6,4},{7,5},{8,10},{9,11},{10,... | collective-permute-start | bytes 393224 | tf_op jit(solution)/shard_map/latent_grad1_near/ppermute | solution.py:55
  26.5 0.6 latent_grad0_far.1
  27.1 2.7 %collective-permute-start.5 = (bf16[4,128,128]{2,1,0:T(8,128)(2,1)S(1)}, bf16[4,128,128]{2,1,0:T(8,128)(2,1)S(1)}, u32[]{:S(2)}, u32[]{:S(2)}) collective-permute-start(bf16[4,128,128]{2,1,0:T(8,128)(2,1)S(1)} %get-tuple-element.140), channel_id=1, source_target_pairs={{0,4},{1,5},{2,6},{3,7},{4,0},{5,1},{6,2},{7,3},{8,12},{9,13},{10,... | collective-permute-start | bytes 393224 | tf_op jit(solution)/shard_map/latent_grad0_far/ppermute | solution.py:55
  29.9 0.6 latent0_near.1
  30.5 1.6 %collective-permute-start.12 = (bf16[2,256,128]{2,1,0:T(8,128)(2,1)S(1)}, bf16[2,256,128]{2,1,0:T(8,128)(2,1)S(1)}, u32[]{:S(2)}, u32[]{:S(2)}) collective-permute-start(bf16[2,256,128]{2,1,0:T(8,128)(2,1)S(1)} %get-tuple-element.144), channel_id=1, source_target_pairs={{0,2},{1,3},{2,0},{3,1},{4,6},{5,7},{6,4},{7,5},{8,10},{9,11},{10,... | collective-permute-start | bytes 393224 | tf_op jit(solution)/shard_map/latent0_near/ppermute | solution.py:55
  32.1 0.6 latent_grad1_far.1
  32.7 2.7 %collective-permute-start.11 = (bf16[4,128,128]{2,1,0:T(8,128)(2,1)S(1)}, bf16[4,128,128]{2,1,0:T(8,128)(2,1)S(1)}, u32[]{:S(2)}, u32[]{:S(2)}) collective-permute-start(bf16[4,128,128]{2,1,0:T(8,128)(2,1)S(1)} %get-tuple-element.148), channel_id=1, source_target_pairs={{0,4},{1,5},{2,6},{3,7},{4,0},{5,1},{6,2},{7,3},{8,12},{9,13},{10,... | collective-permute-start | bytes 393224 | tf_op jit(solution)/shard_map/latent_grad1_far/ppermute | solution.py:55
  35.3 0.6 latent1_near.1
  36.0 1.2 %collective-permute-start.10 = (bf16[2,256,128]{2,1,0:T(8,128)(2,1)S(1)}, bf16[2,256,128]{2,1,0:T(8,128)(2,1)S(1)}, u32[]{:S(2)}, u32[]{:S(2)}) collective-permute-start(bf16[2,256,128]{2,1,0:T(8,128)(2,1)S(1)} %get-tuple-element.152), channel_id=1, source_target_pairs={{0,2},{1,3},{2,0},{3,1},{4,6},{5,7},{6,4},{7,5},{8,10},{9,11},{10,... | collective-permute-start | bytes 393224 | tf_op jit(solution)/shard_map/latent1_near/ppermute | solution.py:55
  37.7 0.9 %collective-permute-start.9 = (bf16[4,128,128]{2,1,0:T(8,128)(2,1)S(1)}, bf16[4,128,128]{2,1,0:T(8,128)(2,1)S(1)}, u32[]{:S(2)}, u32[]{:S(2)}) collective-permute-start(bf16[4,128,128]{2,1,0:T(8,128)(2,1)S(1)} %latent_grad0_last.1.mine), channel_id=1, source_target_pairs={{0,2},{1,3},{2,0},{3,1},{4,6},{5,7},{6,4},{7,5},{8,10},{9,11},{10,... | collective-permute-start | bytes 393224 | tf_op jit(solution)/shard_map/latent_grad0_last/ppermute | solution.py:55
  39.3 2.2 %collective-permute-start.15 = (bf16[2,256,128]{2,1,0:T(8,128)(2,1)S(1)}, bf16[2,256,128]{2,1,0:T(8,128)(2,1)S(1)}, u32[]{:S(2)}, u32[]{:S(2)}) collective-permute-start(bf16[2,256,128]{2,1,0:T(8,128)(2,1)S(1)} %get-tuple-element.158), channel_id=1, source_target_pairs={{0,4},{1,5},{2,6},{3,7},{4,0},{5,1},{6,2},{7,3},{8,12},{9,13},{10,... | collective-permute-start | bytes 393224 | tf_op jit(solution)/shard_map/latent0_far/ppermute | solution.py:55
  42.1 1.6 %collective-permute-start.14 = (bf16[4,128,128]{2,1,0:T(8,128)(2,1)S(1)}, bf16[4,128,128]{2,1,0:T(8,128)(2,1)S(1)}, u32[]{:S(2)}, u32[]{:S(2)}) collective-permute-start(bf16[4,128,128]{2,1,0:T(8,128)(2,1)S(1)} %latent_grad1_last.1.mine), channel_id=1, source_target_pairs={{0,2},{1,3},{2,0},{3,1},{4,6},{5,7},{6,4},{7,5},{8,10},{9,11},{10,... | collective-permute-start | bytes 393224 | tf_op jit(solution)/shard_map/latent_grad1_last/ppermute | solution.py:55
  43.7 2.3 %collective-permute-done.10.other = bf16[2,256,128]{2,1,0:T(8,128)(2,1)S(1)} collective-permute-done((bf16[2,256,128]{2,1,0:T(8,128)(2,1)S(1)}, bf16[2,256,128]{2,1,0:T(8,128)(2,1)S(1)}, u32[]{:S(2)}, u32[]{:S(2)}) %collective-permute-start.10) | collective-permute-done | bytes 131104 | tf_op jit(solution)/shard_map/latent1_near/ppermute | solution.py:55
  46.6 3.6 %collective-permute-done.9.other = bf16[4,128,128]{2,1,0:T(8,128)(2,1)S(1)} collective-permute-done((bf16[4,128,128]{2,1,0:T(8,128)(2,1)S(1)}, bf16[4,128,128]{2,1,0:T(8,128)(2,1)S(1)}, u32[]{:S(2)}, u32[]{:S(2)}) %collective-permute-start.9) | collective-permute-done | bytes 131104 | tf_op jit(solution)/shard_map/latent_grad0_last/ppermute | solution.py:55
  50.8 0.6 latent0_last.1
  51.4 0.6 collective-permute-start.18
  52.0 1.5 %collective-permute-start.13 = (bf16[4,256,128]{2,1,0:T(8,128)(2,1)S(1)}, bf16[4,256,128]{2,1,0:T(8,128)(2,1)S(1)}, u32[]{:S(2)}, u32[]{:S(2)}) collective-permute-start(bf16[4,256,128]{2,1,0:T(8,128)(2,1)S(1)} %latent_grad0_join.1.near.refs_0_), channel_id=1, source_target_pairs={{0,1},{1,0},{2,3},{3,2},{4,5},{5,4},{6,7},{7,6},{8,9},{9,8},{10,11... | collective-permute-start | bytes 786440 | tf_op jit(solution)/shard_map/latent_grad0_join/ppermute | solution.py:55
  54.6 1.1 %collective-permute-done.18.refs_1_ = bf16[256,128]{1,0:T(8,128)(2,1)S(1)} collective-permute-done((bf16[256,128]{1,0:T(8,128)(2,1)S(1)}, bf16[256,128]{1,0:T(8,128)(2,1)S(1)}, u32[]{:S(2)}, u32[]{:S(2)}) %collective-permute-start.18) | collective-permute-done | bytes 65568 | tf_op jit(solution)/shard_map/latent0_last/ppermute | solution.py:55
  56.9 0.6 collective-permute-start.19
  57.8 1.8 %collective-permute-done.13.far.refs_1_ = bf16[4,256,128]{2,1,0:T(8,128)(2,1)S(1)} collective-permute-done((bf16[4,256,128]{2,1,0:T(8,128)(2,1)S(1)}, bf16[4,256,128]{2,1,0:T(8,128)(2,1)S(1)}, u32[]{:S(2)}, u32[]{:S(2)}) %collective-permute-start.13) | collective-permute-done | bytes 262176 | tf_op jit(solution)/shard_map/latent_grad0_join/ppermute | solution.py:55
  60.2 1.0 %collective-permute-done.20.other = bf16[2,256,128]{2,1,0:T(8,128)(2,1)S(1)} collective-permute-done((bf16[2,256,128]{2,1,0:T(8,128)(2,1)S(1)}, bf16[2,256,128]{2,1,0:T(8,128)(2,1)S(1)}, u32[]{:S(2)}, u32[]{:S(2)}) %collective-permute-start.20) | collective-permute-done | bytes 131104 | tf_op jit(solution)/shard_map/latent0_stack/ppermute | solution.py:55
  62.4 1.5 %collective-permute-start.22 = (bf16[2,256,128]{2,1,0:T(8,128)(2,1)S(1)}, bf16[2,256,128]{2,1,0:T(8,128)(2,1)S(1)}, u32[]{:S(2)}, u32[]{:S(2)}) collective-permute-start(bf16[2,256,128]{2,1,0:T(8,128)(2,1)S(1)} %latent1_stack.1.mine), channel_id=1, source_target_pairs={{0,2},{1,3},{2,0},{3,1},{4,6},{5,7},{6,4},{7,5},{8,10},{9,11},{10,... | collective-permute-start | bytes 393224 | tf_op jit(solution)/shard_map/latent1_stack/ppermute | solution.py:55
  64.4 3.1 %collective-permute-done.22.other = bf16[2,256,128]{2,1,0:T(8,128)(2,1)S(1)} collective-permute-done((bf16[2,256,128]{2,1,0:T(8,128)(2,1)S(1)}, bf16[2,256,128]{2,1,0:T(8,128)(2,1)S(1)}, u32[]{:S(2)}, u32[]{:S(2)}) %collective-permute-start.22) | collective-permute-done | bytes 131104 | tf_op jit(solution)/shard_map/latent1_stack/ppermute | solution.py:55
  68.6 1.4 %latent_grad0_left.1 = (f32[128,1024]{1,0:T(8,128)S(1)}, bf16[128,1024]{1,0:T(8,128)(2,1)S(1)}) custom-call(s32[5]{0:T(128)S(1)} %stack.23.where, bf16[4,256,128]{2,1,0:T(8,128)(2,1)S(1)} %latent_grad0_join.1.near.refs_0_, bf16[4,256,128]{2,1,0:T(8,128)(2,1)S(1)} %collective-permute-done.13.far.refs_1_, ...), custom_call_target="tpu_custom_call" | custom-call | flops 536870912 | bytes 3670016 | tf_op jit(solution)/shard_map/latent_grad0_left/pallas_call | solution.py:41
  70.6 1.6 %collective-permute-start.31 = (bf16[2,512,128]{2,1,0:T(8,128)(2,1)S(1)}, bf16[2,512,128]{2,1,0:T(8,128)(2,1)S(1)}, u32[]{:S(2)}, u32[]{:S(2)}) collective-permute-start(bf16[2,512,128]{2,1,0:T(8,128)(2,1)S(1)} %latent0_join.1.refs_0_), channel_id=1, source_target_pairs={{0,1},{1,0},{2,3},{3,2},{4,5},{5,4},{6,7},{7,6},{8,9},{9,8},{10,11... | collective-permute-start | bytes 786440 | tf_op jit(solution)/shard_map/latent0_join/ppermute | solution.py:55
  72.7 1.4 %latent_grad1_left.1 = (f32[128,1024]{1,0:T(8,128)S(1)}, bf16[128,1024]{1,0:T(8,128)(2,1)S(1)}) custom-call(s32[5]{0:T(128)S(1)} %stack.23.where, bf16[4,256,128]{2,1,0:T(8,128)(2,1)S(1)} %latent_grad1_join.1.near.refs_2_, bf16[4,256,128]{2,1,0:T(8,128)(2,1)S(1)} %collective-permute-done.16.far.refs_3_, ...), custom_call_target="tpu_custom_call" | custom-call | flops 536870912 | bytes 3670016 | tf_op jit(solution)/shard_map/latent_grad1_left/pallas_call | solution.py:41
  74.2 1.1 %collective-permute-start.25 = (bf16[128,1024]{1,0:T(8,128)(2,1)S(1)}, bf16[128,1024]{1,0:T(8,128)(2,1)S(1)}, u32[]{:S(2)}, u32[]{:S(2)}) collective-permute-start(bf16[128,1024]{1,0:T(8,128)(2,1)S(1)} %get-tuple-element.202), channel_id=1, source_target_pairs={{0,16},{8,24},{16,0},{24,8},{1,17},{9,25},{17,1},{25,9},{2,18},{10... | collective-permute-start | bytes 786440 | tf_op jit(solution)/shard_map/latent_grad1_left/ppermute | solution.py:55
  75.3 1.0 %collective-permute-start.24 = (bf16[128,1024]{1,0:T(8,128)(2,1)S(1)}, bf16[128,1024]{1,0:T(8,128)(2,1)S(1)}, u32[]{:S(2)}, u32[]{:S(2)}) collective-permute-start(bf16[128,1024]{1,0:T(8,128)(2,1)S(1)} %get-tuple-element.193), channel_id=1, source_target_pairs={{0,16},{8,24},{16,0},{24,8},{1,17},{9,25},{17,1},{25,9},{2,18},{10... | collective-permute-start | bytes 786440 | tf_op jit(solution)/shard_map/latent_grad0_left/ppermute | solution.py:55
  76.3 2.9 %latent_grad_input.1 = bf16[512,1024]{1,0:T(8,128)(2,1)} custom-call(s32[5]{0:T(128)S(1)} %stack.23.where, bf16[4,256,128]{2,1,0:T(8,128)(2,1)S(1)} %latent_grad0_join.1.near.refs_0_, bf16[4,256,128]{2,1,0:T(8,128)(2,1)S(1)} %collective-permute-done.13.far.refs_1_, bf16[4,256,128]{2,1,0:T(8,128)(2,1)S(1)} %latent_grad1_join.1.near.refs_2_, ...), custom_call_target="tpu_custom_call" | custom-call | flops 1073741824 | bytes 3145728 | tf_op jit(solution)/shard_map/latent_grad_input/pallas_call | solution.py:246
  79.2 2.9 %latent_rn.1.refs_9_ = f32[256,2048]{1,0:T(8,128)S(1)} custom-call(s32[5]{0:T(128)S(1)} %stack.23.where, bf16[2,512,128]{2,1,0:T(8,128)(2,1)S(1)} %latent0_join.1.refs_0_, bf16[2,512,128]{2,1,0:T(8,128)(2,1)S(1)} %latent1_join.1.refs_1_, bf16[512,2048]{1,0:T(8,128)(2,1)S(1)} %copy-done.1, bf16[512,2048]{1,0:T(8,128)(2,1)} %collective-permute-done.2.refs_3_, ...), custom_call_target="tpu_custom_call" | custom-call | flops 1073741824 | bytes 11010048 | tf_op jit(solution)/shard_map/latent_rn/pallas_call | solution.py:41
  82.2 2.4 %collective-permute-done.32.refs_1_ = bf16[2,512,128]{2,1,0:T(8,128)(2,1)S(1)} collective-permute-done((bf16[2,512,128]{2,1,0:T(8,128)(2,1)S(1)}, bf16[2,512,128]{2,1,0:T(8,128)(2,1)S(1)}, u32[]{:S(2)}, u32[]{:S(2)}) %collective-permute-start.32) | collective-permute-done | bytes 262176 | tf_op jit(solution)/shard_map/latent1_join/ppermute | solution.py:55
  84.5 3.9 %latent_rf.1 = f32[256,2048]{1,0:T(8,128)} custom-call(s32[5]{0:T(128)S(1)} %stack.23.where, bf16[2,512,128]{2,1,0:T(8,128)(2,1)S(1)} %collective-permute-done.31.refs_0_, bf16[2,512,128]{2,1,0:T(8,128)(2,1)S(1)} %collective-permute-done.32.refs_1_, bf16[512,2048]{1,0:T(8,128)(2,1)S(1)} %copy-done.1, bf16[512,2048]{1,0:T(8,128)(2,1)} %collective-permute-done.2.refs_3_, ...), custom_call_target="tpu_custom_call" | custom-call | flops 1073741824 | bytes 11010048 | tf_op jit(solution)/shard_map/latent_rf/pallas_call | solution.py:246
  88.4 1.6 %latent_grad_final.1 = f32[256,1024]{1,0:T(8,128)} custom-call(s32[5]{0:T(128)S(1)} %stack.23.where, f32[128,1024]{1,0:T(8,128)S(1)} %get-tuple-element.227.refs_0_, bf16[128,1024]{1,0:T(8,128)(2,1)S(1)} %collective-permute-done.24.refs_1_, f32[128,1024]{1,0:T(8,128)S(1)} %get-tuple-element.229.refs_2_, bf16[128,1024]{1,0:T(8,128)(2,1)S(1)} %collective-permute-done.25.refs_3_), custom_call_target="tpu_custom_call" | custom-call | bytes 1572864 | tf_op jit(solution)/shard_map/latent_grad_final/pallas_call | solution.py:246
  (61 shorter events, 11.4 us)
Async XLA Ops:
  0.6 17.7 %collective-permute-start.2 = (bf16[512,2048]{1,0:T(8,128)(2,1)}, bf16[512,2048]{1,0:T(8,128)(2,1)}, u32[]{:S(2)}, u32[]{:S(2)}) collective-permute-start(bf16[512,2048]{1,0:T(8,128)(2,1)} %refs_2_.1), channel_id=1, source_target_pairs={{0,8},{8,0},{16,24},{24,16},{1,9},{9,1},{17,25},{25,17},{2,10},{10... | collective-permute-start | bytes 6291464 | tf_op jit(solution)/shard_map/core_own/ppermute | solution.py:55
  1.1 56.4 %collective-permute-start.26 = (bf16[512,2048]{1,0:T(8,128)(2,1)}, bf16[512,2048]{1,0:T(8,128)(2,1)S(1)}, u32[]{:S(2)}, u32[]{:S(2)}) collective-permute-start(bf16[512,2048]{1,0:T(8,128)(2,1)} %refs_2_.1), channel_id=1, source_target_pairs={{0,16},{8,24},{16,0},{24,8},{1,17},{9,25},{17,1},{25,9},{2,18},{10... | collective-permute-start | bytes 6291464 | tf_op jit(solution)/shard_map/far_og/ppermute | solution.py:55
  3.7 11.7 %collective-permute-start.1 = (bf16[512,1024]{1,0:T(8,128)(2,1)}, bf16[512,1024]{1,0:T(8,128)(2,1)S(1)}, u32[]{:S(2)}, u32[]{:S(2)}) collective-permute-start(bf16[512,1024]{1,0:T(8,128)(2,1)} %acts.1), channel_id=1, source_target_pairs={{0,8},{8,0},{16,24},{24,16},{1,9},{9,1},{17,25},{25,17},{2,10},{10... | collective-permute-start | bytes 3145736 | tf_op jit(solution)/shard_map/core_acts/ppermute | solution.py:55
  4.0 1.6 %copy-start = (bf16[512,2048]{1,0:T(8,128)(2,1)S(1)}, bf16[512,2048]{1,0:T(8,128)(2,1)}, u32[]{:S(2)}) copy-start(bf16[512,2048]{1,0:T(8,128)(2,1)} %refs_2_.1) | copy-start | bytes 6291460
  5.6 2.2 %copy-start.2 = (bf16[1024,2048]{1,0:T(8,128)(2,1)S(1)}, bf16[1024,2048]{1,0:T(8,128)(2,1)}, u32[]{:S(2)}) copy-start(bf16[1024,2048]{1,0:T(8,128)(2,1)} %param.6) | copy-start | bytes 12582916
  9.4 10.6 %collective-permute-start = (bf16[4,256,128]{2,1,0:T(8,128)(2,1)S(1)}, bf16[4,256,128]{2,1,0:T(8,128)(2,1)S(1)}, u32[]{:S(2)}, u32[]{:S(2)}) collective-permute-start(bf16[4,256,128]{2,1,0:T(8,128)(2,1)S(1)} %latent_grad0_S.1), channel_id=1, source_target_pairs={{0,1},{1,0},{2,3},{3,2},{4,5},{5,4},{6,7},{7,6},{8,9},{9,8},{10,11... | collective-permute-start | bytes 786440 | tf_op jit(solution)/shard_map/latent_grad0_S/ppermute | solution.py:55
  12.7 2.7 %copy-start.3 = (bf16[1024,1024]{1,0:T(8,128)(2,1)S(1)}, bf16[1024,1024]{1,0:T(8,128)(2,1)}, u32[]{:S(2)}) copy-start(bf16[1024,1024]{1,0:T(8,128)(2,1)} %refs_4_) | copy-start | bytes 6291460
  12.7 2.7 %copy-start.4 = (bf16[512,1024]{1,0:T(8,128)(2,1)S(1)}, bf16[512,1024]{1,0:T(8,128)(2,1)}, u32[]{:S(2)}) copy-start(bf16[512,1024]{1,0:T(8,128)(2,1)} %acts.1) | copy-start | bytes 3145732
  12.7 11.5 %collective-permute-start.4 = (bf16[4,256,128]{2,1,0:T(8,128)(2,1)S(1)}, bf16[4,256,128]{2,1,0:T(8,128)(2,1)S(1)}, u32[]{:S(2)}, u32[]{:S(2)}) collective-permute-start(bf16[4,256,128]{2,1,0:T(8,128)(2,1)S(1)} %latent_grad1_S.1), channel_id=1, source_target_pairs={{0,1},{1,0},{2,3},{3,2},{4,5},{5,4},{6,7},{7,6},{8,9},{9,8},{10,11... | collective-permute-start | bytes 786440 | tf_op jit(solution)/shard_map/latent_grad1_S/ppermute | solution.py:55
  16.7 13.2 %collective-permute-start.8 = (bf16[2,512,128]{2,1,0:T(8,128)(2,1)S(1)}, bf16[2,512,128]{2,1,0:T(8,128)(2,1)S(1)}, u32[]{:S(2)}, u32[]{:S(2)}) collective-permute-start(bf16[2,512,128]{2,1,0:T(8,128)(2,1)S(1)} %get-tuple-element.123), channel_id=1, source_target_pairs={{0,1},{1,0},{2,3},{3,2},{4,5},{5,4},{6,7},{7,6},{8,9},{9,8},{10,11... | collective-permute-start | bytes 786440 | tf_op jit(solution)/shard_map/latent_S/ppermute | solution.py:55
  18.3 17.1 %collective-permute-start.6 = (bf16[2,512,128]{2,1,0:T(8,128)(2,1)S(1)}, bf16[2,512,128]{2,1,0:T(8,128)(2,1)S(1)}, u32[]{:S(2)}, u32[]{:S(2)}) collective-permute-start(bf16[2,512,128]{2,1,0:T(8,128)(2,1)S(1)} %get-tuple-element.124), channel_id=1, source_target_pairs={{0,1},{1,0},{2,3},{3,2},{4,5},{5,4},{6,7},{7,6},{8,9},{9,8},{10,11... | collective-permute-start | bytes 786440 | tf_op jit(solution)/shard_map/latent_S/ppermute | solution.py:55
  20.7 5.8 %collective-permute-start.3 = (bf16[4,128,128]{2,1,0:T(8,128)(2,1)S(1)}, bf16[4,128,128]{2,1,0:T(8,128)(2,1)S(1)}, u32[]{:S(2)}, u32[]{:S(2)}) collective-permute-start(bf16[4,128,128]{2,1,0:T(8,128)(2,1)S(1)} %get-tuple-element.132), channel_id=1, source_target_pairs={{0,2},{1,3},{2,0},{3,1},{4,6},{5,7},{6,4},{7,5},{8,10},{9,11},{10,... | collective-permute-start | bytes 393224 | tf_op jit(solution)/shard_map/latent_grad0_near/ppermute | solution.py:55
  24.8 7.3 %collective-permute-start.7 = (bf16[4,128,128]{2,1,0:T(8,128)(2,1)S(1)}, bf16[4,128,128]{2,1,0:T(8,128)(2,1)S(1)}, u32[]{:S(2)}, u32[]{:S(2)}) collective-permute-start(bf16[4,128,128]{2,1,0:T(8,128)(2,1)S(1)} %get-tuple-element.136), channel_id=1, source_target_pairs={{0,2},{1,3},{2,0},{3,1},{4,6},{5,7},{6,4},{7,5},{8,10},{9,11},{10,... | collective-permute-start | bytes 393224 | tf_op jit(solution)/shard_map/latent_grad1_near/ppermute | solution.py:55
  27.1 10.1 %collective-permute-start.5 = (bf16[4,128,128]{2,1,0:T(8,128)(2,1)S(1)}, bf16[4,128,128]{2,1,0:T(8,128)(2,1)S(1)}, u32[]{:S(2)}, u32[]{:S(2)}) collective-permute-start(bf16[4,128,128]{2,1,0:T(8,128)(2,1)S(1)} %get-tuple-element.140), channel_id=1, source_target_pairs={{0,4},{1,5},{2,6},{3,7},{4,0},{5,1},{6,2},{7,3},{8,12},{9,13},{10,... | collective-permute-start | bytes 393224 | tf_op jit(solution)/shard_map/latent_grad0_far/ppermute | solution.py:55
  30.5 8.2 %collective-permute-start.12 = (bf16[2,256,128]{2,1,0:T(8,128)(2,1)S(1)}, bf16[2,256,128]{2,1,0:T(8,128)(2,1)S(1)}, u32[]{:S(2)}, u32[]{:S(2)}) collective-permute-start(bf16[2,256,128]{2,1,0:T(8,128)(2,1)S(1)} %get-tuple-element.144), channel_id=1, source_target_pairs={{0,2},{1,3},{2,0},{3,1},{4,6},{5,7},{6,4},{7,5},{8,10},{9,11},{10,... | collective-permute-start | bytes 393224 | tf_op jit(solution)/shard_map/latent0_near/ppermute | solution.py:55
  32.7 8.8 %collective-permute-start.11 = (bf16[4,128,128]{2,1,0:T(8,128)(2,1)S(1)}, bf16[4,128,128]{2,1,0:T(8,128)(2,1)S(1)}, u32[]{:S(2)}, u32[]{:S(2)}) collective-permute-start(bf16[4,128,128]{2,1,0:T(8,128)(2,1)S(1)} %get-tuple-element.148), channel_id=1, source_target_pairs={{0,4},{1,5},{2,6},{3,7},{4,0},{5,1},{6,2},{7,3},{8,12},{9,13},{10,... | collective-permute-start | bytes 393224 | tf_op jit(solution)/shard_map/latent_grad1_far/ppermute | solution.py:55
  36.0 10.0 %collective-permute-start.10 = (bf16[2,256,128]{2,1,0:T(8,128)(2,1)S(1)}, bf16[2,256,128]{2,1,0:T(8,128)(2,1)S(1)}, u32[]{:S(2)}, u32[]{:S(2)}) collective-permute-start(bf16[2,256,128]{2,1,0:T(8,128)(2,1)S(1)} %get-tuple-element.152), channel_id=1, source_target_pairs={{0,2},{1,3},{2,0},{3,1},{4,6},{5,7},{6,4},{7,5},{8,10},{9,11},{10,... | collective-permute-start | bytes 393224 | tf_op jit(solution)/shard_map/latent1_near/ppermute | solution.py:55
  37.7 12.5 %collective-permute-start.9 = (bf16[4,128,128]{2,1,0:T(8,128)(2,1)S(1)}, bf16[4,128,128]{2,1,0:T(8,128)(2,1)S(1)}, u32[]{:S(2)}, u32[]{:S(2)}) collective-permute-start(bf16[4,128,128]{2,1,0:T(8,128)(2,1)S(1)} %latent_grad0_last.1.mine), channel_id=1, source_target_pairs={{0,2},{1,3},{2,0},{3,1},{4,6},{5,7},{6,4},{7,5},{8,10},{9,11},{10,... | collective-permute-start | bytes 393224 | tf_op jit(solution)/shard_map/latent_grad0_last/ppermute | solution.py:55
  39.3 11.5 %collective-permute-start.15 = (bf16[2,256,128]{2,1,0:T(8,128)(2,1)S(1)}, bf16[2,256,128]{2,1,0:T(8,128)(2,1)S(1)}, u32[]{:S(2)}, u32[]{:S(2)}) collective-permute-start(bf16[2,256,128]{2,1,0:T(8,128)(2,1)S(1)} %get-tuple-element.158), channel_id=1, source_target_pairs={{0,4},{1,5},{2,6},{3,7},{4,0},{5,1},{6,2},{7,3},{8,12},{9,13},{10,... | collective-permute-start | bytes 393224 | tf_op jit(solution)/shard_map/latent0_far/ppermute | solution.py:55
  42.1 11.4 %collective-permute-start.14 = (bf16[4,128,128]{2,1,0:T(8,128)(2,1)S(1)}, bf16[4,128,128]{2,1,0:T(8,128)(2,1)S(1)}, u32[]{:S(2)}, u32[]{:S(2)}) collective-permute-start(bf16[4,128,128]{2,1,0:T(8,128)(2,1)S(1)} %latent_grad1_last.1.mine), channel_id=1, source_target_pairs={{0,2},{1,3},{2,0},{3,1},{4,6},{5,7},{6,4},{7,5},{8,10},{9,11},{10,... | collective-permute-start | bytes 393224 | tf_op jit(solution)/shard_map/latent_grad1_last/ppermute | solution.py:55
  46.6 9.8 %collective-permute-start.17 = (bf16[2,256,128]{2,1,0:T(8,128)(2,1)S(1)}, bf16[2,256,128]{2,1,0:T(8,128)(2,1)S(1)}, u32[]{:S(2)}, u32[]{:S(2)}) collective-permute-start(bf16[2,256,128]{2,1,0:T(8,128)(2,1)S(1)} %get-tuple-element.164), channel_id=1, source_target_pairs={{0,4},{1,5},{2,6},{3,7},{4,0},{5,1},{6,2},{7,3},{8,12},{9,13},{10,... | collective-permute-start | bytes 393224 | tf_op jit(solution)/shard_map/latent1_far/ppermute | solution.py:55
  51.4 4.3 %collective-permute-start.18 = (bf16[256,128]{1,0:T(8,128)(2,1)S(1)}, bf16[256,128]{1,0:T(8,128)(2,1)S(1)}, u32[]{:S(2)}, u32[]{:S(2)}) collective-permute-start(bf16[256,128]{1,0:T(8,128)(2,1)S(1)} %get-tuple-element.170), channel_id=1, source_target_pairs={{0,16},{8,24},{16,0},{24,8},{1,17},{9,25},{17,1},{25,9},{2,18},{10... | collective-permute-start | bytes 196616 | tf_op jit(solution)/shard_map/latent0_last/ppermute | solution.py:55
  52.0 7.6 %collective-permute-start.13 = (bf16[4,256,128]{2,1,0:T(8,128)(2,1)S(1)}, bf16[4,256,128]{2,1,0:T(8,128)(2,1)S(1)}, u32[]{:S(2)}, u32[]{:S(2)}) collective-permute-start(bf16[4,256,128]{2,1,0:T(8,128)(2,1)S(1)} %latent_grad0_join.1.near.refs_0_), channel_id=1, source_target_pairs={{0,1},{1,0},{2,3},{3,2},{4,5},{5,4},{6,7},{7,6},{8,9},{9,8},{10,11... | collective-permute-start | bytes 786440 | tf_op jit(solution)/shard_map/latent_grad0_join/ppermute | solution.py:55
  54.1 9.8 %collective-permute-start.16 = (bf16[4,256,128]{2,1,0:T(8,128)(2,1)S(1)}, bf16[4,256,128]{2,1,0:T(8,128)(2,1)S(1)}, u32[]{:S(2)}, u32[]{:S(2)}) collective-permute-start(bf16[4,256,128]{2,1,0:T(8,128)(2,1)S(1)} %latent_grad1_join.1.near.refs_2_), channel_id=1, source_target_pairs={{0,1},{1,0},{2,3},{3,2},{4,5},{5,4},{6,7},{7,6},{8,9},{9,8},{10,11... | collective-permute-start | bytes 786440 | tf_op jit(solution)/shard_map/latent_grad1_join/ppermute | solution.py:55
  56.2 5.0 %collective-permute-start.20 = (bf16[2,256,128]{2,1,0:T(8,128)(2,1)S(1)}, bf16[2,256,128]{2,1,0:T(8,128)(2,1)S(1)}, u32[]{:S(2)}, u32[]{:S(2)}) collective-permute-start(bf16[2,256,128]{2,1,0:T(8,128)(2,1)S(1)} %latent0_stack.1.mine), channel_id=1, source_target_pairs={{0,2},{1,3},{2,0},{3,1},{4,6},{5,7},{6,4},{7,5},{8,10},{9,11},{10,... | collective-permute-start | bytes 393224 | tf_op jit(solution)/shard_map/latent0_stack/ppermute | solution.py:55
  56.9 4.9 %collective-permute-start.19 = (bf16[256,128]{1,0:T(8,128)(2,1)S(1)}, bf16[256,128]{1,0:T(8,128)(2,1)S(1)}, u32[]{:S(2)}, u32[]{:S(2)}) collective-permute-start(bf16[256,128]{1,0:T(8,128)(2,1)S(1)} %get-tuple-element.178), channel_id=1, source_target_pairs={{0,16},{8,24},{16,0},{24,8},{1,17},{9,25},{17,1},{25,9},{2,18},{10... | collective-permute-start | bytes 196616 | tf_op jit(solution)/shard_map/latent1_last/ppermute | solution.py:55
  57.7 12.9 %collective-permute-start.30 = (bf16[512,512]{1,0:T(8,128)(2,1)S(1)}, bf16[512,512]{1,0:T(8,128)(2,1)S(1)}, u32[]{:S(2)}, u32[]{:S(2)}) collective-permute-start(bf16[512,512]{1,0:T(8,128)(2,1)S(1)} %get-tuple-element.231), channel_id=1, source_target_pairs={{0,8},{8,0},{16,24},{24,16},{1,9},{9,1},{17,25},{25,17},{2,10},{10... | collective-permute-start | bytes 1572872 | tf_op jit(solution)/shard_map/core_far/ppermute | solution.py:55
  60.2 7.9 %collective-permute-start.23 = (bf16[2,2,256,128]{3,2,1,0:T(8,128)(2,1)S(1)}, bf16[2,2,256,128]{3,2,1,0:T(8,128)(2,1)S(1)}, u32[]{:S(2)}, u32[]{:S(2)}) collective-permute-start(bf16[2,2,256,128]{3,2,1,0:T(8,128)(2,1)S(1)} %latent_grad0_halves.1), channel_id=1, source_target_pairs={{0,8},{8,0},{16,24},{24,16},{1,9},{9,1},{17,25},{25,17},{2,10},{10... | collective-permute-start | bytes 786440 | tf_op jit(solution)/shard_map/latent_grad0_halves/ppermute | solution.py:55
  62.4 5.0 %collective-permute-start.22 = (bf16[2,256,128]{2,1,0:T(8,128)(2,1)S(1)}, bf16[2,256,128]{2,1,0:T(8,128)(2,1)S(1)}, u32[]{:S(2)}, u32[]{:S(2)}) collective-permute-start(bf16[2,256,128]{2,1,0:T(8,128)(2,1)S(1)} %latent1_stack.1.mine), channel_id=1, source_target_pairs={{0,2},{1,3},{2,0},{3,1},{4,6},{5,7},{6,4},{7,5},{8,10},{9,11},{10,... | collective-permute-start | bytes 393224 | tf_op jit(solution)/shard_map/latent1_stack/ppermute | solution.py:55
  63.9 10.3 %collective-permute-start.29 = (bf16[512,512]{1,0:T(8,128)(2,1)S(1)}, bf16[512,512]{1,0:T(8,128)(2,1)S(1)}, u32[]{:S(2)}, u32[]{:S(2)}) collective-permute-start(bf16[512,512]{1,0:T(8,128)(2,1)S(1)} %get-tuple-element.232), channel_id=1, source_target_pairs={{0,8},{8,0},{16,24},{24,16},{1,9},{9,1},{17,25},{25,17},{2,10},{10... | collective-permute-start | bytes 1572872 | tf_op jit(solution)/shard_map/core_far/ppermute | solution.py:55
  63.9 11.4 %collective-permute-start.28 = (bf16[512,512]{1,0:T(8,128)(2,1)S(1)}, bf16[512,512]{1,0:T(8,128)(2,1)S(1)}, u32[]{:S(2)}, u32[]{:S(2)}) collective-permute-start(bf16[512,512]{1,0:T(8,128)(2,1)S(1)} %get-tuple-element.233), channel_id=1, source_target_pairs={{0,8},{8,0},{16,24},{24,16},{1,9},{9,1},{17,25},{25,17},{2,10},{10... | collective-permute-start | bytes 1572872 | tf_op jit(solution)/shard_map/core_far/ppermute | solution.py:55
  67.5 11.8 %collective-permute-start.27 = (bf16[512,512]{1,0:T(8,128)(2,1)S(1)}, bf16[512,512]{1,0:T(8,128)(2,1)S(1)}, u32[]{:S(2)}, u32[]{:S(2)}) collective-permute-start(bf16[512,512]{1,0:T(8,128)(2,1)S(1)} %get-tuple-element.234), channel_id=1, source_target_pairs={{0,8},{8,0},{16,24},{24,16},{1,9},{9,1},{17,25},{25,17},{2,10},{10... | collective-permute-start | bytes 1572872 | tf_op jit(solution)/shard_map/core_far/ppermute | solution.py:55
  68.0 4.2 %collective-permute-start.21 = (bf16[2,2,256,128]{3,2,1,0:T(8,128)(2,1)S(1)}, bf16[2,2,256,128]{3,2,1,0:T(8,128)(2,1)S(1)}, u32[]{:S(2)}, u32[]{:S(2)}) collective-permute-start(bf16[2,2,256,128]{3,2,1,0:T(8,128)(2,1)S(1)} %latent_grad1_halves.1), channel_id=1, source_target_pairs={{0,8},{8,0},{16,24},{24,16},{1,9},{9,1},{17,25},{25,17},{2,10},{10... | collective-permute-start | bytes 786440 | tf_op jit(solution)/shard_map/latent_grad1_halves/ppermute | solution.py:55
  70.6 11.5 %collective-permute-start.31 = (bf16[2,512,128]{2,1,0:T(8,128)(2,1)S(1)}, bf16[2,512,128]{2,1,0:T(8,128)(2,1)S(1)}, u32[]{:S(2)}, u32[]{:S(2)}) collective-permute-start(bf16[2,512,128]{2,1,0:T(8,128)(2,1)S(1)} %latent0_join.1.refs_0_), channel_id=1, source_target_pairs={{0,1},{1,0},{2,3},{3,2},{4,5},{5,4},{6,7},{7,6},{8,9},{9,8},{10,11... | collective-permute-start | bytes 786440 | tf_op jit(solution)/shard_map/latent0_join/ppermute | solution.py:55
  72.2 12.3 %collective-permute-start.32 = (bf16[2,512,128]{2,1,0:T(8,128)(2,1)S(1)}, bf16[2,512,128]{2,1,0:T(8,128)(2,1)S(1)}, u32[]{:S(2)}, u32[]{:S(2)}) collective-permute-start(bf16[2,512,128]{2,1,0:T(8,128)(2,1)S(1)} %latent1_join.1.refs_1_), channel_id=1, source_target_pairs={{0,1},{1,0},{2,3},{3,2},{4,5},{5,4},{6,7},{7,6},{8,9},{9,8},{10,11... | collective-permute-start | bytes 786440 | tf_op jit(solution)/shard_map/latent1_join/ppermute | solution.py:55
  74.1 5.1 %copy-start.1 = (bf16[512,2048]{1,0:T(8,128)(2,1)S(1)}, bf16[512,2048]{1,0:T(8,128)(2,1)}, u32[]{:S(2)}) copy-start(bf16[512,2048]{1,0:T(8,128)(2,1)} %refs_2_.1) | copy-start | bytes 6291460
  74.2 14.3 %collective-permute-start.25 = (bf16[128,1024]{1,0:T(8,128)(2,1)S(1)}, bf16[128,1024]{1,0:T(8,128)(2,1)S(1)}, u32[]{:S(2)}, u32[]{:S(2)}) collective-permute-start(bf16[128,1024]{1,0:T(8,128)(2,1)S(1)} %get-tuple-element.202), channel_id=1, source_target_pairs={{0,16},{8,24},{16,0},{24,8},{1,17},{9,25},{17,1},{25,9},{2,18},{10... | collective-permute-start | bytes 786440 | tf_op jit(solution)/shard_map/latent_grad1_left/ppermute | solution.py:55
  75.3 13.2 %collective-permute-start.24 = (bf16[128,1024]{1,0:T(8,128)(2,1)S(1)}, bf16[128,1024]{1,0:T(8,128)(2,1)S(1)}, u32[]{:S(2)}, u32[]{:S(2)}) collective-permute-start(bf16[128,1024]{1,0:T(8,128)(2,1)S(1)} %get-tuple-element.193), channel_id=1, source_target_pairs={{0,16},{8,24},{16,0},{24,8},{1,17},{9,25},{17,1},{25,9},{2,18},{10... | collective-permute-start | bytes 786440 | tf_op jit(solution)/shard_map/latent_grad0_left/ppermute | solution.py:55

commit v5 on v4

--- a/solution.py
+++ b/solution.py
@@ -12,7 +12,7 @@
 NAMES = {"G": "latent_grad", "L": "latent", "x": "far", "c": "core"}
 PIECES = 4
 ORDER = (
-    "own", "acts", "far", "G0S", "G1S", "GK", "LS", "@own", "LK", "G0near", "G1near", "G0far",
+    "own", "far", "G0S", "acts", "G1S", "GK", "LS", "@own", "LK", "G0near", "G1near", "G0far",
     "L0near", "G1far", "L1near", "G0last", "L0far", "G1last", "L1far", "G0join", "L0last",
     "G1join", "L0stack", "L1last", "G0halves", "L0join", "og", "L1stack", "G1halves", "G0left",
     "L1join", "G1left", "input", "Lrn", "Lrf", "final",
@@ -73,47 +73,42 @@
         return result
 
 
-def product_kernel(chunks, where, *refs):
-    values, factor, outs = refs[:-chunks - 1], refs[-chunks - 1], refs[-chunks:]
-    count, width = outs[0].shape[0], outs[0].shape[2]
-    flat = factor[...].reshape(count * chunks * width, factor.shape[-1])
-    rows = values[0].shape[0]
-    for i, value in enumerate(values):
-        result = dot(value[...], flat, COLS)
-        for j in range(count):
-            for c in range(chunks):
-                lane = (j * chunks + c) * width
-                part = result[:, lane : lane + width]
-                outs[c][j, i * rows : (i + 1) * rows, :] = part.astype(outs[c].dtype)
-
-
-def products(where, which, values, factor, block, place, dtype, batch, chunks, limit):
+def product_kernel(bit, which, first, by_core, where, *refs):
+    factor = next(i for i, ref in enumerate(refs) if ref.ndim > 2)
+    values, factor, outs = refs[:factor], refs[factor], refs[factor + 1 :]
+    count, half, width = outs[0].shape
+    half //= len(values)
+    low = where[bit] if which else 1 - where[bit]
+    span = pl.ds(pl.multiple_of(low * half, half), half)
+    chunks = slice(first, first + len(outs))
+    group = 2 if len(outs) == 1 and count % 2 == 0 else 1
+    for j in range(0, count, group):
+        blocks = []
+        for k in range(j, j + group):
+            block = factor[k, where[2], chunks] if by_core else factor[k, chunks]
+            blocks.append(block.reshape(len(outs) * width, block.shape[-1]))
+        flat = jnp.concatenate(blocks) if group > 1 else blocks[0]
+        for i, value in enumerate(values):
+            result = dot(value[span, :], flat, COLS)
+            for k in range(group):
+                for c, out in enumerate(outs):
+                    lane = (k * len(outs) + c) * width
+                    part = result[:, lane : lane + width]
+                    out[j + k, i * half : (i + 1) * half, :] = part.astype(out.dtype)
+
+
+def products(where, bit, which, values, factor, dtype, first, chunks, by_core):
     rows, depth = values[0].shape
-    half = rows // 2
-    width = block[-2]
-    count = math.prod(block[:-3])
-    total = half * len(values)
-
-    def half_of(i, where):
-        return (where[0] if which else 1 - where[0], 0)
-
-    return pl.pallas_call(
-        functools.partial(product_kernel, chunks),
-        out_shape=[jax.ShapeDtypeStruct((count, total, width), dtype)] * chunks,
-        grid_spec=pltpu.PrefetchScalarGridSpec(
-            num_scalar_prefetch=1,
-            grid=(count // batch,),
-            in_specs=[pl.BlockSpec((half, depth), half_of)] * len(values)
-            + [pl.BlockSpec((batch,) + block[1:], place)],
-            out_specs=[pl.BlockSpec((batch, total, width), lambda i, where: (i, 0, 0))] * chunks,
-        ),
-        compiler_params=pltpu.CompilerParams(vmem_limit_bytes=limit * MIB),
-        cost_estimate=cost(
-            2 * total * depth * count * chunks * width,
-            *values,
-            ((count, chunks, width, depth), BF16),
-        ),
-    )(where, *values, factor)
+    count, width = factor.shape[0], factor.shape[-2]
+    total = rows // 2 * len(values)
+    return whole_call(
+        functools.partial(product_kernel, bit, which, first, by_core),
+        where,
+        [*values, factor],
+        [((count, total, width), dtype)] * chunks,
+        (),
+        2 * total * depth * count * chunks * width,
+    )
 
 
 def split_kernel(where, kept, sent, mine, away):
@@ -367,7 +362,7 @@
 def right_far(where, scale, parts, grads, done):
     owners, rows, width = parts[0].shape
     columns = grads[0].shape[1]
-    blocks = max(columns // 256, PIECES)
+    blocks = max(columns // 512, PIECES)
     return written_call(
         functools.partial(right_far_kernel, blocks, scale),
         where,
@@ -419,35 +414,14 @@
     left_blocks = left_factor.reshape(owners, 2, CHUNKS, step, depth)
     right_blocks = right_factor.reshape(groups, CHUNKS, step, out_grad.shape[1])
 
-    features = out_grad.shape[1]
-
-    def grad_product(which, dtype, first, chunks, limit):
-        return lambda *values: products(
-            where,
-            which,
-            values,
-            right_blocks,
-            (groups, chunks, step, features),
-            lambda i, where: (i, first, 0, 0),
-            dtype,
-            2,
-            chunks,
-            limit,
-        )
+
+    def grad_product(which, dtype, first, chunks):
+        bit = 0
+        return lambda v, f: products(where, bit, which, [v], f, dtype, first, chunks, False)
 
     def latent_product(which, dtype):
-        return lambda *values: products(
-            where,
-            which,
-            values,
-            left_blocks,
-            (owners, 1, CHUNKS, step, depth),
-            lambda i, where: (i, where[2], 0, 0, 0),
-            dtype,
-            owners,
-            CHUNKS,
-            24,
-        )
+        bit = 0
+        return lambda a, b, f: products(where, bit, which, [a, b], f, dtype, 0, CHUNKS, True)
 
     def halve(which, c):
         return 2 if HALVES[which][c] and peers > 1 else 1
@@ -465,22 +439,22 @@
 
     def grad_send(c):
         with scoped("G", c, "S"):
-            (away,) = run(grad_product(0, BF16, c, 1, 24), out_grad)
+            (away,) = run(grad_product(0, BF16, c, 1), out_grad, right_blocks)
             comes["G", c] = latest["G", c] = swap(away, "tensor", 1)
 
     def grad_keep():
         with scoped("G", "", "K"):
-            for c, value in enumerate(run(grad_product(1, F32, 0, CHUNKS, 24), out_grad)):
+            for c, value in enumerate(run(grad_product(1, F32, 0, CHUNKS), out_grad, right_blocks)):
                 kept["G", c] = value
 
     def latent_send():
         with scoped("L", "", "S"):
-            for c, value in enumerate(run(latent_product(0, BF16), *acts)):
+            for c, value in enumerate(run(latent_product(0, BF16), *acts, left_blocks)):
                 comes["L", c] = latest["L", c] = swap(value, "tensor", 1)
 
     def latent_keep():
         with scoped("L", "", "K"):
-            for c, value in enumerate(run(latent_product(1, F32), *acts)):
+            for c, value in enumerate(run(latent_product(1, F32), *acts, left_blocks)):
                 kept["L", c] = value
 
     def near_sum(name, c):

time: 90.3 us -> 89.8 us (level)
  Pallas kernels: 33.6 us -> 32.5 us
    pallas_call x5 -> x0, Pallas kernels: 7.99 us -> none  [products(): pl.pallas_call(functools.partial(product_kernel, chunks), out_shape=[jax....]
    pallas_call x23 -> x28, Pallas kernels: 17.2 us -> 24.2 us  [whole_call(): pl.pallas_call(kernel, out_shape=[jax.ShapeDtypeStruct(s, t) for s, t in...]
  transfers between devices with their start and end apart: 33 -> 33, of which waited for: 9 -> 9; matrix products, arithmetic and copies ran while one was open for 0% -> 0% of each run, Pallas kernels for 36% -> 35%
where the time goes in v5:
time: 89.8 us; the launch traced here: 89.5 us
  starting transfers between devices  34 us (38%)
  Pallas kernels  32.5 us (36%)
  waiting for transfers between devices  17.9 us (20%)
  local copies, waits for them, and re-layouts  4.03 us (4%)
  between operations  1.06 us (1%)
    ppermute x33, starting transfers between devices, swap(): return lax.ppermute(value, axis, [(i, i ^ mask) for i in range(size)])  34 us
    pallas_call x28, Pallas kernels, whole_call(): pl.pallas_call(kernel, out_shape=[jax.ShapeDtypeStruct(s, t) for s, t in...  24.2 us
    ppermute x33, waiting for transfers between devices, swap(): return lax.ppermute(value, axis, [(i, i ^ mask) for i in range(size)])  17.9 us
    pallas_call x3, Pallas kernels, written_call(): pl.pallas_call(kernel, out_shape=jax.ShapeDtypeStruct(shape, dtype), in_s...  8.31 us
    unnamed x10, local copies, waits for them, and re-layouts  3.79 us
  transfers between devices with their start and end apart: 33, of which 9 were waited for; matrix products, arithmetic and copies ran while one was open for 0% of the time, Pallas kernels for 35%

profile of v5, /device:TPU:0, one launch (start us, length us, event | category | flops | bytes accessed | tf_op | source)
XLA Modules:
  0.0 89.5 jit_solution(8263405513588344986)
XLA Ops:
  1.1 2.6 %collective-permute-start.26 = (bf16[512,2048]{1,0:T(8,128)(2,1)}, bf16[512,2048]{1,0:T(8,128)(2,1)S(1)}, u32[]{:S(2)}, u32[]{:S(2)}) collective-permute-start(bf16[512,2048]{1,0:T(8,128)(2,1)} %refs_2_.1), channel_id=1, source_target_pairs={{0,16},{8,24},{16,0},{24,8},{1,17},{9,25},{17,1},{25,9},{2,18},{10... | collective-permute-start | bytes 6291464 | tf_op jit(solution)/shard_map/far_og/ppermute | solution.py:55
  3.8 1.6 %copy-done = bf16[512,2048]{1,0:T(8,128)(2,1)S(1)} copy-done((bf16[512,2048]{1,0:T(8,128)(2,1)S(1)}, bf16[512,2048]{1,0:T(8,128)(2,1)}, u32[]{:S(2)}) %copy-start) | copy-done | bytes 2097176
  5.4 2.2 %copy-done.2 = bf16[1024,2048]{1,0:T(8,128)(2,1)S(1)} copy-done((bf16[1024,2048]{1,0:T(8,128)(2,1)S(1)}, bf16[1024,2048]{1,0:T(8,128)(2,1)}, u32[]{:S(2)}) %copy-start.2) | copy-done | bytes 4194328
  7.6 1.3 %latent_grad0_S.1 = bf16[4,256,128]{2,1,0:T(8,128)(2,1)S(1)} custom-call(s32[5]{0:T(128)S(1)} %stack.23.where, bf16[512,2048]{1,0:T(8,128)(2,1)S(1)} %copy-done, bf16[4,2,128,2048]{3,2,1,0:T(8,128)(2,1)S(1)} %bitcast.7), custom_call_target="tpu_custom_call" | custom-call | flops 536870912 | bytes 6553600 | tf_op jit(solution)/shard_map/latent_grad0_S/pallas_call | solution.py:41
  9.1 1.5 %collective-permute-start = (bf16[4,256,128]{2,1,0:T(8,128)(2,1)S(1)}, bf16[4,256,128]{2,1,0:T(8,128)(2,1)S(1)}, u32[]{:S(2)}, u32[]{:S(2)}) collective-permute-start(bf16[4,256,128]{2,1,0:T(8,128)(2,1)S(1)} %latent_grad0_S.1), channel_id=1, source_target_pairs={{0,1},{1,0},{2,3},{3,2},{4,5},{5,4},{6,7},{7,6},{8,9},{9,8},{10,11... | collective-permute-start | bytes 786440 | tf_op jit(solution)/shard_map/latent_grad0_S/ppermute | solution.py:55
  10.6 1.3 %latent_grad1_S.1 = bf16[4,256,128]{2,1,0:T(8,128)(2,1)S(1)} custom-call(s32[5]{0:T(128)S(1)} %stack.23.where, bf16[512,2048]{1,0:T(8,128)(2,1)S(1)} %copy-done, bf16[4,2,128,2048]{3,2,1,0:T(8,128)(2,1)S(1)} %bitcast.8), custom_call_target="tpu_custom_call" | custom-call | flops 536870912 | bytes 6553600 | tf_op jit(solution)/shard_map/latent_grad1_S/pallas_call | solution.py:41
  12.5 1.8 %latent_grad_K.1 = (f32[4,256,128]{2,1,0:T(8,128)S(1)}, f32[4,256,128]{2,1,0:T(8,128)S(1)}) custom-call(s32[5]{0:T(128)S(1)} %stack.23.where, bf16[512,2048]{1,0:T(8,128)(2,1)S(1)} %copy-done, bf16[4,2,128,2048]{3,2,1,0:T(8,128)(2,1)S(1)} %bitcast.9), custom_call_target="tpu_custom_call" | custom-call | flops 1073741824 | bytes 7340032 | tf_op jit(solution)/shard_map/latent_grad_K/pallas_call | solution.py:41
  14.3 1.3 %latent_S.1 = (bf16[2,512,128]{2,1,0:T(8,128)(2,1)S(1)}, bf16[2,512,128]{2,1,0:T(8,128)(2,1)S(1)}) custom-call(s32[5]{0:T(128)S(1)} %stack.23.where, bf16[512,1024]{1,0:T(8,128)(2,1)S(1)} %copy-done.4, bf16[512,1024]{1,0:T(8,128)(2,1)S(1)} %collective-permute-done.1.refs_1_.acts_other, bf16[2,2,2,128,1024]{4,3,2,1,0:T(8,128)(2,1)S(1)} %bitcast.10), custom_call_target="tpu_custom_call" | custom-call | flops 536870912 | bytes 4718592 | tf_op jit(solution)/shard_map/latent_S/pallas_call | solution.py:41
  15.6 1.6 %collective-permute-start.8 = (bf16[2,512,128]{2,1,0:T(8,128)(2,1)S(1)}, bf16[2,512,128]{2,1,0:T(8,128)(2,1)S(1)}, u32[]{:S(2)}, u32[]{:S(2)}) collective-permute-start(bf16[2,512,128]{2,1,0:T(8,128)(2,1)S(1)} %get-tuple-element.136), channel_id=1, source_target_pairs={{0,1},{1,0},{2,3},{3,2},{4,5},{5,4},{6,7},{7,6},{8,9},{9,8},{10,11... | collective-permute-start | bytes 786440 | tf_op jit(solution)/shard_map/latent_S/ppermute | solution.py:55
  17.7 1.3 %latent_K.1 = (f32[2,512,128]{2,1,0:T(8,128)S(1)}, f32[2,512,128]{2,1,0:T(8,128)S(1)}) custom-call(s32[5]{0:T(128)S(1)} %stack.23.where, bf16[512,1024]{1,0:T(8,128)(2,1)S(1)} %copy-done.4, bf16[512,1024]{1,0:T(8,128)(2,1)S(1)} %collective-permute-done.1.refs_1_.acts_other, bf16[2,2,2,128,1024]{4,3,2,1,0:T(8,128)(2,1)S(1)} %bitcast.11), custom_call_target="tpu_custom_call" | custom-call | flops 536870912 | bytes 5242880 | tf_op jit(solution)/shard_map/latent_K/pallas_call | solution.py:41
  19.0 0.6 latent_grad0_near.1
  19.6 1.6 %collective-permute-start.3 = (bf16[4,128,128]{2,1,0:T(8,128)(2,1)S(1)}, bf16[4,128,128]{2,1,0:T(8,128)(2,1)S(1)}, u32[]{:S(2)}, u32[]{:S(2)}) collective-permute-start(bf16[4,128,128]{2,1,0:T(8,128)(2,1)S(1)} %get-tuple-element.146), channel_id=1, source_target_pairs={{0,2},{1,3},{2,0},{3,1},{4,6},{5,7},{6,4},{7,5},{8,10},{9,11},{10,... | collective-permute-start | bytes 393224 | tf_op jit(solution)/shard_map/latent_grad0_near/ppermute | solution.py:55
  21.3 2.6 %collective-permute-done.4.sent = bf16[4,256,128]{2,1,0:T(8,128)(2,1)S(1)} collective-permute-done((bf16[4,256,128]{2,1,0:T(8,128)(2,1)S(1)}, bf16[4,256,128]{2,1,0:T(8,128)(2,1)S(1)}, u32[]{:S(2)}, u32[]{:S(2)}) %collective-permute-start.4) | collective-permute-done | bytes 262176 | tf_op jit(solution)/shard_map/latent_grad1_S/ppermute | solution.py:55
  23.8 0.6 latent_grad1_near.1
  24.4 1.6 %collective-permute-start.7 = (bf16[4,128,128]{2,1,0:T(8,128)(2,1)S(1)}, bf16[4,128,128]{2,1,0:T(8,128)(2,1)S(1)}, u32[]{:S(2)}, u32[]{:S(2)}) collective-permute-start(bf16[4,128,128]{2,1,0:T(8,128)(2,1)S(1)} %get-tuple-element.150), channel_id=1, source_target_pairs={{0,2},{1,3},{2,0},{3,1},{4,6},{5,7},{6,4},{7,5},{8,10},{9,11},{10,... | collective-permute-start | bytes 393224 | tf_op jit(solution)/shard_map/latent_grad1_near/ppermute | solution.py:55
  26.1 0.6 latent_grad0_far.1
  26.7 2.7 %collective-permute-start.5 = (bf16[4,128,128]{2,1,0:T(8,128)(2,1)S(1)}, bf16[4,128,128]{2,1,0:T(8,128)(2,1)S(1)}, u32[]{:S(2)}, u32[]{:S(2)}) collective-permute-start(bf16[4,128,128]{2,1,0:T(8,128)(2,1)S(1)} %get-tuple-element.154), channel_id=1, source_target_pairs={{0,4},{1,5},{2,6},{3,7},{4,0},{5,1},{6,2},{7,3},{8,12},{9,13},{10,... | collective-permute-start | bytes 393224 | tf_op jit(solution)/shard_map/latent_grad0_far/ppermute | solution.py:55
  29.5 0.6 latent0_near.1
  30.1 1.6 %collective-permute-start.12 = (bf16[2,256,128]{2,1,0:T(8,128)(2,1)S(1)}, bf16[2,256,128]{2,1,0:T(8,128)(2,1)S(1)}, u32[]{:S(2)}, u32[]{:S(2)}) collective-permute-start(bf16[2,256,128]{2,1,0:T(8,128)(2,1)S(1)} %get-tuple-element.158), channel_id=1, source_target_pairs={{0,2},{1,3},{2,0},{3,1},{4,6},{5,7},{6,4},{7,5},{8,10},{9,11},{10,... | collective-permute-start | bytes 393224 | tf_op jit(solution)/shard_map/latent0_near/ppermute | solution.py:55
  31.7 0.6 latent_grad1_far.1
  32.3 2.7 %collective-permute-start.11 = (bf16[4,128,128]{2,1,0:T(8,128)(2,1)S(1)}, bf16[4,128,128]{2,1,0:T(8,128)(2,1)S(1)}, u32[]{:S(2)}, u32[]{:S(2)}) collective-permute-start(bf16[4,128,128]{2,1,0:T(8,128)(2,1)S(1)} %get-tuple-element.162), channel_id=1, source_target_pairs={{0,4},{1,5},{2,6},{3,7},{4,0},{5,1},{6,2},{7,3},{8,12},{9,13},{10,... | collective-permute-start | bytes 393224 | tf_op jit(solution)/shard_map/latent_grad1_far/ppermute | solution.py:55
  34.9 0.6 latent1_near.1
  35.6 1.2 %collective-permute-start.10 = (bf16[2,256,128]{2,1,0:T(8,128)(2,1)S(1)}, bf16[2,256,128]{2,1,0:T(8,128)(2,1)S(1)}, u32[]{:S(2)}, u32[]{:S(2)}) collective-permute-start(bf16[2,256,128]{2,1,0:T(8,128)(2,1)S(1)} %get-tuple-element.166), channel_id=1, source_target_pairs={{0,2},{1,3},{2,0},{3,1},{4,6},{5,7},{6,4},{7,5},{8,10},{9,11},{10,... | collective-permute-start | bytes 393224 | tf_op jit(solution)/shard_map/latent1_near/ppermute | solution.py:55
  37.4 0.9 %collective-permute-start.9 = (bf16[4,128,128]{2,1,0:T(8,128)(2,1)S(1)}, bf16[4,128,128]{2,1,0:T(8,128)(2,1)S(1)}, u32[]{:S(2)}, u32[]{:S(2)}) collective-permute-start(bf16[4,128,128]{2,1,0:T(8,128)(2,1)S(1)} %latent_grad0_last.1.mine), channel_id=1, source_target_pairs={{0,2},{1,3},{2,0},{3,1},{4,6},{5,7},{6,4},{7,5},{8,10},{9,11},{10,... | collective-permute-start | bytes 393224 | tf_op jit(solution)/shard_map/latent_grad0_last/ppermute | solution.py:55
  38.3 0.6 latent0_far.1
  38.9 2.2 %collective-permute-start.15 = (bf16[2,256,128]{2,1,0:T(8,128)(2,1)S(1)}, bf16[2,256,128]{2,1,0:T(8,128)(2,1)S(1)}, u32[]{:S(2)}, u32[]{:S(2)}) collective-permute-start(bf16[2,256,128]{2,1,0:T(8,128)(2,1)S(1)} %get-tuple-element.172), channel_id=1, source_target_pairs={{0,4},{1,5},{2,6},{3,7},{4,0},{5,1},{6,2},{7,3},{8,12},{9,13},{10,... | collective-permute-start | bytes 393224 | tf_op jit(solution)/shard_map/latent0_far/ppermute | solution.py:55
  41.7 1.6 %collective-permute-start.14 = (bf16[4,128,128]{2,1,0:T(8,128)(2,1)S(1)}, bf16[4,128,128]{2,1,0:T(8,128)(2,1)S(1)}, u32[]{:S(2)}, u32[]{:S(2)}) collective-permute-start(bf16[4,128,128]{2,1,0:T(8,128)(2,1)S(1)} %latent_grad1_last.1.mine), channel_id=1, source_target_pairs={{0,2},{1,3},{2,0},{3,1},{4,6},{5,7},{6,4},{7,5},{8,10},{9,11},{10,... | collective-permute-start | bytes 393224 | tf_op jit(solution)/shard_map/latent_grad1_last/ppermute | solution.py:55
  43.3 2.3 %collective-permute-done.10.other = bf16[2,256,128]{2,1,0:T(8,128)(2,1)S(1)} collective-permute-done((bf16[2,256,128]{2,1,0:T(8,128)(2,1)S(1)}, bf16[2,256,128]{2,1,0:T(8,128)(2,1)S(1)}, u32[]{:S(2)}, u32[]{:S(2)}) %collective-permute-start.10) | collective-permute-done | bytes 131104 | tf_op jit(solution)/shard_map/latent1_near/ppermute | solution.py:55
  45.6 0.6 latent1_far.1
  46.2 3.6 %collective-permute-done.9.other = bf16[4,128,128]{2,1,0:T(8,128)(2,1)S(1)} collective-permute-done((bf16[4,128,128]{2,1,0:T(8,128)(2,1)S(1)}, bf16[4,128,128]{2,1,0:T(8,128)(2,1)S(1)}, u32[]{:S(2)}, u32[]{:S(2)}) %collective-permute-start.9) | collective-permute-done | bytes 131104 | tf_op jit(solution)/shard_map/latent_grad0_last/ppermute | solution.py:55
  51.0 0.6 collective-permute-start.18
  51.6 1.5 %collective-permute-start.13 = (bf16[4,256,128]{2,1,0:T(8,128)(2,1)S(1)}, bf16[4,256,128]{2,1,0:T(8,128)(2,1)S(1)}, u32[]{:S(2)}, u32[]{:S(2)}) collective-permute-start(bf16[4,256,128]{2,1,0:T(8,128)(2,1)S(1)} %latent_grad0_join.1.near.refs_0_), channel_id=1, source_target_pairs={{0,1},{1,0},{2,3},{3,2},{4,5},{5,4},{6,7},{7,6},{8,9},{9,8},{10,11... | collective-permute-start | bytes 786440 | tf_op jit(solution)/shard_map/latent_grad0_join/ppermute | solution.py:55
  54.2 1.1 %collective-permute-done.18.refs_1_ = bf16[256,128]{1,0:T(8,128)(2,1)S(1)} collective-permute-done((bf16[256,128]{1,0:T(8,128)(2,1)S(1)}, bf16[256,128]{1,0:T(8,128)(2,1)S(1)}, u32[]{:S(2)}, u32[]{:S(2)}) %collective-permute-start.18) | collective-permute-done | bytes 65568 | tf_op jit(solution)/shard_map/latent0_last/ppermute | solution.py:55
  56.5 0.6 collective-permute-start.19
  57.4 1.8 %collective-permute-done.13.far.refs_1_ = bf16[4,256,128]{2,1,0:T(8,128)(2,1)S(1)} collective-permute-done((bf16[4,256,128]{2,1,0:T(8,128)(2,1)S(1)}, bf16[4,256,128]{2,1,0:T(8,128)(2,1)S(1)}, u32[]{:S(2)}, u32[]{:S(2)}) %collective-permute-start.13) | collective-permute-done | bytes 262176 | tf_op jit(solution)/shard_map/latent_grad0_join/ppermute | solution.py:55
  59.8 1.0 %collective-permute-done.20.other = bf16[2,256,128]{2,1,0:T(8,128)(2,1)S(1)} collective-permute-done((bf16[2,256,128]{2,1,0:T(8,128)(2,1)S(1)}, bf16[2,256,128]{2,1,0:T(8,128)(2,1)S(1)}, u32[]{:S(2)}, u32[]{:S(2)}) %collective-permute-start.20) | collective-permute-done | bytes 131104 | tf_op jit(solution)/shard_map/latent0_stack/ppermute | solution.py:55
  62.0 1.5 %collective-permute-start.22 = (bf16[2,256,128]{2,1,0:T(8,128)(2,1)S(1)}, bf16[2,256,128]{2,1,0:T(8,128)(2,1)S(1)}, u32[]{:S(2)}, u32[]{:S(2)}) collective-permute-start(bf16[2,256,128]{2,1,0:T(8,128)(2,1)S(1)} %latent1_stack.1.mine), channel_id=1, source_target_pairs={{0,2},{1,3},{2,0},{3,1},{4,6},{5,7},{6,4},{7,5},{8,10},{9,11},{10,... | collective-permute-start | bytes 393224 | tf_op jit(solution)/shard_map/latent1_stack/ppermute | solution.py:55
  64.0 3.1 %collective-permute-done.22.other = bf16[2,256,128]{2,1,0:T(8,128)(2,1)S(1)} collective-permute-done((bf16[2,256,128]{2,1,0:T(8,128)(2,1)S(1)}, bf16[2,256,128]{2,1,0:T(8,128)(2,1)S(1)}, u32[]{:S(2)}, u32[]{:S(2)}) %collective-permute-start.22) | collective-permute-done | bytes 131104 | tf_op jit(solution)/shard_map/latent1_stack/ppermute | solution.py:55
  68.2 1.4 %latent_grad0_left.1 = (f32[128,1024]{1,0:T(8,128)S(1)}, bf16[128,1024]{1,0:T(8,128)(2,1)S(1)}) custom-call(s32[5]{0:T(128)S(1)} %stack.23.where, bf16[4,256,128]{2,1,0:T(8,128)(2,1)S(1)} %latent_grad0_join.1.near.refs_0_, bf16[4,256,128]{2,1,0:T(8,128)(2,1)S(1)} %collective-permute-done.13.far.refs_1_, ...), custom_call_target="tpu_custom_call" | custom-call | flops 536870912 | bytes 3670016 | tf_op jit(solution)/shard_map/latent_grad0_left/pallas_call | solution.py:41
  70.2 1.6 %collective-permute-start.31 = (bf16[2,512,128]{2,1,0:T(8,128)(2,1)S(1)}, bf16[2,512,128]{2,1,0:T(8,128)(2,1)S(1)}, u32[]{:S(2)}, u32[]{:S(2)}) collective-permute-start(bf16[2,512,128]{2,1,0:T(8,128)(2,1)S(1)} %latent0_join.1.refs_0_), channel_id=1, source_target_pairs={{0,1},{1,0},{2,3},{3,2},{4,5},{5,4},{6,7},{7,6},{8,9},{9,8},{10,11... | collective-permute-start | bytes 786440 | tf_op jit(solution)/shard_map/latent0_join/ppermute | solution.py:55
  72.3 1.4 %latent_grad1_left.1 = (f32[128,1024]{1,0:T(8,128)S(1)}, bf16[128,1024]{1,0:T(8,128)(2,1)S(1)}) custom-call(s32[5]{0:T(128)S(1)} %stack.23.where, bf16[4,256,128]{2,1,0:T(8,128)(2,1)S(1)} %latent_grad1_join.1.near.refs_2_, bf16[4,256,128]{2,1,0:T(8,128)(2,1)S(1)} %collective-permute-done.16.far.refs_3_, ...), custom_call_target="tpu_custom_call" | custom-call | flops 536870912 | bytes 3670016 | tf_op jit(solution)/shard_map/latent_grad1_left/pallas_call | solution.py:41
  73.8 1.1 %collective-permute-start.25 = (bf16[128,1024]{1,0:T(8,128)(2,1)S(1)}, bf16[128,1024]{1,0:T(8,128)(2,1)S(1)}, u32[]{:S(2)}, u32[]{:S(2)}) collective-permute-start(bf16[128,1024]{1,0:T(8,128)(2,1)S(1)} %get-tuple-element.216), channel_id=1, source_target_pairs={{0,16},{8,24},{16,0},{24,8},{1,17},{9,25},{17,1},{25,9},{2,18},{10... | collective-permute-start | bytes 786440 | tf_op jit(solution)/shard_map/latent_grad1_left/ppermute | solution.py:55
  74.9 1.0 %collective-permute-start.24 = (bf16[128,1024]{1,0:T(8,128)(2,1)S(1)}, bf16[128,1024]{1,0:T(8,128)(2,1)S(1)}, u32[]{:S(2)}, u32[]{:S(2)}) collective-permute-start(bf16[128,1024]{1,0:T(8,128)(2,1)S(1)} %get-tuple-element.207), channel_id=1, source_target_pairs={{0,16},{8,24},{16,0},{24,8},{1,17},{9,25},{17,1},{25,9},{2,18},{10... | collective-permute-start | bytes 786440 | tf_op jit(solution)/shard_map/latent_grad0_left/ppermute | solution.py:55
  75.9 2.9 %latent_grad_input.1 = bf16[512,1024]{1,0:T(8,128)(2,1)} custom-call(s32[5]{0:T(128)S(1)} %stack.23.where, bf16[4,256,128]{2,1,0:T(8,128)(2,1)S(1)} %latent_grad0_join.1.near.refs_0_, bf16[4,256,128]{2,1,0:T(8,128)(2,1)S(1)} %collective-permute-done.13.far.refs_1_, bf16[4,256,128]{2,1,0:T(8,128)(2,1)S(1)} %latent_grad1_join.1.near.refs_2_, ...), custom_call_target="tpu_custom_call" | custom-call | flops 1073741824 | bytes 3145728 | tf_op jit(solution)/shard_map/latent_grad_input/pallas_call | solution.py:241
  78.9 2.9 %latent_rn.1.refs_9_ = f32[256,2048]{1,0:T(8,128)S(1)} custom-call(s32[5]{0:T(128)S(1)} %stack.23.where, bf16[2,512,128]{2,1,0:T(8,128)(2,1)S(1)} %latent0_join.1.refs_0_, bf16[2,512,128]{2,1,0:T(8,128)(2,1)S(1)} %latent1_join.1.refs_1_, bf16[512,2048]{1,0:T(8,128)(2,1)S(1)} %copy-done.1, bf16[512,2048]{1,0:T(8,128)(2,1)} %collective-permute-done.2.refs_3_, ...), custom_call_target="tpu_custom_call" | custom-call | flops 1073741824 | bytes 11010048 | tf_op jit(solution)/shard_map/latent_rn/pallas_call | solution.py:41
  81.8 2.4 %collective-permute-done.32.refs_1_ = bf16[2,512,128]{2,1,0:T(8,128)(2,1)S(1)} collective-permute-done((bf16[2,512,128]{2,1,0:T(8,128)(2,1)S(1)}, bf16[2,512,128]{2,1,0:T(8,128)(2,1)S(1)}, u32[]{:S(2)}, u32[]{:S(2)}) %collective-permute-start.32) | collective-permute-done | bytes 262176 | tf_op jit(solution)/shard_map/latent1_join/ppermute | solution.py:55
  84.1 3.8 %latent_rf.1 = f32[256,2048]{1,0:T(8,128)} custom-call(s32[5]{0:T(128)S(1)} %stack.23.where, bf16[2,512,128]{2,1,0:T(8,128)(2,1)S(1)} %collective-permute-done.31.refs_0_, bf16[2,512,128]{2,1,0:T(8,128)(2,1)S(1)} %collective-permute-done.32.refs_1_, bf16[512,2048]{1,0:T(8,128)(2,1)S(1)} %copy-done.1, bf16[512,2048]{1,0:T(8,128)(2,1)} %collective-permute-done.2.refs_3_, ...), custom_call_target="tpu_custom_call" | custom-call | flops 1073741824 | bytes 11010048 | tf_op jit(solution)/shard_map/latent_rf/pallas_call | solution.py:241
  88.0 1.6 %latent_grad_final.1 = f32[256,1024]{1,0:T(8,128)} custom-call(s32[5]{0:T(128)S(1)} %stack.23.where, f32[128,1024]{1,0:T(8,128)S(1)} %get-tuple-element.241.refs_0_, bf16[128,1024]{1,0:T(8,128)(2,1)S(1)} %collective-permute-done.24.refs_1_, f32[128,1024]{1,0:T(8,128)S(1)} %get-tuple-element.243.refs_2_, bf16[128,1024]{1,0:T(8,128)(2,1)S(1)} %collective-permute-done.25.refs_3_), custom_call_target="tpu_custom_call" | custom-call | bytes 1572864 | tf_op jit(solution)/shard_map/latent_grad_final/pallas_call | solution.py:241
  (61 shorter events, 11.5 us)
Async XLA Ops:
  0.6 16.6 %collective-permute-start.2 = (bf16[512,2048]{1,0:T(8,128)(2,1)}, bf16[512,2048]{1,0:T(8,128)(2,1)}, u32[]{:S(2)}, u32[]{:S(2)}) collective-permute-start(bf16[512,2048]{1,0:T(8,128)(2,1)} %refs_2_.1), channel_id=1, source_target_pairs={{0,8},{8,0},{16,24},{24,16},{1,9},{9,1},{17,25},{25,17},{2,10},{10... | collective-permute-start | bytes 6291464 | tf_op jit(solution)/shard_map/core_own/ppermute | solution.py:55
  1.1 56.0 %collective-permute-start.26 = (bf16[512,2048]{1,0:T(8,128)(2,1)}, bf16[512,2048]{1,0:T(8,128)(2,1)S(1)}, u32[]{:S(2)}, u32[]{:S(2)}) collective-permute-start(bf16[512,2048]{1,0:T(8,128)(2,1)} %refs_2_.1), channel_id=1, source_target_pairs={{0,16},{8,24},{16,0},{24,8},{1,17},{9,25},{17,1},{25,9},{2,18},{10... | collective-permute-start | bytes 6291464 | tf_op jit(solution)/shard_map/far_og/ppermute | solution.py:55
  3.8 1.6 %copy-start = (bf16[512,2048]{1,0:T(8,128)(2,1)S(1)}, bf16[512,2048]{1,0:T(8,128)(2,1)}, u32[]{:S(2)}) copy-start(bf16[512,2048]{1,0:T(8,128)(2,1)} %refs_2_.1) | copy-start | bytes 6291460
  5.4 2.2 %copy-start.2 = (bf16[1024,2048]{1,0:T(8,128)(2,1)S(1)}, bf16[1024,2048]{1,0:T(8,128)(2,1)}, u32[]{:S(2)}) copy-start(bf16[1024,2048]{1,0:T(8,128)(2,1)} %param.6) | copy-start | bytes 12582916
  7.6 1.3 %copy-start.4 = (bf16[512,1024]{1,0:T(8,128)(2,1)S(1)}, bf16[512,1024]{1,0:T(8,128)(2,1)}, u32[]{:S(2)}) copy-start(bf16[512,1024]{1,0:T(8,128)(2,1)} %acts.1) | copy-start | bytes 3145732
  8.9 5.4 %collective-permute-start.1 = (bf16[512,1024]{1,0:T(8,128)(2,1)S(1)}, bf16[512,1024]{1,0:T(8,128)(2,1)S(1)}, u32[]{:S(2)}, u32[]{:S(2)}) collective-permute-start(bf16[512,1024]{1,0:T(8,128)(2,1)S(1)} %copy-done.4), channel_id=1, source_target_pairs={{0,8},{8,0},{16,24},{24,16},{1,9},{9,1},{17,25},{25,17},{2,10},{10... | collective-permute-start | bytes 3145736 | tf_op jit(solution)/shard_map/core_acts/ppermute | solution.py:55
  9.1 9.9 %collective-permute-start = (bf16[4,256,128]{2,1,0:T(8,128)(2,1)S(1)}, bf16[4,256,128]{2,1,0:T(8,128)(2,1)S(1)}, u32[]{:S(2)}, u32[]{:S(2)}) collective-permute-start(bf16[4,256,128]{2,1,0:T(8,128)(2,1)S(1)} %latent_grad0_S.1), channel_id=1, source_target_pairs={{0,1},{1,0},{2,3},{3,2},{4,5},{5,4},{6,7},{7,6},{8,9},{9,8},{10,11... | collective-permute-start | bytes 786440 | tf_op jit(solution)/shard_map/latent_grad0_S/ppermute | solution.py:55
  11.9 2.4 %copy-start.3 = (bf16[1024,1024]{1,0:T(8,128)(2,1)S(1)}, bf16[1024,1024]{1,0:T(8,128)(2,1)}, u32[]{:S(2)}) copy-start(bf16[1024,1024]{1,0:T(8,128)(2,1)} %refs_4_) | copy-start | bytes 6291460
  11.9 11.9 %collective-permute-start.4 = (bf16[4,256,128]{2,1,0:T(8,128)(2,1)S(1)}, bf16[4,256,128]{2,1,0:T(8,128)(2,1)S(1)}, u32[]{:S(2)}, u32[]{:S(2)}) collective-permute-start(bf16[4,256,128]{2,1,0:T(8,128)(2,1)S(1)} %latent_grad1_S.1), channel_id=1, source_target_pairs={{0,1},{1,0},{2,3},{3,2},{4,5},{5,4},{6,7},{7,6},{8,9},{9,8},{10,11... | collective-permute-start | bytes 786440 | tf_op jit(solution)/shard_map/latent_grad1_S/ppermute | solution.py:55
  15.6 13.8 %collective-permute-start.8 = (bf16[2,512,128]{2,1,0:T(8,128)(2,1)S(1)}, bf16[2,512,128]{2,1,0:T(8,128)(2,1)S(1)}, u32[]{:S(2)}, u32[]{:S(2)}) collective-permute-start(bf16[2,512,128]{2,1,0:T(8,128)(2,1)S(1)} %get-tuple-element.136), channel_id=1, source_target_pairs={{0,1},{1,0},{2,3},{3,2},{4,5},{5,4},{6,7},{7,6},{8,9},{9,8},{10,11... | collective-permute-start | bytes 786440 | tf_op jit(solution)/shard_map/latent_S/ppermute | solution.py:55
  17.2 17.7 %collective-permute-start.6 = (bf16[2,512,128]{2,1,0:T(8,128)(2,1)S(1)}, bf16[2,512,128]{2,1,0:T(8,128)(2,1)S(1)}, u32[]{:S(2)}, u32[]{:S(2)}) collective-permute-start(bf16[2,512,128]{2,1,0:T(8,128)(2,1)S(1)} %get-tuple-element.137), channel_id=1, source_target_pairs={{0,1},{1,0},{2,3},{3,2},{4,5},{5,4},{6,7},{7,6},{8,9},{9,8},{10,11... | collective-permute-start | bytes 786440 | tf_op jit(solution)/shard_map/latent_S/ppermute | solution.py:55
  19.6 6.4 %collective-permute-start.3 = (bf16[4,128,128]{2,1,0:T(8,128)(2,1)S(1)}, bf16[4,128,128]{2,1,0:T(8,128)(2,1)S(1)}, u32[]{:S(2)}, u32[]{:S(2)}) collective-permute-start(bf16[4,128,128]{2,1,0:T(8,128)(2,1)S(1)} %get-tuple-element.146), channel_id=1, source_target_pairs={{0,2},{1,3},{2,0},{3,1},{4,6},{5,7},{6,4},{7,5},{8,10},{9,11},{10,... | collective-permute-start | bytes 393224 | tf_op jit(solution)/shard_map/latent_grad0_near/ppermute | solution.py:55
  24.4 7.3 %collective-permute-start.7 = (bf16[4,128,128]{2,1,0:T(8,128)(2,1)S(1)}, bf16[4,128,128]{2,1,0:T(8,128)(2,1)S(1)}, u32[]{:S(2)}, u32[]{:S(2)}) collective-permute-start(bf16[4,128,128]{2,1,0:T(8,128)(2,1)S(1)} %get-tuple-element.150), channel_id=1, source_target_pairs={{0,2},{1,3},{2,0},{3,1},{4,6},{5,7},{6,4},{7,5},{8,10},{9,11},{10,... | collective-permute-start | bytes 393224 | tf_op jit(solution)/shard_map/latent_grad1_near/ppermute | solution.py:55
  26.7 10.1 %collective-permute-start.5 = (bf16[4,128,128]{2,1,0:T(8,128)(2,1)S(1)}, bf16[4,128,128]{2,1,0:T(8,128)(2,1)S(1)}, u32[]{:S(2)}, u32[]{:S(2)}) collective-permute-start(bf16[4,128,128]{2,1,0:T(8,128)(2,1)S(1)} %get-tuple-element.154), channel_id=1, source_target_pairs={{0,4},{1,5},{2,6},{3,7},{4,0},{5,1},{6,2},{7,3},{8,12},{9,13},{10,... | collective-permute-start | bytes 393224 | tf_op jit(solution)/shard_map/latent_grad0_far/ppermute | solution.py:55
  30.1 8.2 %collective-permute-start.12 = (bf16[2,256,128]{2,1,0:T(8,128)(2,1)S(1)}, bf16[2,256,128]{2,1,0:T(8,128)(2,1)S(1)}, u32[]{:S(2)}, u32[]{:S(2)}) collective-permute-start(bf16[2,256,128]{2,1,0:T(8,128)(2,1)S(1)} %get-tuple-element.158), channel_id=1, source_target_pairs={{0,2},{1,3},{2,0},{3,1},{4,6},{5,7},{6,4},{7,5},{8,10},{9,11},{10,... | collective-permute-start | bytes 393224 | tf_op jit(solution)/shard_map/latent0_near/ppermute | solution.py:55
  32.3 8.8 %collective-permute-start.11 = (bf16[4,128,128]{2,1,0:T(8,128)(2,1)S(1)}, bf16[4,128,128]{2,1,0:T(8,128)(2,1)S(1)}, u32[]{:S(2)}, u32[]{:S(2)}) collective-permute-start(bf16[4,128,128]{2,1,0:T(8,128)(2,1)S(1)} %get-tuple-element.162), channel_id=1, source_target_pairs={{0,4},{1,5},{2,6},{3,7},{4,0},{5,1},{6,2},{7,3},{8,12},{9,13},{10,... | collective-permute-start | bytes 393224 | tf_op jit(solution)/shard_map/latent_grad1_far/ppermute | solution.py:55
  35.6 10.0 %collective-permute-start.10 = (bf16[2,256,128]{2,1,0:T(8,128)(2,1)S(1)}, bf16[2,256,128]{2,1,0:T(8,128)(2,1)S(1)}, u32[]{:S(2)}, u32[]{:S(2)}) collective-permute-start(bf16[2,256,128]{2,1,0:T(8,128)(2,1)S(1)} %get-tuple-element.166), channel_id=1, source_target_pairs={{0,2},{1,3},{2,0},{3,1},{4,6},{5,7},{6,4},{7,5},{8,10},{9,11},{10,... | collective-permute-start | bytes 393224 | tf_op jit(solution)/shard_map/latent1_near/ppermute | solution.py:55
  37.4 12.4 %collective-permute-start.9 = (bf16[4,128,128]{2,1,0:T(8,128)(2,1)S(1)}, bf16[4,128,128]{2,1,0:T(8,128)(2,1)S(1)}, u32[]{:S(2)}, u32[]{:S(2)}) collective-permute-start(bf16[4,128,128]{2,1,0:T(8,128)(2,1)S(1)} %latent_grad0_last.1.mine), channel_id=1, source_target_pairs={{0,2},{1,3},{2,0},{3,1},{4,6},{5,7},{6,4},{7,5},{8,10},{9,11},{10,... | collective-permute-start | bytes 393224 | tf_op jit(solution)/shard_map/latent_grad0_last/ppermute | solution.py:55
  38.9 11.5 %collective-permute-start.15 = (bf16[2,256,128]{2,1,0:T(8,128)(2,1)S(1)}, bf16[2,256,128]{2,1,0:T(8,128)(2,1)S(1)}, u32[]{:S(2)}, u32[]{:S(2)}) collective-permute-start(bf16[2,256,128]{2,1,0:T(8,128)(2,1)S(1)} %get-tuple-element.172), channel_id=1, source_target_pairs={{0,4},{1,5},{2,6},{3,7},{4,0},{5,1},{6,2},{7,3},{8,12},{9,13},{10,... | collective-permute-start | bytes 393224 | tf_op jit(solution)/shard_map/latent0_far/ppermute | solution.py:55
  41.7 11.4 %collective-permute-start.14 = (bf16[4,128,128]{2,1,0:T(8,128)(2,1)S(1)}, bf16[4,128,128]{2,1,0:T(8,128)(2,1)S(1)}, u32[]{:S(2)}, u32[]{:S(2)}) collective-permute-start(bf16[4,128,128]{2,1,0:T(8,128)(2,1)S(1)} %latent_grad1_last.1.mine), channel_id=1, source_target_pairs={{0,2},{1,3},{2,0},{3,1},{4,6},{5,7},{6,4},{7,5},{8,10},{9,11},{10,... | collective-permute-start | bytes 393224 | tf_op jit(solution)/shard_map/latent_grad1_last/ppermute | solution.py:55
  46.2 9.8 %collective-permute-start.17 = (bf16[2,256,128]{2,1,0:T(8,128)(2,1)S(1)}, bf16[2,256,128]{2,1,0:T(8,128)(2,1)S(1)}, u32[]{:S(2)}, u32[]{:S(2)}) collective-permute-start(bf16[2,256,128]{2,1,0:T(8,128)(2,1)S(1)} %get-tuple-element.178), channel_id=1, source_target_pairs={{0,4},{1,5},{2,6},{3,7},{4,0},{5,1},{6,2},{7,3},{8,12},{9,13},{10,... | collective-permute-start | bytes 393224 | tf_op jit(solution)/shard_map/latent1_far/ppermute | solution.py:55
  51.0 4.3 %collective-permute-start.18 = (bf16[256,128]{1,0:T(8,128)(2,1)S(1)}, bf16[256,128]{1,0:T(8,128)(2,1)S(1)}, u32[]{:S(2)}, u32[]{:S(2)}) collective-permute-start(bf16[256,128]{1,0:T(8,128)(2,1)S(1)} %get-tuple-element.184), channel_id=1, source_target_pairs={{0,16},{8,24},{16,0},{24,8},{1,17},{9,25},{17,1},{25,9},{2,18},{10... | collective-permute-start | bytes 196616 | tf_op jit(solution)/shard_map/latent0_last/ppermute | solution.py:55
  51.6 7.6 %collective-permute-start.13 = (bf16[4,256,128]{2,1,0:T(8,128)(2,1)S(1)}, bf16[4,256,128]{2,1,0:T(8,128)(2,1)S(1)}, u32[]{:S(2)}, u32[]{:S(2)}) collective-permute-start(bf16[4,256,128]{2,1,0:T(8,128)(2,1)S(1)} %latent_grad0_join.1.near.refs_0_), channel_id=1, source_target_pairs={{0,1},{1,0},{2,3},{3,2},{4,5},{5,4},{6,7},{7,6},{8,9},{9,8},{10,11... | collective-permute-start | bytes 786440 | tf_op jit(solution)/shard_map/latent_grad0_join/ppermute | solution.py:55
  53.7 9.8 %collective-permute-start.16 = (bf16[4,256,128]{2,1,0:T(8,128)(2,1)S(1)}, bf16[4,256,128]{2,1,0:T(8,128)(2,1)S(1)}, u32[]{:S(2)}, u32[]{:S(2)}) collective-permute-start(bf16[4,256,128]{2,1,0:T(8,128)(2,1)S(1)} %latent_grad1_join.1.near.refs_2_), channel_id=1, source_target_pairs={{0,1},{1,0},{2,3},{3,2},{4,5},{5,4},{6,7},{7,6},{8,9},{9,8},{10,11... | collective-permute-start | bytes 786440 | tf_op jit(solution)/shard_map/latent_grad1_join/ppermute | solution.py:55
  55.8 5.0 %collective-permute-start.20 = (bf16[2,256,128]{2,1,0:T(8,128)(2,1)S(1)}, bf16[2,256,128]{2,1,0:T(8,128)(2,1)S(1)}, u32[]{:S(2)}, u32[]{:S(2)}) collective-permute-start(bf16[2,256,128]{2,1,0:T(8,128)(2,1)S(1)} %latent0_stack.1.mine), channel_id=1, source_target_pairs={{0,2},{1,3},{2,0},{3,1},{4,6},{5,7},{6,4},{7,5},{8,10},{9,11},{10,... | collective-permute-start | bytes 393224 | tf_op jit(solution)/shard_map/latent0_stack/ppermute | solution.py:55
  56.5 4.9 %collective-permute-start.19 = (bf16[256,128]{1,0:T(8,128)(2,1)S(1)}, bf16[256,128]{1,0:T(8,128)(2,1)S(1)}, u32[]{:S(2)}, u32[]{:S(2)}) collective-permute-start(bf16[256,128]{1,0:T(8,128)(2,1)S(1)} %get-tuple-element.192), channel_id=1, source_target_pairs={{0,16},{8,24},{16,0},{24,8},{1,17},{9,25},{17,1},{25,9},{2,18},{10... | collective-permute-start | bytes 196616 | tf_op jit(solution)/shard_map/latent1_last/ppermute | solution.py:55
  57.3 12.9 %collective-permute-start.30 = (bf16[512,512]{1,0:T(8,128)(2,1)S(1)}, bf16[512,512]{1,0:T(8,128)(2,1)S(1)}, u32[]{:S(2)}, u32[]{:S(2)}) collective-permute-start(bf16[512,512]{1,0:T(8,128)(2,1)S(1)} %get-tuple-element.245), channel_id=1, source_target_pairs={{0,8},{8,0},{16,24},{24,16},{1,9},{9,1},{17,25},{25,17},{2,10},{10... | collective-permute-start | bytes 1572872 | tf_op jit(solution)/shard_map/core_far/ppermute | solution.py:55
  59.8 7.9 %collective-permute-start.23 = (bf16[2,2,256,128]{3,2,1,0:T(8,128)(2,1)S(1)}, bf16[2,2,256,128]{3,2,1,0:T(8,128)(2,1)S(1)}, u32[]{:S(2)}, u32[]{:S(2)}) collective-permute-start(bf16[2,2,256,128]{3,2,1,0:T(8,128)(2,1)S(1)} %latent_grad0_halves.1), channel_id=1, source_target_pairs={{0,8},{8,0},{16,24},{24,16},{1,9},{9,1},{17,25},{25,17},{2,10},{10... | collective-permute-start | bytes 786440 | tf_op jit(solution)/shard_map/latent_grad0_halves/ppermute | solution.py:55
  62.0 5.0 %collective-permute-start.22 = (bf16[2,256,128]{2,1,0:T(8,128)(2,1)S(1)}, bf16[2,256,128]{2,1,0:T(8,128)(2,1)S(1)}, u32[]{:S(2)}, u32[]{:S(2)}) collective-permute-start(bf16[2,256,128]{2,1,0:T(8,128)(2,1)S(1)} %latent1_stack.1.mine), channel_id=1, source_target_pairs={{0,2},{1,3},{2,0},{3,1},{4,6},{5,7},{6,4},{7,5},{8,10},{9,11},{10,... | collective-permute-start | bytes 393224 | tf_op jit(solution)/shard_map/latent1_stack/ppermute | solution.py:55
  63.5 10.3 %collective-permute-start.29 = (bf16[512,512]{1,0:T(8,128)(2,1)S(1)}, bf16[512,512]{1,0:T(8,128)(2,1)S(1)}, u32[]{:S(2)}, u32[]{:S(2)}) collective-permute-start(bf16[512,512]{1,0:T(8,128)(2,1)S(1)} %get-tuple-element.246), channel_id=1, source_target_pairs={{0,8},{8,0},{16,24},{24,16},{1,9},{9,1},{17,25},{25,17},{2,10},{10... | collective-permute-start | bytes 1572872 | tf_op jit(solution)/shard_map/core_far/ppermute | solution.py:55
  63.5 11.4 %collective-permute-start.28 = (bf16[512,512]{1,0:T(8,128)(2,1)S(1)}, bf16[512,512]{1,0:T(8,128)(2,1)S(1)}, u32[]{:S(2)}, u32[]{:S(2)}) collective-permute-start(bf16[512,512]{1,0:T(8,128)(2,1)S(1)} %get-tuple-element.247), channel_id=1, source_target_pairs={{0,8},{8,0},{16,24},{24,16},{1,9},{9,1},{17,25},{25,17},{2,10},{10... | collective-permute-start | bytes 1572872 | tf_op jit(solution)/shard_map/core_far/ppermute | solution.py:55
  67.0 11.8 %collective-permute-start.27 = (bf16[512,512]{1,0:T(8,128)(2,1)S(1)}, bf16[512,512]{1,0:T(8,128)(2,1)S(1)}, u32[]{:S(2)}, u32[]{:S(2)}) collective-permute-start(bf16[512,512]{1,0:T(8,128)(2,1)S(1)} %get-tuple-element.248), channel_id=1, source_target_pairs={{0,8},{8,0},{16,24},{24,16},{1,9},{9,1},{17,25},{25,17},{2,10},{10... | collective-permute-start | bytes 1572872 | tf_op jit(solution)/shard_map/core_far/ppermute | solution.py:55
  67.6 4.2 %collective-permute-start.21 = (bf16[2,2,256,128]{3,2,1,0:T(8,128)(2,1)S(1)}, bf16[2,2,256,128]{3,2,1,0:T(8,128)(2,1)S(1)}, u32[]{:S(2)}, u32[]{:S(2)}) collective-permute-start(bf16[2,2,256,128]{3,2,1,0:T(8,128)(2,1)S(1)} %latent_grad1_halves.1), channel_id=1, source_target_pairs={{0,8},{8,0},{16,24},{24,16},{1,9},{9,1},{17,25},{25,17},{2,10},{10... | collective-permute-start | bytes 786440 | tf_op jit(solution)/shard_map/latent_grad1_halves/ppermute | solution.py:55
  70.2 11.5 %collective-permute-start.31 = (bf16[2,512,128]{2,1,0:T(8,128)(2,1)S(1)}, bf16[2,512,128]{2,1,0:T(8,128)(2,1)S(1)}, u32[]{:S(2)}, u32[]{:S(2)}) collective-permute-start(bf16[2,512,128]{2,1,0:T(8,128)(2,1)S(1)} %latent0_join.1.refs_0_), channel_id=1, source_target_pairs={{0,1},{1,0},{2,3},{3,2},{4,5},{5,4},{6,7},{7,6},{8,9},{9,8},{10,11... | collective-permute-start | bytes 786440 | tf_op jit(solution)/shard_map/latent0_join/ppermute | solution.py:55
  71.8 12.3 %collective-permute-start.32 = (bf16[2,512,128]{2,1,0:T(8,128)(2,1)S(1)}, bf16[2,512,128]{2,1,0:T(8,128)(2,1)S(1)}, u32[]{:S(2)}, u32[]{:S(2)}) collective-permute-start(bf16[2,512,128]{2,1,0:T(8,128)(2,1)S(1)} %latent1_join.1.refs_1_), channel_id=1, source_target_pairs={{0,1},{1,0},{2,3},{3,2},{4,5},{5,4},{6,7},{7,6},{8,9},{9,8},{10,11... | collective-permute-start | bytes 786440 | tf_op jit(solution)/shard_map/latent1_join/ppermute | solution.py:55
  73.8 5.1 %copy-start.1 = (bf16[512,2048]{1,0:T(8,128)(2,1)S(1)}, bf16[512,2048]{1,0:T(8,128)(2,1)}, u32[]{:S(2)}) copy-start(bf16[512,2048]{1,0:T(8,128)(2,1)} %refs_2_.1) | copy-start | bytes 6291460
  73.8 14.2 %collective-permute-start.25 = (bf16[128,1024]{1,0:T(8,128)(2,1)S(1)}, bf16[128,1024]{1,0:T(8,128)(2,1)S(1)}, u32[]{:S(2)}, u32[]{:S(2)}) collective-permute-start(bf16[128,1024]{1,0:T(8,128)(2,1)S(1)} %get-tuple-element.216), channel_id=1, source_target_pairs={{0,16},{8,24},{16,0},{24,8},{1,17},{9,25},{17,1},{25,9},{2,18},{10... | collective-permute-start | bytes 786440 | tf_op jit(solution)/shard_map/latent_grad1_left/ppermute | solution.py:55
  74.9 13.1 %collective-permute-start.24 = (bf16[128,1024]{1,0:T(8,128)(2,1)S(1)}, bf16[128,1024]{1,0:T(8,128)(2,1)S(1)}, u32[]{:S(2)}, u32[]{:S(2)}) collective-permute-start(bf16[128,1024]{1,0:T(8,128)(2,1)S(1)} %get-tuple-element.207), channel_id=1, source_target_pairs={{0,16},{8,24},{16,0},{24,8},{1,17},{9,25},{17,1},{25,9},{2,18},{10... | collective-permute-start | bytes 786440 | tf_op jit(solution)/shard_map/latent_grad0_left/ppermute | solution.py:55

commit v6 on v5

--- a/solution.py
+++ b/solution.py
@@ -375,25 +375,35 @@
     )
 
 
-def final_kernel(scale, count, where, *refs):
+def final_kernel(scale, count, blocks, where, *refs):
     refs, (out, held, sems) = refs[:-3], refs[-3:]
     per = len(refs) // count
     width = refs[0].shape[0]
+    rows = width // blocks
     copies = []
     for chunk in range(count):
-        total = refs[chunk * per][...]
-        for other in refs[chunk * per + 1 : (chunk + 1) * per]:
-            total = total + other[...].astype(F32)
-        rows = slice(chunk * width, (chunk + 1) * width)
-        held[rows, :] = total * scale
-        copies.append(write(held, out, sems, chunk, (rows, slice(None))))
+        for i in range(blocks):
+            part = slice(i * rows, (i + 1) * rows)
+            total = refs[chunk * per][part, :]
+            for other in refs[chunk * per + 1 : (chunk + 1) * per]:
+                total = total + other[part, :].astype(F32)
+            span = slice(chunk * width + i * rows, chunk * width + (i + 1) * rows)
+            held[span, :] = total * scale
+            copies.append(write(held, out, sems, chunk * blocks + i, (span, slice(None))))
     for copy in copies:
         copy.wait()
 
 
 def left_final(where, scale, values, shape):
     return written_call(
-        functools.partial(final_kernel, scale, CHUNKS), where, values, (shape, F32), CHUNKS, [], 0, 16
+        functools.partial(final_kernel, scale, CHUNKS, 2),
+        where,
+        values,
+        (shape, F32),
+        2 * CHUNKS,
+        [],
+        0,
+        16,
     )
 
 

time: 89.8 us -> 89.8 us (level)
  no operation moved by 1% of the time
where the time goes in v6:
time: 89.8 us; the launch traced here: 89.5 us
  starting transfers between devices  34 us (38%)
  Pallas kernels  32.4 us (36%)
  waiting for transfers between devices  17.9 us (20%)
  local copies, waits for them, and re-layouts  4.03 us (4%)
  between operations  1.06 us (1%)
    ppermute x33, starting transfers between devices, swap(): return lax.ppermute(value, axis, [(i, i ^ mask) for i in range(size)])  34 us
    pallas_call x28, Pallas kernels, whole_call(): pl.pallas_call(kernel, out_shape=[jax.ShapeDtypeStruct(s, t) for s, t in...  24.2 us
    ppermute x33, waiting for transfers between devices, swap(): return lax.ppermute(value, axis, [(i, i ^ mask) for i in range(size)])  17.9 us
    pallas_call x3, Pallas kernels, written_call(): pl.pallas_call(kernel, out_shape=jax.ShapeDtypeStruct(shape, dtype), in_s...  8.3 us
    unnamed x10, local copies, waits for them, and re-layouts  3.79 us
  transfers between devices with their start and end apart: 33, of which 9 were waited for; matrix products, arithmetic and copies ran while one was open for 0% of the time, Pallas kernels for 35%

profile of v6, /device:TPU:0, one launch (start us, length us, event | category | flops | bytes accessed | tf_op | source)
XLA Modules:
  0.0 89.5 jit_solution(5260190140684065096)
XLA Ops:
  1.1 2.6 %collective-permute-start.26 = (bf16[512,2048]{1,0:T(8,128)(2,1)}, bf16[512,2048]{1,0:T(8,128)(2,1)S(1)}, u32[]{:S(2)}, u32[]{:S(2)}) collective-permute-start(bf16[512,2048]{1,0:T(8,128)(2,1)} %refs_2_.1), channel_id=1, source_target_pairs={{0,16},{8,24},{16,0},{24,8},{1,17},{9,25},{17,1},{25,9},{2,18},{10... | collective-permute-start | bytes 6291464 | tf_op jit(solution)/shard_map/far_og/ppermute | solution.py:55
  3.8 1.6 %copy-done = bf16[512,2048]{1,0:T(8,128)(2,1)S(1)} copy-done((bf16[512,2048]{1,0:T(8,128)(2,1)S(1)}, bf16[512,2048]{1,0:T(8,128)(2,1)}, u32[]{:S(2)}) %copy-start) | copy-done | bytes 2097176
  5.4 2.2 %copy-done.2 = bf16[1024,2048]{1,0:T(8,128)(2,1)S(1)} copy-done((bf16[1024,2048]{1,0:T(8,128)(2,1)S(1)}, bf16[1024,2048]{1,0:T(8,128)(2,1)}, u32[]{:S(2)}) %copy-start.2) | copy-done | bytes 4194328
  7.6 1.3 %latent_grad0_S.1 = bf16[4,256,128]{2,1,0:T(8,128)(2,1)S(1)} custom-call(s32[5]{0:T(128)S(1)} %stack.23.where, bf16[512,2048]{1,0:T(8,128)(2,1)S(1)} %copy-done, bf16[4,2,128,2048]{3,2,1,0:T(8,128)(2,1)S(1)} %bitcast.7), custom_call_target="tpu_custom_call" | custom-call | flops 536870912 | bytes 6553600 | tf_op jit(solution)/shard_map/latent_grad0_S/pallas_call | solution.py:41
  9.1 1.5 %collective-permute-start = (bf16[4,256,128]{2,1,0:T(8,128)(2,1)S(1)}, bf16[4,256,128]{2,1,0:T(8,128)(2,1)S(1)}, u32[]{:S(2)}, u32[]{:S(2)}) collective-permute-start(bf16[4,256,128]{2,1,0:T(8,128)(2,1)S(1)} %latent_grad0_S.1), channel_id=1, source_target_pairs={{0,1},{1,0},{2,3},{3,2},{4,5},{5,4},{6,7},{7,6},{8,9},{9,8},{10,11... | collective-permute-start | bytes 786440 | tf_op jit(solution)/shard_map/latent_grad0_S/ppermute | solution.py:55
  10.6 1.3 %latent_grad1_S.1 = bf16[4,256,128]{2,1,0:T(8,128)(2,1)S(1)} custom-call(s32[5]{0:T(128)S(1)} %stack.23.where, bf16[512,2048]{1,0:T(8,128)(2,1)S(1)} %copy-done, bf16[4,2,128,2048]{3,2,1,0:T(8,128)(2,1)S(1)} %bitcast.8), custom_call_target="tpu_custom_call" | custom-call | flops 536870912 | bytes 6553600 | tf_op jit(solution)/shard_map/latent_grad1_S/pallas_call | solution.py:41
  12.5 1.8 %latent_grad_K.1 = (f32[4,256,128]{2,1,0:T(8,128)S(1)}, f32[4,256,128]{2,1,0:T(8,128)S(1)}) custom-call(s32[5]{0:T(128)S(1)} %stack.23.where, bf16[512,2048]{1,0:T(8,128)(2,1)S(1)} %copy-done, bf16[4,2,128,2048]{3,2,1,0:T(8,128)(2,1)S(1)} %bitcast.9), custom_call_target="tpu_custom_call" | custom-call | flops 1073741824 | bytes 7340032 | tf_op jit(solution)/shard_map/latent_grad_K/pallas_call | solution.py:41
  14.3 1.3 %latent_S.1 = (bf16[2,512,128]{2,1,0:T(8,128)(2,1)S(1)}, bf16[2,512,128]{2,1,0:T(8,128)(2,1)S(1)}) custom-call(s32[5]{0:T(128)S(1)} %stack.23.where, bf16[512,1024]{1,0:T(8,128)(2,1)S(1)} %copy-done.4, bf16[512,1024]{1,0:T(8,128)(2,1)S(1)} %collective-permute-done.1.refs_1_.acts_other, bf16[2,2,2,128,1024]{4,3,2,1,0:T(8,128)(2,1)S(1)} %bitcast.10), custom_call_target="tpu_custom_call" | custom-call | flops 536870912 | bytes 4718592 | tf_op jit(solution)/shard_map/latent_S/pallas_call | solution.py:41
  15.6 1.6 %collective-permute-start.8 = (bf16[2,512,128]{2,1,0:T(8,128)(2,1)S(1)}, bf16[2,512,128]{2,1,0:T(8,128)(2,1)S(1)}, u32[]{:S(2)}, u32[]{:S(2)}) collective-permute-start(bf16[2,512,128]{2,1,0:T(8,128)(2,1)S(1)} %get-tuple-element.136), channel_id=1, source_target_pairs={{0,1},{1,0},{2,3},{3,2},{4,5},{5,4},{6,7},{7,6},{8,9},{9,8},{10,11... | collective-permute-start | bytes 786440 | tf_op jit(solution)/shard_map/latent_S/ppermute | solution.py:55
  17.7 1.3 %latent_K.1 = (f32[2,512,128]{2,1,0:T(8,128)S(1)}, f32[2,512,128]{2,1,0:T(8,128)S(1)}) custom-call(s32[5]{0:T(128)S(1)} %stack.23.where, bf16[512,1024]{1,0:T(8,128)(2,1)S(1)} %copy-done.4, bf16[512,1024]{1,0:T(8,128)(2,1)S(1)} %collective-permute-done.1.refs_1_.acts_other, bf16[2,2,2,128,1024]{4,3,2,1,0:T(8,128)(2,1)S(1)} %bitcast.11), custom_call_target="tpu_custom_call" | custom-call | flops 536870912 | bytes 5242880 | tf_op jit(solution)/shard_map/latent_K/pallas_call | solution.py:41
  19.0 0.6 latent_grad0_near.1
  19.6 1.6 %collective-permute-start.3 = (bf16[4,128,128]{2,1,0:T(8,128)(2,1)S(1)}, bf16[4,128,128]{2,1,0:T(8,128)(2,1)S(1)}, u32[]{:S(2)}, u32[]{:S(2)}) collective-permute-start(bf16[4,128,128]{2,1,0:T(8,128)(2,1)S(1)} %get-tuple-element.146), channel_id=1, source_target_pairs={{0,2},{1,3},{2,0},{3,1},{4,6},{5,7},{6,4},{7,5},{8,10},{9,11},{10,... | collective-permute-start | bytes 393224 | tf_op jit(solution)/shard_map/latent_grad0_near/ppermute | solution.py:55
  21.3 2.6 %collective-permute-done.4.sent = bf16[4,256,128]{2,1,0:T(8,128)(2,1)S(1)} collective-permute-done((bf16[4,256,128]{2,1,0:T(8,128)(2,1)S(1)}, bf16[4,256,128]{2,1,0:T(8,128)(2,1)S(1)}, u32[]{:S(2)}, u32[]{:S(2)}) %collective-permute-start.4) | collective-permute-done | bytes 262176 | tf_op jit(solution)/shard_map/latent_grad1_S/ppermute | solution.py:55
  23.8 0.6 latent_grad1_near.1
  24.4 1.6 %collective-permute-start.7 = (bf16[4,128,128]{2,1,0:T(8,128)(2,1)S(1)}, bf16[4,128,128]{2,1,0:T(8,128)(2,1)S(1)}, u32[]{:S(2)}, u32[]{:S(2)}) collective-permute-start(bf16[4,128,128]{2,1,0:T(8,128)(2,1)S(1)} %get-tuple-element.150), channel_id=1, source_target_pairs={{0,2},{1,3},{2,0},{3,1},{4,6},{5,7},{6,4},{7,5},{8,10},{9,11},{10,... | collective-permute-start | bytes 393224 | tf_op jit(solution)/shard_map/latent_grad1_near/ppermute | solution.py:55
  26.1 0.6 latent_grad0_far.1
  26.7 2.7 %collective-permute-start.5 = (bf16[4,128,128]{2,1,0:T(8,128)(2,1)S(1)}, bf16[4,128,128]{2,1,0:T(8,128)(2,1)S(1)}, u32[]{:S(2)}, u32[]{:S(2)}) collective-permute-start(bf16[4,128,128]{2,1,0:T(8,128)(2,1)S(1)} %get-tuple-element.154), channel_id=1, source_target_pairs={{0,4},{1,5},{2,6},{3,7},{4,0},{5,1},{6,2},{7,3},{8,12},{9,13},{10,... | collective-permute-start | bytes 393224 | tf_op jit(solution)/shard_map/latent_grad0_far/ppermute | solution.py:55
  29.5 0.6 latent0_near.1
  30.1 1.6 %collective-permute-start.12 = (bf16[2,256,128]{2,1,0:T(8,128)(2,1)S(1)}, bf16[2,256,128]{2,1,0:T(8,128)(2,1)S(1)}, u32[]{:S(2)}, u32[]{:S(2)}) collective-permute-start(bf16[2,256,128]{2,1,0:T(8,128)(2,1)S(1)} %get-tuple-element.158), channel_id=1, source_target_pairs={{0,2},{1,3},{2,0},{3,1},{4,6},{5,7},{6,4},{7,5},{8,10},{9,11},{10,... | collective-permute-start | bytes 393224 | tf_op jit(solution)/shard_map/latent0_near/ppermute | solution.py:55
  31.7 0.6 latent_grad1_far.1
  32.3 2.7 %collective-permute-start.11 = (bf16[4,128,128]{2,1,0:T(8,128)(2,1)S(1)}, bf16[4,128,128]{2,1,0:T(8,128)(2,1)S(1)}, u32[]{:S(2)}, u32[]{:S(2)}) collective-permute-start(bf16[4,128,128]{2,1,0:T(8,128)(2,1)S(1)} %get-tuple-element.162), channel_id=1, source_target_pairs={{0,4},{1,5},{2,6},{3,7},{4,0},{5,1},{6,2},{7,3},{8,12},{9,13},{10,... | collective-permute-start | bytes 393224 | tf_op jit(solution)/shard_map/latent_grad1_far/ppermute | solution.py:55
  34.9 0.6 latent1_near.1
  35.6 1.2 %collective-permute-start.10 = (bf16[2,256,128]{2,1,0:T(8,128)(2,1)S(1)}, bf16[2,256,128]{2,1,0:T(8,128)(2,1)S(1)}, u32[]{:S(2)}, u32[]{:S(2)}) collective-permute-start(bf16[2,256,128]{2,1,0:T(8,128)(2,1)S(1)} %get-tuple-element.166), channel_id=1, source_target_pairs={{0,2},{1,3},{2,0},{3,1},{4,6},{5,7},{6,4},{7,5},{8,10},{9,11},{10,... | collective-permute-start | bytes 393224 | tf_op jit(solution)/shard_map/latent1_near/ppermute | solution.py:55
  37.4 0.9 %collective-permute-start.9 = (bf16[4,128,128]{2,1,0:T(8,128)(2,1)S(1)}, bf16[4,128,128]{2,1,0:T(8,128)(2,1)S(1)}, u32[]{:S(2)}, u32[]{:S(2)}) collective-permute-start(bf16[4,128,128]{2,1,0:T(8,128)(2,1)S(1)} %latent_grad0_last.1.mine), channel_id=1, source_target_pairs={{0,2},{1,3},{2,0},{3,1},{4,6},{5,7},{6,4},{7,5},{8,10},{9,11},{10,... | collective-permute-start | bytes 393224 | tf_op jit(solution)/shard_map/latent_grad0_last/ppermute | solution.py:55
  38.3 0.6 latent0_far.1
  38.9 2.2 %collective-permute-start.15 = (bf16[2,256,128]{2,1,0:T(8,128)(2,1)S(1)}, bf16[2,256,128]{2,1,0:T(8,128)(2,1)S(1)}, u32[]{:S(2)}, u32[]{:S(2)}) collective-permute-start(bf16[2,256,128]{2,1,0:T(8,128)(2,1)S(1)} %get-tuple-element.172), channel_id=1, source_target_pairs={{0,4},{1,5},{2,6},{3,7},{4,0},{5,1},{6,2},{7,3},{8,12},{9,13},{10,... | collective-permute-start | bytes 393224 | tf_op jit(solution)/shard_map/latent0_far/ppermute | solution.py:55
  41.7 1.6 %collective-permute-start.14 = (bf16[4,128,128]{2,1,0:T(8,128)(2,1)S(1)}, bf16[4,128,128]{2,1,0:T(8,128)(2,1)S(1)}, u32[]{:S(2)}, u32[]{:S(2)}) collective-permute-start(bf16[4,128,128]{2,1,0:T(8,128)(2,1)S(1)} %latent_grad1_last.1.mine), channel_id=1, source_target_pairs={{0,2},{1,3},{2,0},{3,1},{4,6},{5,7},{6,4},{7,5},{8,10},{9,11},{10,... | collective-permute-start | bytes 393224 | tf_op jit(solution)/shard_map/latent_grad1_last/ppermute | solution.py:55
  43.3 2.3 %collective-permute-done.10.other = bf16[2,256,128]{2,1,0:T(8,128)(2,1)S(1)} collective-permute-done((bf16[2,256,128]{2,1,0:T(8,128)(2,1)S(1)}, bf16[2,256,128]{2,1,0:T(8,128)(2,1)S(1)}, u32[]{:S(2)}, u32[]{:S(2)}) %collective-permute-start.10) | collective-permute-done | bytes 131104 | tf_op jit(solution)/shard_map/latent1_near/ppermute | solution.py:55
  45.6 0.6 latent1_far.1
  46.2 3.6 %collective-permute-done.9.other = bf16[4,128,128]{2,1,0:T(8,128)(2,1)S(1)} collective-permute-done((bf16[4,128,128]{2,1,0:T(8,128)(2,1)S(1)}, bf16[4,128,128]{2,1,0:T(8,128)(2,1)S(1)}, u32[]{:S(2)}, u32[]{:S(2)}) %collective-permute-start.9) | collective-permute-done | bytes 131104 | tf_op jit(solution)/shard_map/latent_grad0_last/ppermute | solution.py:55
  51.0 0.6 collective-permute-start.18
  51.6 1.5 %collective-permute-start.13 = (bf16[4,256,128]{2,1,0:T(8,128)(2,1)S(1)}, bf16[4,256,128]{2,1,0:T(8,128)(2,1)S(1)}, u32[]{:S(2)}, u32[]{:S(2)}) collective-permute-start(bf16[4,256,128]{2,1,0:T(8,128)(2,1)S(1)} %latent_grad0_join.1.near.refs_0_), channel_id=1, source_target_pairs={{0,1},{1,0},{2,3},{3,2},{4,5},{5,4},{6,7},{7,6},{8,9},{9,8},{10,11... | collective-permute-start | bytes 786440 | tf_op jit(solution)/shard_map/latent_grad0_join/ppermute | solution.py:55
  54.2 1.1 %collective-permute-done.18.refs_1_ = bf16[256,128]{1,0:T(8,128)(2,1)S(1)} collective-permute-done((bf16[256,128]{1,0:T(8,128)(2,1)S(1)}, bf16[256,128]{1,0:T(8,128)(2,1)S(1)}, u32[]{:S(2)}, u32[]{:S(2)}) %collective-permute-start.18) | collective-permute-done | bytes 65568 | tf_op jit(solution)/shard_map/latent0_last/ppermute | solution.py:55
  56.5 0.6 collective-permute-start.19
  57.4 1.8 %collective-permute-done.13.far.refs_1_ = bf16[4,256,128]{2,1,0:T(8,128)(2,1)S(1)} collective-permute-done((bf16[4,256,128]{2,1,0:T(8,128)(2,1)S(1)}, bf16[4,256,128]{2,1,0:T(8,128)(2,1)S(1)}, u32[]{:S(2)}, u32[]{:S(2)}) %collective-permute-start.13) | collective-permute-done | bytes 262176 | tf_op jit(solution)/shard_map/latent_grad0_join/ppermute | solution.py:55
  59.8 1.0 %collective-permute-done.20.other = bf16[2,256,128]{2,1,0:T(8,128)(2,1)S(1)} collective-permute-done((bf16[2,256,128]{2,1,0:T(8,128)(2,1)S(1)}, bf16[2,256,128]{2,1,0:T(8,128)(2,1)S(1)}, u32[]{:S(2)}, u32[]{:S(2)}) %collective-permute-start.20) | collective-permute-done | bytes 131104 | tf_op jit(solution)/shard_map/latent0_stack/ppermute | solution.py:55
  62.0 1.5 %collective-permute-start.22 = (bf16[2,256,128]{2,1,0:T(8,128)(2,1)S(1)}, bf16[2,256,128]{2,1,0:T(8,128)(2,1)S(1)}, u32[]{:S(2)}, u32[]{:S(2)}) collective-permute-start(bf16[2,256,128]{2,1,0:T(8,128)(2,1)S(1)} %latent1_stack.1.mine), channel_id=1, source_target_pairs={{0,2},{1,3},{2,0},{3,1},{4,6},{5,7},{6,4},{7,5},{8,10},{9,11},{10,... | collective-permute-start | bytes 393224 | tf_op jit(solution)/shard_map/latent1_stack/ppermute | solution.py:55
  64.0 3.1 %collective-permute-done.22.other = bf16[2,256,128]{2,1,0:T(8,128)(2,1)S(1)} collective-permute-done((bf16[2,256,128]{2,1,0:T(8,128)(2,1)S(1)}, bf16[2,256,128]{2,1,0:T(8,128)(2,1)S(1)}, u32[]{:S(2)}, u32[]{:S(2)}) %collective-permute-start.22) | collective-permute-done | bytes 131104 | tf_op jit(solution)/shard_map/latent1_stack/ppermute | solution.py:55
  68.2 1.4 %latent_grad0_left.1 = (f32[128,1024]{1,0:T(8,128)S(1)}, bf16[128,1024]{1,0:T(8,128)(2,1)S(1)}) custom-call(s32[5]{0:T(128)S(1)} %stack.23.where, bf16[4,256,128]{2,1,0:T(8,128)(2,1)S(1)} %latent_grad0_join.1.near.refs_0_, bf16[4,256,128]{2,1,0:T(8,128)(2,1)S(1)} %collective-permute-done.13.far.refs_1_, ...), custom_call_target="tpu_custom_call" | custom-call | flops 536870912 | bytes 3670016 | tf_op jit(solution)/shard_map/latent_grad0_left/pallas_call | solution.py:41
  70.2 1.6 %collective-permute-start.31 = (bf16[2,512,128]{2,1,0:T(8,128)(2,1)S(1)}, bf16[2,512,128]{2,1,0:T(8,128)(2,1)S(1)}, u32[]{:S(2)}, u32[]{:S(2)}) collective-permute-start(bf16[2,512,128]{2,1,0:T(8,128)(2,1)S(1)} %latent0_join.1.refs_0_), channel_id=1, source_target_pairs={{0,1},{1,0},{2,3},{3,2},{4,5},{5,4},{6,7},{7,6},{8,9},{9,8},{10,11... | collective-permute-start | bytes 786440 | tf_op jit(solution)/shard_map/latent0_join/ppermute | solution.py:55
  72.3 1.4 %latent_grad1_left.1 = (f32[128,1024]{1,0:T(8,128)S(1)}, bf16[128,1024]{1,0:T(8,128)(2,1)S(1)}) custom-call(s32[5]{0:T(128)S(1)} %stack.23.where, bf16[4,256,128]{2,1,0:T(8,128)(2,1)S(1)} %latent_grad1_join.1.near.refs_2_, bf16[4,256,128]{2,1,0:T(8,128)(2,1)S(1)} %collective-permute-done.16.far.refs_3_, ...), custom_call_target="tpu_custom_call" | custom-call | flops 536870912 | bytes 3670016 | tf_op jit(solution)/shard_map/latent_grad1_left/pallas_call | solution.py:41
  73.8 1.1 %collective-permute-start.25 = (bf16[128,1024]{1,0:T(8,128)(2,1)S(1)}, bf16[128,1024]{1,0:T(8,128)(2,1)S(1)}, u32[]{:S(2)}, u32[]{:S(2)}) collective-permute-start(bf16[128,1024]{1,0:T(8,128)(2,1)S(1)} %get-tuple-element.216), channel_id=1, source_target_pairs={{0,16},{8,24},{16,0},{24,8},{1,17},{9,25},{17,1},{25,9},{2,18},{10... | collective-permute-start | bytes 786440 | tf_op jit(solution)/shard_map/latent_grad1_left/ppermute | solution.py:55
  74.9 1.0 %collective-permute-start.24 = (bf16[128,1024]{1,0:T(8,128)(2,1)S(1)}, bf16[128,1024]{1,0:T(8,128)(2,1)S(1)}, u32[]{:S(2)}, u32[]{:S(2)}) collective-permute-start(bf16[128,1024]{1,0:T(8,128)(2,1)S(1)} %get-tuple-element.207), channel_id=1, source_target_pairs={{0,16},{8,24},{16,0},{24,8},{1,17},{9,25},{17,1},{25,9},{2,18},{10... | collective-permute-start | bytes 786440 | tf_op jit(solution)/shard_map/latent_grad0_left/ppermute | solution.py:55
  75.9 2.9 %latent_grad_input.1 = bf16[512,1024]{1,0:T(8,128)(2,1)} custom-call(s32[5]{0:T(128)S(1)} %stack.23.where, bf16[4,256,128]{2,1,0:T(8,128)(2,1)S(1)} %latent_grad0_join.1.near.refs_0_, bf16[4,256,128]{2,1,0:T(8,128)(2,1)S(1)} %collective-permute-done.13.far.refs_1_, bf16[4,256,128]{2,1,0:T(8,128)(2,1)S(1)} %latent_grad1_join.1.near.refs_2_, ...), custom_call_target="tpu_custom_call" | custom-call | flops 1073741824 | bytes 3145728 | tf_op jit(solution)/shard_map/latent_grad_input/pallas_call | solution.py:241
  78.9 2.9 %latent_rn.1.refs_9_ = f32[256,2048]{1,0:T(8,128)S(1)} custom-call(s32[5]{0:T(128)S(1)} %stack.23.where, bf16[2,512,128]{2,1,0:T(8,128)(2,1)S(1)} %latent0_join.1.refs_0_, bf16[2,512,128]{2,1,0:T(8,128)(2,1)S(1)} %latent1_join.1.refs_1_, bf16[512,2048]{1,0:T(8,128)(2,1)S(1)} %copy-done.1, bf16[512,2048]{1,0:T(8,128)(2,1)} %collective-permute-done.2.refs_3_, ...), custom_call_target="tpu_custom_call" | custom-call | flops 1073741824 | bytes 11010048 | tf_op jit(solution)/shard_map/latent_rn/pallas_call | solution.py:41
  81.8 2.4 %collective-permute-done.32.refs_1_ = bf16[2,512,128]{2,1,0:T(8,128)(2,1)S(1)} collective-permute-done((bf16[2,512,128]{2,1,0:T(8,128)(2,1)S(1)}, bf16[2,512,128]{2,1,0:T(8,128)(2,1)S(1)}, u32[]{:S(2)}, u32[]{:S(2)}) %collective-permute-start.32) | collective-permute-done | bytes 262176 | tf_op jit(solution)/shard_map/latent1_join/ppermute | solution.py:55
  84.1 3.8 %latent_rf.1 = f32[256,2048]{1,0:T(8,128)} custom-call(s32[5]{0:T(128)S(1)} %stack.23.where, bf16[2,512,128]{2,1,0:T(8,128)(2,1)S(1)} %collective-permute-done.31.refs_0_, bf16[2,512,128]{2,1,0:T(8,128)(2,1)S(1)} %collective-permute-done.32.refs_1_, bf16[512,2048]{1,0:T(8,128)(2,1)S(1)} %copy-done.1, bf16[512,2048]{1,0:T(8,128)(2,1)} %collective-permute-done.2.refs_3_, ...), custom_call_target="tpu_custom_call" | custom-call | flops 1073741824 | bytes 11010048 | tf_op jit(solution)/shard_map/latent_rf/pallas_call | solution.py:241
  88.0 1.6 %latent_grad_final.1 = f32[256,1024]{1,0:T(8,128)} custom-call(s32[5]{0:T(128)S(1)} %stack.23.where, f32[128,1024]{1,0:T(8,128)S(1)} %get-tuple-element.241.refs_0_, bf16[128,1024]{1,0:T(8,128)(2,1)S(1)} %collective-permute-done.24.refs_1_, f32[128,1024]{1,0:T(8,128)S(1)} %get-tuple-element.243.refs_2_, bf16[128,1024]{1,0:T(8,128)(2,1)S(1)} %collective-permute-done.25.refs_3_), custom_call_target="tpu_custom_call" | custom-call | bytes 1572864 | tf_op jit(solution)/shard_map/latent_grad_final/pallas_call | solution.py:241
  (61 shorter events, 11.5 us)
Async XLA Ops:
  0.6 16.6 %collective-permute-start.2 = (bf16[512,2048]{1,0:T(8,128)(2,1)}, bf16[512,2048]{1,0:T(8,128)(2,1)}, u32[]{:S(2)}, u32[]{:S(2)}) collective-permute-start(bf16[512,2048]{1,0:T(8,128)(2,1)} %refs_2_.1), channel_id=1, source_target_pairs={{0,8},{8,0},{16,24},{24,16},{1,9},{9,1},{17,25},{25,17},{2,10},{10... | collective-permute-start | bytes 6291464 | tf_op jit(solution)/shard_map/core_own/ppermute | solution.py:55
  1.1 56.0 %collective-permute-start.26 = (bf16[512,2048]{1,0:T(8,128)(2,1)}, bf16[512,2048]{1,0:T(8,128)(2,1)S(1)}, u32[]{:S(2)}, u32[]{:S(2)}) collective-permute-start(bf16[512,2048]{1,0:T(8,128)(2,1)} %refs_2_.1), channel_id=1, source_target_pairs={{0,16},{8,24},{16,0},{24,8},{1,17},{9,25},{17,1},{25,9},{2,18},{10... | collective-permute-start | bytes 6291464 | tf_op jit(solution)/shard_map/far_og/ppermute | solution.py:55
  3.8 1.6 %copy-start = (bf16[512,2048]{1,0:T(8,128)(2,1)S(1)}, bf16[512,2048]{1,0:T(8,128)(2,1)}, u32[]{:S(2)}) copy-start(bf16[512,2048]{1,0:T(8,128)(2,1)} %refs_2_.1) | copy-start | bytes 6291460
  5.4 2.2 %copy-start.2 = (bf16[1024,2048]{1,0:T(8,128)(2,1)S(1)}, bf16[1024,2048]{1,0:T(8,128)(2,1)}, u32[]{:S(2)}) copy-start(bf16[1024,2048]{1,0:T(8,128)(2,1)} %param.6) | copy-start | bytes 12582916
  7.6 1.3 %copy-start.4 = (bf16[512,1024]{1,0:T(8,128)(2,1)S(1)}, bf16[512,1024]{1,0:T(8,128)(2,1)}, u32[]{:S(2)}) copy-start(bf16[512,1024]{1,0:T(8,128)(2,1)} %acts.1) | copy-start | bytes 3145732
  8.9 5.4 %collective-permute-start.1 = (bf16[512,1024]{1,0:T(8,128)(2,1)S(1)}, bf16[512,1024]{1,0:T(8,128)(2,1)S(1)}, u32[]{:S(2)}, u32[]{:S(2)}) collective-permute-start(bf16[512,1024]{1,0:T(8,128)(2,1)S(1)} %copy-done.4), channel_id=1, source_target_pairs={{0,8},{8,0},{16,24},{24,16},{1,9},{9,1},{17,25},{25,17},{2,10},{10... | collective-permute-start | bytes 3145736 | tf_op jit(solution)/shard_map/core_acts/ppermute | solution.py:55
  9.1 9.9 %collective-permute-start = (bf16[4,256,128]{2,1,0:T(8,128)(2,1)S(1)}, bf16[4,256,128]{2,1,0:T(8,128)(2,1)S(1)}, u32[]{:S(2)}, u32[]{:S(2)}) collective-permute-start(bf16[4,256,128]{2,1,0:T(8,128)(2,1)S(1)} %latent_grad0_S.1), channel_id=1, source_target_pairs={{0,1},{1,0},{2,3},{3,2},{4,5},{5,4},{6,7},{7,6},{8,9},{9,8},{10,11... | collective-permute-start | bytes 786440 | tf_op jit(solution)/shard_map/latent_grad0_S/ppermute | solution.py:55
  11.9 2.4 %copy-start.3 = (bf16[1024,1024]{1,0:T(8,128)(2,1)S(1)}, bf16[1024,1024]{1,0:T(8,128)(2,1)}, u32[]{:S(2)}) copy-start(bf16[1024,1024]{1,0:T(8,128)(2,1)} %refs_4_) | copy-start | bytes 6291460
  11.9 11.9 %collective-permute-start.4 = (bf16[4,256,128]{2,1,0:T(8,128)(2,1)S(1)}, bf16[4,256,128]{2,1,0:T(8,128)(2,1)S(1)}, u32[]{:S(2)}, u32[]{:S(2)}) collective-permute-start(bf16[4,256,128]{2,1,0:T(8,128)(2,1)S(1)} %latent_grad1_S.1), channel_id=1, source_target_pairs={{0,1},{1,0},{2,3},{3,2},{4,5},{5,4},{6,7},{7,6},{8,9},{9,8},{10,11... | collective-permute-start | bytes 786440 | tf_op jit(solution)/shard_map/latent_grad1_S/ppermute | solution.py:55
  15.6 13.8 %collective-permute-start.8 = (bf16[2,512,128]{2,1,0:T(8,128)(2,1)S(1)}, bf16[2,512,128]{2,1,0:T(8,128)(2,1)S(1)}, u32[]{:S(2)}, u32[]{:S(2)}) collective-permute-start(bf16[2,512,128]{2,1,0:T(8,128)(2,1)S(1)} %get-tuple-element.136), channel_id=1, source_target_pairs={{0,1},{1,0},{2,3},{3,2},{4,5},{5,4},{6,7},{7,6},{8,9},{9,8},{10,11... | collective-permute-start | bytes 786440 | tf_op jit(solution)/shard_map/latent_S/ppermute | solution.py:55
  17.2 17.7 %collective-permute-start.6 = (bf16[2,512,128]{2,1,0:T(8,128)(2,1)S(1)}, bf16[2,512,128]{2,1,0:T(8,128)(2,1)S(1)}, u32[]{:S(2)}, u32[]{:S(2)}) collective-permute-start(bf16[2,512,128]{2,1,0:T(8,128)(2,1)S(1)} %get-tuple-element.137), channel_id=1, source_target_pairs={{0,1},{1,0},{2,3},{3,2},{4,5},{5,4},{6,7},{7,6},{8,9},{9,8},{10,11... | collective-permute-start | bytes 786440 | tf_op jit(solution)/shard_map/latent_S/ppermute | solution.py:55
  19.6 6.4 %collective-permute-start.3 = (bf16[4,128,128]{2,1,0:T(8,128)(2,1)S(1)}, bf16[4,128,128]{2,1,0:T(8,128)(2,1)S(1)}, u32[]{:S(2)}, u32[]{:S(2)}) collective-permute-start(bf16[4,128,128]{2,1,0:T(8,128)(2,1)S(1)} %get-tuple-element.146), channel_id=1, source_target_pairs={{0,2},{1,3},{2,0},{3,1},{4,6},{5,7},{6,4},{7,5},{8,10},{9,11},{10,... | collective-permute-start | bytes 393224 | tf_op jit(solution)/shard_map/latent_grad0_near/ppermute | solution.py:55
  24.4 7.3 %collective-permute-start.7 = (bf16[4,128,128]{2,1,0:T(8,128)(2,1)S(1)}, bf16[4,128,128]{2,1,0:T(8,128)(2,1)S(1)}, u32[]{:S(2)}, u32[]{:S(2)}) collective-permute-start(bf16[4,128,128]{2,1,0:T(8,128)(2,1)S(1)} %get-tuple-element.150), channel_id=1, source_target_pairs={{0,2},{1,3},{2,0},{3,1},{4,6},{5,7},{6,4},{7,5},{8,10},{9,11},{10,... | collective-permute-start | bytes 393224 | tf_op jit(solution)/shard_map/latent_grad1_near/ppermute | solution.py:55
  26.7 10.1 %collective-permute-start.5 = (bf16[4,128,128]{2,1,0:T(8,128)(2,1)S(1)}, bf16[4,128,128]{2,1,0:T(8,128)(2,1)S(1)}, u32[]{:S(2)}, u32[]{:S(2)}) collective-permute-start(bf16[4,128,128]{2,1,0:T(8,128)(2,1)S(1)} %get-tuple-element.154), channel_id=1, source_target_pairs={{0,4},{1,5},{2,6},{3,7},{4,0},{5,1},{6,2},{7,3},{8,12},{9,13},{10,... | collective-permute-start | bytes 393224 | tf_op jit(solution)/shard_map/latent_grad0_far/ppermute | solution.py:55
  30.1 8.2 %collective-permute-start.12 = (bf16[2,256,128]{2,1,0:T(8,128)(2,1)S(1)}, bf16[2,256,128]{2,1,0:T(8,128)(2,1)S(1)}, u32[]{:S(2)}, u32[]{:S(2)}) collective-permute-start(bf16[2,256,128]{2,1,0:T(8,128)(2,1)S(1)} %get-tuple-element.158), channel_id=1, source_target_pairs={{0,2},{1,3},{2,0},{3,1},{4,6},{5,7},{6,4},{7,5},{8,10},{9,11},{10,... | collective-permute-start | bytes 393224 | tf_op jit(solution)/shard_map/latent0_near/ppermute | solution.py:55
  32.3 8.8 %collective-permute-start.11 = (bf16[4,128,128]{2,1,0:T(8,128)(2,1)S(1)}, bf16[4,128,128]{2,1,0:T(8,128)(2,1)S(1)}, u32[]{:S(2)}, u32[]{:S(2)}) collective-permute-start(bf16[4,128,128]{2,1,0:T(8,128)(2,1)S(1)} %get-tuple-element.162), channel_id=1, source_target_pairs={{0,4},{1,5},{2,6},{3,7},{4,0},{5,1},{6,2},{7,3},{8,12},{9,13},{10,... | collective-permute-start | bytes 393224 | tf_op jit(solution)/shard_map/latent_grad1_far/ppermute | solution.py:55
  35.6 10.0 %collective-permute-start.10 = (bf16[2,256,128]{2,1,0:T(8,128)(2,1)S(1)}, bf16[2,256,128]{2,1,0:T(8,128)(2,1)S(1)}, u32[]{:S(2)}, u32[]{:S(2)}) collective-permute-start(bf16[2,256,128]{2,1,0:T(8,128)(2,1)S(1)} %get-tuple-element.166), channel_id=1, source_target_pairs={{0,2},{1,3},{2,0},{3,1},{4,6},{5,7},{6,4},{7,5},{8,10},{9,11},{10,... | collective-permute-start | bytes 393224 | tf_op jit(solution)/shard_map/latent1_near/ppermute | solution.py:55
  37.4 12.4 %collective-permute-start.9 = (bf16[4,128,128]{2,1,0:T(8,128)(2,1)S(1)}, bf16[4,128,128]{2,1,0:T(8,128)(2,1)S(1)}, u32[]{:S(2)}, u32[]{:S(2)}) collective-permute-start(bf16[4,128,128]{2,1,0:T(8,128)(2,1)S(1)} %latent_grad0_last.1.mine), channel_id=1, source_target_pairs={{0,2},{1,3},{2,0},{3,1},{4,6},{5,7},{6,4},{7,5},{8,10},{9,11},{10,... | collective-permute-start | bytes 393224 | tf_op jit(solution)/shard_map/latent_grad0_last/ppermute | solution.py:55
  38.9 11.5 %collective-permute-start.15 = (bf16[2,256,128]{2,1,0:T(8,128)(2,1)S(1)}, bf16[2,256,128]{2,1,0:T(8,128)(2,1)S(1)}, u32[]{:S(2)}, u32[]{:S(2)}) collective-permute-start(bf16[2,256,128]{2,1,0:T(8,128)(2,1)S(1)} %get-tuple-element.172), channel_id=1, source_target_pairs={{0,4},{1,5},{2,6},{3,7},{4,0},{5,1},{6,2},{7,3},{8,12},{9,13},{10,... | collective-permute-start | bytes 393224 | tf_op jit(solution)/shard_map/latent0_far/ppermute | solution.py:55
  41.7 11.4 %collective-permute-start.14 = (bf16[4,128,128]{2,1,0:T(8,128)(2,1)S(1)}, bf16[4,128,128]{2,1,0:T(8,128)(2,1)S(1)}, u32[]{:S(2)}, u32[]{:S(2)}) collective-permute-start(bf16[4,128,128]{2,1,0:T(8,128)(2,1)S(1)} %latent_grad1_last.1.mine), channel_id=1, source_target_pairs={{0,2},{1,3},{2,0},{3,1},{4,6},{5,7},{6,4},{7,5},{8,10},{9,11},{10,... | collective-permute-start | bytes 393224 | tf_op jit(solution)/shard_map/latent_grad1_last/ppermute | solution.py:55
  46.2 9.8 %collective-permute-start.17 = (bf16[2,256,128]{2,1,0:T(8,128)(2,1)S(1)}, bf16[2,256,128]{2,1,0:T(8,128)(2,1)S(1)}, u32[]{:S(2)}, u32[]{:S(2)}) collective-permute-start(bf16[2,256,128]{2,1,0:T(8,128)(2,1)S(1)} %get-tuple-element.178), channel_id=1, source_target_pairs={{0,4},{1,5},{2,6},{3,7},{4,0},{5,1},{6,2},{7,3},{8,12},{9,13},{10,... | collective-permute-start | bytes 393224 | tf_op jit(solution)/shard_map/latent1_far/ppermute | solution.py:55
  51.0 4.3 %collective-permute-start.18 = (bf16[256,128]{1,0:T(8,128)(2,1)S(1)}, bf16[256,128]{1,0:T(8,128)(2,1)S(1)}, u32[]{:S(2)}, u32[]{:S(2)}) collective-permute-start(bf16[256,128]{1,0:T(8,128)(2,1)S(1)} %get-tuple-element.184), channel_id=1, source_target_pairs={{0,16},{8,24},{16,0},{24,8},{1,17},{9,25},{17,1},{25,9},{2,18},{10... | collective-permute-start | bytes 196616 | tf_op jit(solution)/shard_map/latent0_last/ppermute | solution.py:55
  51.6 7.6 %collective-permute-start.13 = (bf16[4,256,128]{2,1,0:T(8,128)(2,1)S(1)}, bf16[4,256,128]{2,1,0:T(8,128)(2,1)S(1)}, u32[]{:S(2)}, u32[]{:S(2)}) collective-permute-start(bf16[4,256,128]{2,1,0:T(8,128)(2,1)S(1)} %latent_grad0_join.1.near.refs_0_), channel_id=1, source_target_pairs={{0,1},{1,0},{2,3},{3,2},{4,5},{5,4},{6,7},{7,6},{8,9},{9,8},{10,11... | collective-permute-start | bytes 786440 | tf_op jit(solution)/shard_map/latent_grad0_join/ppermute | solution.py:55
  53.7 9.8 %collective-permute-start.16 = (bf16[4,256,128]{2,1,0:T(8,128)(2,1)S(1)}, bf16[4,256,128]{2,1,0:T(8,128)(2,1)S(1)}, u32[]{:S(2)}, u32[]{:S(2)}) collective-permute-start(bf16[4,256,128]{2,1,0:T(8,128)(2,1)S(1)} %latent_grad1_join.1.near.refs_2_), channel_id=1, source_target_pairs={{0,1},{1,0},{2,3},{3,2},{4,5},{5,4},{6,7},{7,6},{8,9},{9,8},{10,11... | collective-permute-start | bytes 786440 | tf_op jit(solution)/shard_map/latent_grad1_join/ppermute | solution.py:55
  55.8 5.0 %collective-permute-start.20 = (bf16[2,256,128]{2,1,0:T(8,128)(2,1)S(1)}, bf16[2,256,128]{2,1,0:T(8,128)(2,1)S(1)}, u32[]{:S(2)}, u32[]{:S(2)}) collective-permute-start(bf16[2,256,128]{2,1,0:T(8,128)(2,1)S(1)} %latent0_stack.1.mine), channel_id=1, source_target_pairs={{0,2},{1,3},{2,0},{3,1},{4,6},{5,7},{6,4},{7,5},{8,10},{9,11},{10,... | collective-permute-start | bytes 393224 | tf_op jit(solution)/shard_map/latent0_stack/ppermute | solution.py:55
  56.5 4.9 %collective-permute-start.19 = (bf16[256,128]{1,0:T(8,128)(2,1)S(1)}, bf16[256,128]{1,0:T(8,128)(2,1)S(1)}, u32[]{:S(2)}, u32[]{:S(2)}) collective-permute-start(bf16[256,128]{1,0:T(8,128)(2,1)S(1)} %get-tuple-element.192), channel_id=1, source_target_pairs={{0,16},{8,24},{16,0},{24,8},{1,17},{9,25},{17,1},{25,9},{2,18},{10... | collective-permute-start | bytes 196616 | tf_op jit(solution)/shard_map/latent1_last/ppermute | solution.py:55
  57.3 12.9 %collective-permute-start.30 = (bf16[512,512]{1,0:T(8,128)(2,1)S(1)}, bf16[512,512]{1,0:T(8,128)(2,1)S(1)}, u32[]{:S(2)}, u32[]{:S(2)}) collective-permute-start(bf16[512,512]{1,0:T(8,128)(2,1)S(1)} %get-tuple-element.245), channel_id=1, source_target_pairs={{0,8},{8,0},{16,24},{24,16},{1,9},{9,1},{17,25},{25,17},{2,10},{10... | collective-permute-start | bytes 1572872 | tf_op jit(solution)/shard_map/core_far/ppermute | solution.py:55
  59.8 7.9 %collective-permute-start.23 = (bf16[2,2,256,128]{3,2,1,0:T(8,128)(2,1)S(1)}, bf16[2,2,256,128]{3,2,1,0:T(8,128)(2,1)S(1)}, u32[]{:S(2)}, u32[]{:S(2)}) collective-permute-start(bf16[2,2,256,128]{3,2,1,0:T(8,128)(2,1)S(1)} %latent_grad0_halves.1), channel_id=1, source_target_pairs={{0,8},{8,0},{16,24},{24,16},{1,9},{9,1},{17,25},{25,17},{2,10},{10... | collective-permute-start | bytes 786440 | tf_op jit(solution)/shard_map/latent_grad0_halves/ppermute | solution.py:55
  62.0 5.0 %collective-permute-start.22 = (bf16[2,256,128]{2,1,0:T(8,128)(2,1)S(1)}, bf16[2,256,128]{2,1,0:T(8,128)(2,1)S(1)}, u32[]{:S(2)}, u32[]{:S(2)}) collective-permute-start(bf16[2,256,128]{2,1,0:T(8,128)(2,1)S(1)} %latent1_stack.1.mine), channel_id=1, source_target_pairs={{0,2},{1,3},{2,0},{3,1},{4,6},{5,7},{6,4},{7,5},{8,10},{9,11},{10,... | collective-permute-start | bytes 393224 | tf_op jit(solution)/shard_map/latent1_stack/ppermute | solution.py:55
  63.5 10.3 %collective-permute-start.29 = (bf16[512,512]{1,0:T(8,128)(2,1)S(1)}, bf16[512,512]{1,0:T(8,128)(2,1)S(1)}, u32[]{:S(2)}, u32[]{:S(2)}) collective-permute-start(bf16[512,512]{1,0:T(8,128)(2,1)S(1)} %get-tuple-element.246), channel_id=1, source_target_pairs={{0,8},{8,0},{16,24},{24,16},{1,9},{9,1},{17,25},{25,17},{2,10},{10... | collective-permute-start | bytes 1572872 | tf_op jit(solution)/shard_map/core_far/ppermute | solution.py:55
  63.5 11.4 %collective-permute-start.28 = (bf16[512,512]{1,0:T(8,128)(2,1)S(1)}, bf16[512,512]{1,0:T(8,128)(2,1)S(1)}, u32[]{:S(2)}, u32[]{:S(2)}) collective-permute-start(bf16[512,512]{1,0:T(8,128)(2,1)S(1)} %get-tuple-element.247), channel_id=1, source_target_pairs={{0,8},{8,0},{16,24},{24,16},{1,9},{9,1},{17,25},{25,17},{2,10},{10... | collective-permute-start | bytes 1572872 | tf_op jit(solution)/shard_map/core_far/ppermute | solution.py:55
  67.0 11.8 %collective-permute-start.27 = (bf16[512,512]{1,0:T(8,128)(2,1)S(1)}, bf16[512,512]{1,0:T(8,128)(2,1)S(1)}, u32[]{:S(2)}, u32[]{:S(2)}) collective-permute-start(bf16[512,512]{1,0:T(8,128)(2,1)S(1)} %get-tuple-element.248), channel_id=1, source_target_pairs={{0,8},{8,0},{16,24},{24,16},{1,9},{9,1},{17,25},{25,17},{2,10},{10... | collective-permute-start | bytes 1572872 | tf_op jit(solution)/shard_map/core_far/ppermute | solution.py:55
  67.6 4.2 %collective-permute-start.21 = (bf16[2,2,256,128]{3,2,1,0:T(8,128)(2,1)S(1)}, bf16[2,2,256,128]{3,2,1,0:T(8,128)(2,1)S(1)}, u32[]{:S(2)}, u32[]{:S(2)}) collective-permute-start(bf16[2,2,256,128]{3,2,1,0:T(8,128)(2,1)S(1)} %latent_grad1_halves.1), channel_id=1, source_target_pairs={{0,8},{8,0},{16,24},{24,16},{1,9},{9,1},{17,25},{25,17},{2,10},{10... | collective-permute-start | bytes 786440 | tf_op jit(solution)/shard_map/latent_grad1_halves/ppermute | solution.py:55
  70.2 11.5 %collective-permute-start.31 = (bf16[2,512,128]{2,1,0:T(8,128)(2,1)S(1)}, bf16[2,512,128]{2,1,0:T(8,128)(2,1)S(1)}, u32[]{:S(2)}, u32[]{:S(2)}) collective-permute-start(bf16[2,512,128]{2,1,0:T(8,128)(2,1)S(1)} %latent0_join.1.refs_0_), channel_id=1, source_target_pairs={{0,1},{1,0},{2,3},{3,2},{4,5},{5,4},{6,7},{7,6},{8,9},{9,8},{10,11... | collective-permute-start | bytes 786440 | tf_op jit(solution)/shard_map/latent0_join/ppermute | solution.py:55
  71.8 12.3 %collective-permute-start.32 = (bf16[2,512,128]{2,1,0:T(8,128)(2,1)S(1)}, bf16[2,512,128]{2,1,0:T(8,128)(2,1)S(1)}, u32[]{:S(2)}, u32[]{:S(2)}) collective-permute-start(bf16[2,512,128]{2,1,0:T(8,128)(2,1)S(1)} %latent1_join.1.refs_1_), channel_id=1, source_target_pairs={{0,1},{1,0},{2,3},{3,2},{4,5},{5,4},{6,7},{7,6},{8,9},{9,8},{10,11... | collective-permute-start | bytes 786440 | tf_op jit(solution)/shard_map/latent1_join/ppermute | solution.py:55
  73.8 5.1 %copy-start.1 = (bf16[512,2048]{1,0:T(8,128)(2,1)S(1)}, bf16[512,2048]{1,0:T(8,128)(2,1)}, u32[]{:S(2)}) copy-start(bf16[512,2048]{1,0:T(8,128)(2,1)} %refs_2_.1) | copy-start | bytes 6291460
  73.8 14.2 %collective-permute-start.25 = (bf16[128,1024]{1,0:T(8,128)(2,1)S(1)}, bf16[128,1024]{1,0:T(8,128)(2,1)S(1)}, u32[]{:S(2)}, u32[]{:S(2)}) collective-permute-start(bf16[128,1024]{1,0:T(8,128)(2,1)S(1)} %get-tuple-element.216), channel_id=1, source_target_pairs={{0,16},{8,24},{16,0},{24,8},{1,17},{9,25},{17,1},{25,9},{2,18},{10... | collective-permute-start | bytes 786440 | tf_op jit(solution)/shard_map/latent_grad1_left/ppermute | solution.py:55
  74.9 13.1 %collective-permute-start.24 = (bf16[128,1024]{1,0:T(8,128)(2,1)S(1)}, bf16[128,1024]{1,0:T(8,128)(2,1)S(1)}, u32[]{:S(2)}, u32[]{:S(2)}) collective-permute-start(bf16[128,1024]{1,0:T(8,128)(2,1)S(1)} %get-tuple-element.207), channel_id=1, source_target_pairs={{0,16},{8,24},{16,0},{24,8},{1,17},{9,25},{17,1},{25,9},{2,18},{10... | collective-permute-start | bytes 786440 | tf_op jit(solution)/shard_map/latent_grad0_left/ppermute | solution.py:55
